TPU v7x, 128 devices: a whole 4x4x4 slice. The times are simulated.
128 devices in a mesh: ray: 4 (over y), region: 32 (over z, x, core).
Axes of the slice: x: 4, y: 4, z: 4, core: 2. Of those that a mesh axis runs over, the one named last changes fastest.
Arguments:
- features: bfloat16 [8192, 128, 256], P(('ray', 'region')), may hold values from -6 to 6
- deltas: bfloat16 [8192, 128], P(('ray', 'region')), may hold values from 0.0005 to 0.06
- weight_one: bfloat16 [32, 256, 256], P('region'), may hold values from -0.375 to 0.375
- weight_two: bfloat16 [32, 256, 256], P('region'), may hold values from -0.375 to 0.375
- weight_out: bfloat16 [32, 256, 4], P('region'), may hold values from -0.375 to 0.375
- target: float32 [2048, 3], P(('ray', 'region')), may hold values from 0 to 1
- block_region: int32 [8192, 1], P(('ray', 'region')), may hold values from 0 to 31; in each aligned block of 64 rows (0 to 63, 64 to 127, ...) at most 4 rows name the same one
- seg_order: int32 [2048, 4], P(('ray', 'region')), may hold values from 0 to 3, each once within a row
- owner_map: int32 [32], replicated, may hold values from 0 to 31, each once
Outputs:
- ray_color: float32 [2048, 3], P(('ray', 'region'))
- grad_one: float32 [32, 256, 256], P('region')
- grad_two: float32 [32, 256, 256], P('region')
- grad_out: float32 [32, 256, 4], P('region')
Inputs may be any that keep to these rules, and one draw needn't show every extreme that they name: `block_region`: among the 64 blocks of one device no region appears more than 4 times, and some region appears exactly 4 times. `seg_order`: each row is a permutation of 0 .. 3. `owner_map`: A permutation of 0 .. 31.
All inputs are finite; a program needn't handle non-finite values.
Results may differ from a plain program's by a relative error of at most 0.0095.
The roundings to bfloat16 on the way count: a program that leaves them out, or rounds other values in their place, can miss the bound.
Values may be sent and summed in bfloat16 or wider, within the bound.
No kernel may reach another device: no remote copies, remote signals or barrier semaphores. Data moves between devices by JAX's collectives and lax.ppermute only.
A program may use at most 128 MiB of HBM per device.

v0:
```python
import jax
import jax.numpy as jnp
from jax import lax
from jax.sharding import PartitionSpec as P


def shade(x, delta, w_one, w_two, w_head):
    f32 = jnp.float32
    pre_one = jnp.einsum("agbpd,gde->agbpe", x, w_one, preferred_element_type=f32)
    hidden_one = jax.nn.relu(pre_one).astype(jnp.bfloat16)
    pre_two = jnp.einsum("agbpd,gde->agbpe", hidden_one, w_two, preferred_element_type=f32)
    hidden_two = jax.nn.relu(pre_two).astype(jnp.bfloat16)
    raw = jnp.einsum("agbpd,gdk->agbkp", hidden_two, w_head, preferred_element_type=f32)
    sigma = jax.nn.softplus(raw[..., 0, :])
    rgb = jax.nn.sigmoid(raw[..., 1:, :])
    tau = sigma * delta.astype(f32)
    transmittance = jnp.exp(-(jnp.cumsum(tau, -1) - tau))
    opacity_value = 1.0 - jnp.exp(-tau)
    weight = transmittance * opacity_value
    color = jnp.sum(weight[..., None, :] * rgb, -1)
    log_trans = -jnp.sum(tau, -1)
    result = jnp.concatenate([color, log_trans[..., None]], -1)
    return (
        result,
        (pre_one, hidden_one, pre_two, hidden_two, raw, rgb, transmittance, opacity_value, weight),
    )


def unshade(x, delta, w_two, w_head, saved, output_gradient):
    f32 = jnp.float32
    pre_one, hidden_one, pre_two, hidden_two, raw, rgb, transmittance, opacity_value, weight = saved
    color_gradient = output_gradient[..., :3]
    log_transmittance_gradient = output_gradient[..., 3]
    d_rgb = weight[..., None, :] * color_gradient[..., None]
    weight_gradient = jnp.sum(rgb * color_gradient[..., None], -2)
    prod = weight_gradient * weight
    following_segments = jnp.sum(prod, -1, keepdims=True) - jnp.cumsum(prod, -1)
    optical_depth_gradient = (
        -log_transmittance_gradient[..., None]
        + weight_gradient * transmittance * (1.0 - opacity_value)
        - following_segments
    )
    d_sig = optical_depth_gradient * delta.astype(f32) * jax.nn.sigmoid(raw[..., 0, :])
    d_col = d_rgb * rgb * (1.0 - rgb)
    d_raw = jnp.concatenate([d_sig[..., None, :], d_col], -2).astype(jnp.bfloat16)
    g_head = jnp.einsum("agbpd,agbkp->gdk", hidden_two, d_raw, preferred_element_type=f32)
    dh_two = jnp.einsum("agbkp,gdk->agbpd", d_raw, w_head, preferred_element_type=f32)
    d_two = jnp.where(pre_two > 0, dh_two, 0.0).astype(jnp.bfloat16)
    g_two = jnp.einsum("agbpd,agbpe->gde", hidden_one, d_two, preferred_element_type=f32)
    dh_one = jnp.einsum("agbpe,gde->agbpd", d_two, w_two, preferred_element_type=f32)
    d_one = jnp.where(pre_one > 0, dh_one, 0.0).astype(jnp.bfloat16)
    g_one = jnp.einsum("agbpd,agbpe->gde", x, d_one, preferred_element_type=f32)
    return (g_one, g_two, g_head)


def composite(results, seg_order, target):
    seg = seg_order.shape[1]
    parts = results.reshape(-1, seg, 4)
    colors = parts[..., :3]
    log_trans = parts[..., 3]
    prior_transmittance = (seg_order[:, None, :] < seg_order[:, :, None]).astype(jnp.float32)
    reach = jnp.exp(jnp.sum(prior_transmittance * log_trans[:, None, :], -1))
    color = jnp.sum(reach[..., None] * colors, 1)
    gray = color - target
    color_gradient = reach[..., None] * gray[:, None, :]
    segment_portion = reach * jnp.sum(colors * gray[:, None, :], -1)
    log_transmittance_gradient = jnp.sum(prior_transmittance * segment_portion[:, :, None], 1)
    output_gradient = jnp.concatenate(
        [color_gradient, log_transmittance_gradient[..., None]], -1
    ).reshape(-1, 4)
    return (color, output_gradient)


def local(
    features, deltas, weight_one, weight_two, weight_out, target, block_region, seg_order, owner_map
):
    regions = owner_map.shape[0]
    blocks = features.shape[0]
    samp = features.shape[1]
    width = features.shape[2]
    most = max(2, 2 * blocks // regions)
    grid = jnp.arange(regions, dtype=jnp.int32)
    region_hot = block_region == grid[None, :]
    slots = jnp.sum(jnp.where(region_hot, owner_map[None, :], 0), 1)
    slot_hot = (slots[:, None] == grid[None, :]).astype(jnp.int32)
    rank = jnp.sum((jnp.cumsum(slot_hot, 0) - slot_hot) * slot_hot, 1)
    index = slots * most + rank
    send_x = jnp.zeros((regions * most, samp, width), jnp.bfloat16).at[index].set(features)
    send_d = jnp.zeros((regions * most, samp), jnp.bfloat16).at[index].set(deltas)
    all_one, all_two, all_head = (
        lax.all_gather(weight_one, "region", axis=0, tiled=True),
        lax.all_gather(weight_two, "region", axis=0, tiled=True),
        lax.all_gather(weight_out, "region", axis=0, tiled=True),
    )
    packed_x = send_x.reshape(1, regions, most, samp, width)
    packed_d = send_d.reshape(1, regions, most, samp)
    outcome, saved = shade(packed_x, packed_d, all_one, all_two, all_head)
    results = outcome.reshape(regions * most, 4)[index]
    color, output_gradient = composite(results, seg_order, target)
    packed_c = jnp.zeros((regions * most, 4), jnp.float32).at[index].set(output_gradient)
    packed_c = packed_c.reshape(1, regions, most, 4)
    pieces = unshade(packed_x, packed_d, all_two, all_head, saved, packed_c)
    grad_one, grad_two, grad_out = (
        lax.psum_scatter(pieces[0], "region", scatter_dimension=0, tiled=True),
        lax.psum_scatter(pieces[1], "region", scatter_dimension=0, tiled=True),
        lax.psum_scatter(pieces[2], "region", scatter_dimension=0, tiled=True),
    )
    grad_one, grad_two, grad_out = lax.psum((grad_one, grad_two, grad_out), "ray")
    return (color, grad_one, grad_two, grad_out)


def solution(mesh):
    in_specs = (
        P(("ray", "region"), None, None),
        P(("ray", "region"), None),
        P("region", None, None),
        P("region", None, None),
        P("region", None, None),
        P(("ray", "region"), None),
        P(("ray", "region"), None),
        P(("ray", "region"), None),
        P(),
    )
    out_specs = (
        P(("ray", "region"), None),
        P("region", None, None),
        P("region", None, None),
        P("region", None, None),
    )
    return jax.shard_map(local, mesh=mesh, in_specs=in_specs, out_specs=out_specs, check_vma=False)
```

profile of v0, /device:TPU:0, one launch (start us, length us, event | category | flops | bytes accessed | tf_op | source)
XLA Modules:
  0.0 494.4 jit_solution(1432768238938957485)
XLA Ops:
  7.2 0.7 all-gather.3.cloned.1.call-update
  7.9 0.7 all-gather.5.cloned.1.call-update
  8.7 0.8 select_reduce_fusion.1
  9.7 0.2 select_reduce_fusion
  9.9 0.9 scatter_custom_fusion.1
  10.9 4.2 broadcast_in_dim.20
  15.1 12.0 %scatter_fusion = bf16[128,128,256]{2,1,0:T(8,128)(2,1)} fusion(bf16[128,128,256]{2,1,0:T(8,128)(2,1)} %broadcast_in_dim.20, s32[64]{0:T(128)S(1)} %fusion.49, bf16[64,128,256]{2,1,0:T(8,128)(2,1)} %param.9), kind=kCustom, calls=%fused_computation.1 | custom fusion | bytes 12583168 | tf_op jit(solution)/shard_map/scatter | solution.py:88
  27.1 25.6 %all_gather.11 = bf16[32,256,4]{1,2,0:T(4,128)(2,1)S(1)} all-gather(bf16[1,256,4]{1,2,0:T(4,128)(2,1)S(1)} %copy-done.2), channel_id=1, replica_groups=mesh['ray'=4,'region'=32] {'region'}, dimensions={0}, use_global_device_ids=true | all-gather | bytes 67584 | tf_op jit(solution)/shard_map/all_gather | solution.py:93
  52.7 6.5 %all-gather.3.cloned.1.call-done = bf16[32,256,256]{2,1,0:T(8,128)(2,1)} async-done(((bf16[1,256,256]{2,1,0:T(8,128)(2,1)}), bf16[32,256,256]{2,1,0:T(8,128)(2,1)}) %all-gather.3.cloned.1.call-update) | async-done | bytes 4194320 | tf_op jit(solution)/shard_map/all_gather | solution.py:91
  59.2 10.5 %convert_reduce_fusion.1 = (u32[4,128,256]{2,1,0:T(8,128)S(1)}, bf16[32,4,128,256]{3,2,1,0:T(8,128)(2,1)}) fusion(bf16[32,4,128,256]{3,2,1,0:T(8,128)(2,1)} %bitcast.166, bf16[32,256,256]{2,1,0:T(8,128)(2,1)} %all-gather.3.cloned.1.call-done), kind=kOutput, calls=%fused_computation.8 | convolution fusion | flops 2168324096 | bytes 21495808 | tf_op jit(solution)/shard_map/agbpd,gde->agbpe/dot_general | solution.py:9
  69.7 37.5 %all-gather.5.cloned.1.call-done = bf16[32,256,256]{2,1,0:T(8,128)(2,1)} async-done(((bf16[1,256,256]{2,1,0:T(8,128)(2,1)}), bf16[32,256,256]{2,1,0:T(8,128)(2,1)}) %all-gather.5.cloned.1.call-update) | async-done | bytes 4194320 | tf_op jit(solution)/shard_map/all_gather | solution.py:92
  107.2 11.7 %convert_reduce_fusion = (u32[4,128,256]{2,1,0:T(8,128)S(1)}, bf16[32,4,128,256]{3,2,1,0:T(8,128)(2,1)}) fusion(bf16[32,256,256]{2,1,0:T(8,128)(2,1)} %all-gather.5.cloned.1.call-done, bf16[32,4,128,256]{3,2,1,0:T(8,128)(2,1)} %get-tuple-element.13), kind=kOutput, calls=%fused_computation.5 | convolution fusion | flops 2180907008 | bytes 21495808 | tf_op jit(solution)/shard_map/agbpd,gde->agbpe/dot_general | solution.py:11
  118.9 5.7 %fusion.6 = f32[32,4,128,4]{2,3,1,0:T(4,128)S(1)} fusion(bf16[32,4,128,256]{3,2,1,0:T(8,128)(2,1)} %get-tuple-element.11, bf16[32,256,4]{1,2,0:T(4,128)(2,1)S(1)} %all_gather.11), kind=kOutput, calls=%fused_computation.21 | convolution fusion | flops 46137344 | bytes 8716288 | tf_op jit(solution)/shard_map/agbpd,gdk->agbkp/dot_general | solution.py:13
  125.0 1.2 reduce_window_sum.33
  126.7 0.6 gather_fusion
  127.4 0.2 copy.268
  128.7 0.9 scatter_custom_fusion.2
  129.8 0.3 copy.270
  130.4 1.2 reduce_window_sum.36
  131.9 4.7 select_convert_fusion.1
  136.6 11.6 %convolution_bitcast_fusion = f32[32,256,256]{2,1,0:T(8,128)} fusion(bf16[32,4,128,256]{3,2,1,0:T(8,128)(2,1)} %select_convert_fusion.1, bf16[32,4,128,256]{3,2,1,0:T(8,128)(2,1)} %get-tuple-element.13), kind=kOutput, calls=%fused_computation.18 | convolution fusion | flops 2160066560 | bytes 25165824 | tf_op jit(solution)/shard_map/agbpd,agbpe->gde/dot_general | solution.py:49
  148.3 12.2 %convolution_bitcast_fusion.1 = f32[32,256,256]{2,1,0:T(8,128)} fusion(bf16[32,4,128,256]{3,2,1,0:T(8,128)(2,1)} %bitcast.167, bf16[32,4,128,256]{3,2,1,0:T(8,128)(2,1)} %select_convert_fusion.1, u32[4,128,256]{2,1,0:T(8,128)S(1)} %get-tuple-element.12, bf16[32,256,256]{2,1,0:T(8,128)(2,1)} %all-gather.5.cloned.1.call-done), kind=kOutput, calls=%fused_computation.19 | convolution fusion | flops 4315938816 | bytes 29884416 | tf_op jit(solution)/shard_map/agbpd,agbpe->gde/dot_general | solution.py:52
  160.6 5.9 %fusion.9 = f32[32,256,4]{1,2,0:T(4,128)} fusion(bf16[32,4,128,256]{3,2,1,0:T(8,128)(2,1)} %get-tuple-element.11, bf16[32,4,4,128]{3,0,2,1:T(8,128)(2,1)S(1)} %pad_maximum_fusion), kind=kOutput, calls=%fused_computation.22 | convolution fusion | flops 46137344 | bytes 8650752 | tf_op jit(solution)/shard_map/agbpd,agbkp->gdk/dot_general | solution.py:46
  166.6 73.9 %reduce-scatter.5.cloned.1.call-done = f32[1,256,256]{2,1,0:T(8,128)} async-done(((f32[32,256,256]{2,1,0:T(8,128)}), f32[1,256,256]{2,1,0:T(8,128)}) %reduce-scatter.5.cloned.1.call-update) | async-done | bytes 262160 | tf_op jit(solution)/shard_map/reduce_scatter | solution.py:105
  240.5 96.1 %reduce-scatter.3.cloned.1.call-done = f32[1,256,256]{2,1,0:T(8,128)} async-done(((f32[32,256,256]{2,1,0:T(8,128)}), f32[1,256,256]{2,1,0:T(8,128)}) %reduce-scatter.3.cloned.1.call-update) | async-done | bytes 262160 | tf_op jit(solution)/shard_map/reduce_scatter | solution.py:104
  336.6 0.6 dynamic-slice
  337.2 102.2 %all-reduce.5.cloned.1.call-done = f32[32,256,4]{1,2,0:T(4,128)} async-done(((f32[32,256,4]{1,2,0:T(4,128)}), f32[32,256,4]{1,2,0:T(4,128)}) %all-reduce.5.cloned.1.call-update) | async-done | bytes 131088
  439.3 1.3 constant_dynamic-slice_fusion
  440.6 11.0 %psum.23 = f32[1,256,4]{1,2,0:T(4,128)} all-reduce(f32[1,256,4]{1,2,0:T(4,128)S(1)} %constant_dynamic-slice_fusion), channel_id=1, replica_groups=mesh['ray'=4,'region'=32] {'ray'}, use_global_device_ids=true, to_apply=%region_21.22 | all-reduce | flops 1024 | bytes 8192 | tf_op jit(solution)/shard_map/psum | solution.py:108
  451.7 32.6 %all-reduce.7.cloned.1.call-done = (f32[1,256,256]{2,1,0:T(8,128)}, f32[1,256,256]{2,1,0:T(8,128)}) async-done(((f32[1,256,256]{2,1,0:T(8,128)}, f32[1,256,256]{2,1,0:T(8,128)}), (f32[1,256,256]{2,1,0:T(8,128)}, f32[1,256,256]{2,1,0:T(8,128)})) %all-reduce.7.cloned.1.call-update) | async-done | bytes 524304 | tf_op jit(solution)/shard_map/psum | solution.py:108
  484.3 1.7 copy.294
  485.9 1.7 copy.295
  (64 shorter events, 3.3 us)
Async XLA Ops:
  7.2 52.1 %all-gather.3.cloned.1.call-start = ((), (), s32[]{:S(2)}) async-start(), calls=%async_computation.2 | async-start | bytes 4325376 | tf_op jit(solution)/shard_map/all_gather | solution.py:91
  7.9 99.3 %all-gather.5.cloned.1.call-start = ((), (), s32[]{:S(2)}) async-start(), calls=%async_computation.3 | async-start | bytes 4325376 | tf_op jit(solution)/shard_map/all_gather | solution.py:92
  8.7 231.8 %reduce-scatter.5.cloned.1.call-start = ((), (), s32[]{:S(2)}) async-start(), calls=%async_computation.5 | async-start | bytes 8650752 | tf_op jit(solution)/shard_map/reduce_scatter | solution.py:105
  15.1 12.0 %copy-start.2 = (bf16[1,256,4]{1,2,0:T(4,128)(2,1)S(1)}, bf16[1,256,4]{1,2,0:T(4,128)(2,1)}, u32[]{:S(2)}) copy-start(bf16[1,256,4]{1,2,0:T(4,128)(2,1)} %param.13) | copy-start | bytes 6148
  118.9 8.8 %copy-start = (s32[16,4]{0,1:T(4,128)S(1)}, s32[16,4]{0,1:T(4,128)}, u32[]{:S(2)}) copy-start(s32[16,4]{0,1:T(4,128)} %param.16) | copy-start | bytes 772
  118.9 9.1 %copy-start.3 = (f32[16,3]{0,1:T(4,128)S(1)}, f32[16,3]{0,1:T(4,128)}, u32[]{:S(2)}) copy-start(f32[16,3]{0,1:T(4,128)} %param.14) | copy-start | bytes 580
  128.0 8.6 %copy-start.1 = (f32[16,3]{0,1:T(4,128)}, f32[16,3]{0,1:T(4,128)S(1)}, u32[]{:S(2)}) copy-start(f32[16,3]{0,1:T(4,128)S(1)} %multiply_reduce_fusion.3) | copy-start | bytes 580
  148.2 188.3 %reduce-scatter.3.cloned.1.call-start = ((), (), s32[]{:S(2)}) async-start(), calls=%async_computation.4 | async-start | bytes 8650752 | tf_op jit(solution)/shard_map/reduce_scatter | solution.py:104
  160.5 176.1 %copy-start.4 = (u32[128]{0:T(128)S(1)}, u32[128]{0:T(128)}, u32[]{:S(2)}) copy-start(u32[128]{0:T(128)} %constant.42) | copy-start | bytes 1540
  160.5 278.8 %all-reduce.5.cloned.1.call-start = ((), (), s32[]{:S(2)}) async-start(), calls=%async_computation.6 | async-start | bytes 262144
  166.5 317.7 %all-reduce.7.cloned.1.call-start = ((), (), s32[]{:S(2)}) async-start(), calls=%async_computation.7 | async-start | bytes 1048576 | tf_op jit(solution)/shard_map/psum | solution.py:108
Sparse Core Ops, SparseCore 0:
  10.3 48.9 all-gather.2
  61.5 45.6 all-gather.4
  148.3 92.0 reduce-scatter.4
  244.5 92.0 reduce-scatter.2
  340.2 99.1 all-reduce.4
  441.7 42.4 all-reduce.6
where the time goes:
time: 495 us; the launch traced here: 494 us
  waiting for transfers between devices  350 us (71%)
  matrix products  62.3 us (13%)
  blocking collectives  36.6 us (7%)
  local copies, waits for them, and re-layouts  26.3 us (5%)
  between operations  14.3 us (3%)
    unnamed x7, waiting for transfers between devices  104 us
    reduce_scatter x1, waiting for transfers between devices, local(): lax.psum_scatter(pieces[0], 'region', scatter_dimension=0, tiled=True)  96.1 us
    reduce_scatter x1, waiting for transfers between devices, local(): lax.psum_scatter(pieces[1], 'region', scatter_dimension=0, tiled=True)  73.9 us
    all_gather x1, waiting for transfers between devices, local(): lax.all_gather(weight_two, 'region', axis=0, tiled=True)  37.5 us
    psum x1, waiting for transfers between devices, local(): lax.psum((grad_one, grad_two, grad_out), 'ray')  32.6 us
    all_gather x1, blocking collectives, local(): lax.all_gather(weight_out, 'region', axis=0, tiled=True)  25.6 us
    dot_general x1, matrix products, unshade(): g_one = jnp.einsum('agbpd,agbpe->gde', x, d_one, preferred_element_type=f32)  12.2 us
    scatter x1, local copies, waits for them, and re-layouts, local(): jnp.zeros((regions * most, samp, width), jnp.bfloat16).at[index]  12 us
  transfers between devices with their start and end apart: 6, of which 6 were waited for; matrix products, arithmetic and copies ran while one was open for 10% of the time, Pallas kernels for 0%

commit v1 on v0

v1 whole, which is shorter than its diff:
```python
import functools

import jax
import jax.numpy as jnp
from jax import lax
from jax.experimental import pallas as pl
from jax.experimental.pallas import tpu as pltpu
from jax.sharding import PartitionSpec as P

F32, BF16, I32 = jnp.float32, jnp.bfloat16, jnp.int32
NS = 16
NP = 64
ROWS = 528
VMEM = pltpu.CompilerParams(vmem_limit_bytes=56 * 1024 * 1024)
HI = lax.Precision.HIGHEST

TREE = (
    ((0, 1), (0, 0), "x", 1),
    ((0, 3), (0, 0), "x", 3),
    ((1, 0), (0, 0), "z", 1),
    ((3, 0), (0, 0), "z", 3),
    ((0, 2), (0, 1), "x", 1),
    ((1, 3), (1, 0), "x", 3),
    ((2, 0), (1, 0), "z", 1),
    ((3, 3), (0, 3), "z", 3),
    ((1, 1), (1, 0), "x", 1),
    ((3, 1), (0, 1), "z", 3),
    ((1, 2), (0, 2), "z", 1),
    ((3, 2), (3, 3), "x", 3),
    ((2, 1), (2, 0), "x", 1),
    ((2, 3), (2, 0), "x", 3),
    ((2, 2), (1, 2), "z", 1),
)


def move(axis, step):
    pairs = []
    for z in range(4):
        for x in range(4):
            for c in range(2):
                z2, x2, c2 = z, x, c
                if axis == "z":
                    z2 = (z + step) % 4
                elif axis == "x":
                    x2 = (x + step) % 4
                else:
                    c2 = 1 - c
                pairs.append((z * 8 + x * 2 + c, z2 * 8 + x2 * 2 + c2))
    return pairs


def iota(shape, dim):
    return lax.broadcasted_iota(I32, shape, dim)


def meta_kernel(place, owner, region, order, target, out):
    spot = region[...]
    slot = jnp.zeros((64, 1), I32)
    for r in range(32):
        slot = jnp.where(spot == r, owner[r], slot)
    dz = ((slot >> 3) - place[0]) & 3
    dx = (((slot >> 1) & 3) - place[1]) & 3
    key = (dz * 4 + dx) * 2 + (slot & 1)
    eye = iota((64, 128), 0) == iota((64, 128), 1)
    key_row = jnp.sum(jnp.where(eye, key.astype(F32), 0.0), 0, keepdims=True)
    lane = iota((16, 128), 1)
    mine = (lane >> 2) == iota((16, 128), 0)
    seg = order[...].astype(F32)
    spread = jnp.zeros((16, 128), F32)
    for k in range(4):
        spread = jnp.where((lane & 3) == k, seg[:, k : k + 1], spread)
    rows = [key_row, jnp.sum(jnp.where(mine, spread, 0.0), 0, keepdims=True)]
    for c in range(3):
        rows.append(jnp.sum(jnp.where(mine, target[:, c : c + 1], 0.0), 0, keepdims=True))
    rows.append(jnp.zeros((3, 128), F32))
    out[...] = jnp.concatenate(rows, 0)


def both(a, b):
    lane = iota(a.shape, 1)
    return jnp.where(lane < 64, a, pltpu.roll(b, 64, 1))


def plan_kernel(place, own, sib, table, code_out):
    meta = both(own[...], sib[...])
    key = meta[0:1].astype(I32)
    rel, valid = key >> 1, (key & 1) == place[2]
    hot = (iota((NS, 128), 0) == rel) & valid
    hotf = jnp.where(hot, 1.0, 0.0)
    before = jnp.where(iota((128, 128), 0) < iota((128, 128), 1), 1.0, 0.0)
    cum = jnp.dot(hotf, before, preferred_element_type=F32)
    rank = jnp.sum(hotf * cum, 0, keepdims=True).astype(I32)
    count = jnp.sum(hotf, 1, keepdims=True).astype(I32)
    pairs = ((count + 1) >> 1).astype(F32)
    eye = iota((NS, 128), 0) == iota((NS, 128), 1)
    pairs_row = jnp.sum(jnp.where(eye, pairs, 0.0), 0, keepdims=True)
    ahead = iota((NS, 128), 1) < iota((NS, 128), 0)
    start = jnp.sum(jnp.where(ahead, pairs_row, 0.0), 1, keepdims=True)
    start_row = jnp.sum(jnp.where(eye, start, 0.0), 0, keepdims=True)
    start_j = jnp.sum(hotf * start, 0, keepdims=True).astype(I32)
    code = start_j + (rank >> 1) + (rank & 1) * NP
    code = jnp.where(valid, code, -1)
    square = iota((128, 128), 0) == iota((128, 128), 1)
    code_col = jnp.sum(jnp.where(square, code.astype(F32), 0.0), 1, keepdims=True)
    source = (iota((128, 128), 0) + 1).astype(F32)
    hit = code_col.astype(I32) == iota((128, 128), 1)
    inverse = jnp.sum(jnp.where(hit, source, 0.0), 0, keepdims=True).astype(I32) - 1
    begun = jnp.where(start.astype(I32) <= iota((NS, 128), 1), 1.0, 0.0)
    slot_of = jnp.sum(begun, 0, keepdims=True).astype(I32) - 1
    total = jnp.sum(pairs_row, 1, keepdims=True).astype(I32)
    table[...] = jnp.concatenate(
        [
            inverse,
            slot_of,
            start_row.astype(I32),
            pairs_row.astype(I32),
            jnp.broadcast_to(total, (1, 128)),
            jnp.zeros((3, 128), I32),
        ],
        0,
    )
    code_out[...] = jnp.broadcast_to(code, (8, 128))


def fetch(table, own, sib, xs, sems, pairs):
    def one(i, h):
        src = table[0, h * NP + i]

        @pl.when(src < 0)
        def _():
            xs[i, h] = jnp.zeros((128, 256), BF16)

        @pl.when((src >= 0) & (src < 64))
        def _():
            pltpu.make_async_copy(own.at[src], xs.at[i, h], sems.at[i, h]).start()

        @pl.when(src >= 64)
        def _():
            pltpu.make_async_copy(sib.at[src - 64], xs.at[i, h], sems.at[i, h]).start()

    def step(i, _):
        one(i, 0)
        one(i, 1)
        return 0

    lax.fori_loop(0, pairs, step, 0)


def arrive(table, own, xs, sems, i):
    for h in range(2):

        @pl.when(table[0, h * NP + i] >= 0)
        def _():
            pltpu.make_async_copy(own.at[0], xs.at[i, h], sems.at[i, h]).wait()


def forward_kernel(*refs):
    table, code, own, sib, d_own, d_sib = refs[:6]
    weights = refs[6 : 6 + NS]
    res, saved, h1_out, h2_out = refs[6 + NS : 10 + NS]
    xs, wv, h1, h2, raw, xsem, wsem, hsem = refs[10 + NS :]
    total = table[4, 0]
    even = (total + 1) // 2 * 2
    for s in range(NS):
        pltpu.make_async_copy(weights[s], wv.at[s], wsem.at[s]).start()
    fetch(table, own, sib, xs, xsem, even)
    raw[...] = jnp.zeros(raw.shape, F32)
    for s in range(NS):
        pltpu.make_async_copy(weights[s], wv.at[s], wsem.at[s]).wait()

    def shade(i):
        slot = table[1, i]
        arrive(table, own, xs, xsem, i)
        x = xs[i].reshape(256, 256)
        pre = jnp.dot(x, wv[slot, 0:256], preferred_element_type=F32)
        one = jnp.maximum(pre, 0.0).astype(BF16)
        h1[i] = one
        pre = jnp.dot(one, wv[slot, 256:512], preferred_element_type=F32)
        two = jnp.maximum(pre, 0.0).astype(BF16)
        h2[i] = two
        out = lax.dot_general(
            wv[slot, 512:528], two, (((1,), (1,)), ((), ())), preferred_element_type=F32
        )
        rows = pl.ds(pl.multiple_of(i * 8, 8), 8)
        raw[0, rows, :] = out[0:8, 0:128]
        raw[1, rows, :] = out[0:8, 128:256]
        pltpu.make_async_copy(h1.at[i], h1_out.at[i], hsem.at[0, i]).start()
        pltpu.make_async_copy(h2.at[i], h2_out.at[i], hsem.at[1, i]).start()

    def step(t, _):
        shade(2 * t)
        shade(2 * t + 1)
        return 0

    lax.fori_loop(0, even // 2, step, 0)

    before = jnp.where(iota((128, 128), 0) < iota((128, 128), 1), 1.0, 0.0)
    spot = code[0:1]
    out = jnp.zeros((4, 128), F32)
    for h in range(2):
        lanes = slice(h * 128, h * 128 + 128)
        pick = spot == iota((NP, 128), 0) + h * NP
        pickb = jnp.where(pick, 1.0, 0.0).astype(BF16)
        deltas = jnp.concatenate([d_own[...], d_sib[...]], 0)
        delta = jnp.dot(pickb, deltas, preferred_element_type=F32)
        ch = [raw[h, pl.ds(c, NP, stride=8), :] for c in range(4)]
        sigma = jnp.maximum(ch[0], 0.0) + jnp.log1p(jnp.exp(-jnp.abs(ch[0])))
        rgb = [jax.nn.sigmoid(ch[c]) for c in (1, 2, 3)]
        tau = sigma * delta
        cum = jnp.dot(tau, before, precision=HI, preferred_element_type=F32)
        trans = jnp.exp(-cum)
        opacity = 1.0 - jnp.exp(-tau)
        weight = trans * opacity
        cols = [jnp.sum(weight * rgb[c], 1, keepdims=True) for c in range(3)]
        cols.append(-jnp.sum(tau, 1, keepdims=True))
        out += jnp.concatenate(
            [jnp.sum(jnp.where(pick, col, 0.0), 0, keepdims=True) for col in cols], 0
        )
        keep = rgb + [weight, trans * (1.0 - opacity), delta * jax.nn.sigmoid(ch[0])]
        for k in range(6):
            saved[k, :, lanes] = keep[k]
    res[...] = jnp.concatenate([out, jnp.zeros((4, 128), F32)], 0)

    def drain(i, _):
        pltpu.make_async_copy(h1.at[i], h1_out.at[i], hsem.at[0, i]).wait()
        pltpu.make_async_copy(h2.at[i], h2_out.at[i], hsem.at[1, i]).wait()
        return 0

    lax.fori_loop(0, even, drain, 0)


def backward_kernel(*refs):
    table, code, own, sib, res, res_sib, m_own, m_sib, saved, h1_in, h2_in = refs[:11]
    weights = refs[11 : 11 + NS]
    color_out = refs[11 + NS]
    grads = refs[12 + NS : 12 + 2 * NS]
    xs, wv, h1, h2, dr, acc1, acc2, acc3, stage, xsem, wsem, hsem, gsem = refs[12 + 2 * NS :]
    total = table[4, 0]
    for s in range(NS):
        pltpu.make_async_copy(weights[s].at[pl.ds(256, 272)], wv.at[s], wsem.at[s]).start()

    def load(i, _):
        pltpu.make_async_copy(h1_in.at[i], h1.at[i], hsem.at[0, i]).start()
        pltpu.make_async_copy(h2_in.at[i], h2.at[i], hsem.at[1, i]).start()
        return 0

    lax.fori_loop(0, total, load, 0)
    fetch(table, own, sib, xs, xsem, total)

    meta = both(m_own[...], m_sib[...])
    parts = res[...] + pltpu.roll(res_sib[...], 64, 1)
    order = meta[1:2]
    square = (128, 128)
    same = (iota(square, 0) >> 2) == (iota(square, 1) >> 2)
    samef = jnp.where(same, 1.0, 0.0)
    eye = iota(square, 0) == iota(square, 1)
    order_col = jnp.sum(jnp.where(eye, order, 0.0), 1, keepdims=True)
    prior = jnp.where(same & (order_col < order), 1.0, 0.0)
    later = jnp.where(same & (order_col > order), 1.0, 0.0)
    ahead = jnp.dot(parts, prior, precision=HI, preferred_element_type=F32)[3:4]
    reach = jnp.exp(ahead)
    shown = parts * reach
    color = jnp.dot(shown, samef, precision=HI, preferred_element_type=F32)
    color_out[...] = color
    gray = color[0:3] - meta[2:5]
    portion = jnp.sum(shown[0:3] * gray, 0, keepdims=True)
    log_cot = jnp.dot(
        jnp.broadcast_to(portion, (8, 128)), later, precision=HI, preferred_element_type=F32
    )[0:1]
    cot = [reach * gray[c : c + 1] for c in range(3)] + [log_cot]

    after = jnp.where(iota(square, 0) > iota(square, 1), 1.0, 0.0)
    spot = code[0:1]
    dr[...] = jnp.zeros(dr.shape, F32)
    for h in range(2):
        lanes = slice(h * 128, h * 128 + 128)
        pick = spot == iota((NP, 128), 0) + h * NP
        col = [jnp.sum(jnp.where(pick, row, 0.0), 1, keepdims=True) for row in cot]
        rgb = [saved[c, :, lanes] for c in range(3)]
        weight = saved[3, :, lanes]
        d_weight = rgb[0] * col[0] + rgb[1] * col[1] + rgb[2] * col[2]
        follow = jnp.dot(d_weight * weight, after, precision=HI, preferred_element_type=F32)
        d_tau = d_weight * saved[4, :, lanes] - col[3] - follow
        dr[h, pl.ds(0, NP, stride=8), :] = d_tau * saved[5, :, lanes]
        for c in range(3):
            d_col = weight * col[c] * rgb[c] * (1.0 - rgb[c])
            dr[h, pl.ds(c + 1, NP, stride=8), :] = d_col

    for s in range(NS):
        pltpu.make_async_copy(weights[s].at[pl.ds(256, 272)], wv.at[s], wsem.at[s]).wait()

    for s in range(NS):
        begin, count = table[2, s], table[3, s]
        acc1[...] = jnp.zeros((256, 256), F32)
        acc2[...] = jnp.zeros((256, 256), F32)
        acc3[...] = jnp.zeros((16, 256), F32)

        def pair(i, _):
            arrive(table, own, xs, xsem, i)
            pltpu.make_async_copy(h1_in.at[i], h1.at[i], hsem.at[0, i]).wait()
            pltpu.make_async_copy(h2_in.at[i], h2.at[i], hsem.at[1, i]).wait()
            rows = pl.ds(pl.multiple_of(i * 8, 8), 8)
            d_raw = jnp.concatenate([dr[0, rows, :], dr[1, rows, :]], 1)
            d_raw = jnp.concatenate([d_raw, jnp.zeros((8, 256), F32)], 0).astype(BF16)
            x = xs[i].reshape(256, 256)
            one, two = h1[i], h2[i]
            acc3[...] += jnp.dot(d_raw, two, preferred_element_type=F32)
            dh = lax.dot_general(
                d_raw, wv[s, 256:272], (((0,), (0,)), ((), ())), preferred_element_type=F32
            )
            d_two = jnp.where(two > 0, dh, 0.0).astype(BF16)
            acc2[...] += lax.dot_general(
                one, d_two, (((0,), (0,)), ((), ())), preferred_element_type=F32
            )
            dh = lax.dot_general(
                d_two, wv[s, 0:256], (((1,), (1,)), ((), ())), preferred_element_type=F32
            )
            d_one = jnp.where(one > 0, dh, 0.0).astype(BF16)
            acc1[...] += lax.dot_general(
                x, d_one, (((0,), (0,)), ((), ())), preferred_element_type=F32
            )
            return 0

        lax.fori_loop(begin, begin + count, pair, 0)
        stage[s, 0:256] = acc1[...].astype(BF16)
        stage[s, 256:512] = acc2[...].astype(BF16)
        stage[s, 512:528] = acc3[...].astype(BF16)
        pltpu.make_async_copy(stage.at[s], grads[s], gsem.at[s]).start()
    for s in range(NS):
        pltpu.make_async_copy(stage.at[s], grads[s], gsem.at[s]).wait()


def spec(space):
    return pl.BlockSpec(memory_space=space)


def local(
    features, deltas, weight_one, weight_two, weight_out, target, block_region, seg_order, owner_map
):
    smem, vmem, hbm = spec(pltpu.SMEM), spec(pltpu.VMEM), spec(pl.ANY)
    shape = jax.ShapeDtypeStruct
    me = lax.axis_index("region")
    place = jnp.stack([me >> 3, (me >> 1) & 3, me & 1]).astype(I32)

    def swap(a):
        return lax.ppermute(a, "region", move("core", 1))

    head = jnp.pad(weight_out[0].T, ((0, 12), (0, 0)))
    held = {(0, 0): jnp.concatenate([weight_one[0], weight_two[0], head], 0)}
    for key, source, axis, step in TREE:
        held[key] = lax.ppermute(held[source], "region", move(axis, -step))
    weights = [held[(s // 4, s % 4)] for s in range(NS)]

    meta = pl.pallas_call(
        meta_kernel,
        out_shape=shape((8, 128), F32),
        in_specs=[smem, smem, vmem, vmem, vmem],
        out_specs=vmem,
        name="meta",
    )(place, owner_map, block_region, seg_order, target)
    meta_sib = swap(meta)
    x_sib, d_sib = swap(features), swap(deltas)
    table, code = pl.pallas_call(
        plan_kernel,
        out_shape=(shape((8, 128), I32), shape((8, 128), I32)),
        in_specs=[smem, vmem, vmem],
        out_specs=(vmem, vmem),
        name="plan",
    )(place, meta, meta_sib)

    dma = pltpu.SemaphoreType.DMA
    res, saved, h1, h2 = pl.pallas_call(
        forward_kernel,
        out_shape=(
            shape((8, 128), F32),
            shape((6, NP, 256), F32),
            shape((NP, 256, 256), BF16),
            shape((NP, 256, 256), BF16),
        ),
        in_specs=[smem, vmem, hbm, hbm, vmem, vmem] + [hbm] * NS,
        out_specs=(vmem, vmem, hbm, hbm),
        scratch_shapes=[
            pltpu.VMEM((NP, 2, 128, 256), BF16),
            pltpu.VMEM((NS, ROWS, 256), BF16),
            pltpu.VMEM((NP, 256, 256), BF16),
            pltpu.VMEM((NP, 256, 256), BF16),
            pltpu.VMEM((2, NP * 8, 128), F32),
            dma((NP, 2)),
            dma((NS,)),
            dma((2, NP)),
        ],
        compiler_params=VMEM,
        name="forward",
    )(table, code, features, x_sib, deltas, d_sib, *weights)
    res_sib = swap(res)
    color, *grads = pl.pallas_call(
        backward_kernel,
        out_shape=(shape((8, 128), F32),) + (shape((ROWS, 256), BF16),) * NS,
        in_specs=[smem, vmem, hbm, hbm, vmem, vmem, vmem, vmem, vmem, hbm, hbm] + [hbm] * NS,
        out_specs=(vmem,) + (hbm,) * NS,
        scratch_shapes=[
            pltpu.VMEM((NP, 2, 128, 256), BF16),
            pltpu.VMEM((NS, 272, 256), BF16),
            pltpu.VMEM((NP, 256, 256), BF16),
            pltpu.VMEM((NP, 256, 256), BF16),
            pltpu.VMEM((2, NP * 8, 128), F32),
            pltpu.VMEM((256, 256), F32),
            pltpu.VMEM((256, 256), F32),
            pltpu.VMEM((16, 256), F32),
            pltpu.VMEM((NS, ROWS, 256), BF16),
            dma((NP, 2)),
            dma((NS,)),
            dma((2, NP)),
            dma((NS,)),
        ],
        compiler_params=VMEM,
        name="backward",
    )(table, code, features, x_sib, res, res_sib, meta, meta_sib, saved, h1, h2, *weights)

    sums = {(s // 4, s % 4): grads[s] for s in range(NS)}
    for key, source, axis, step in reversed(TREE):
        got = lax.ppermute(sums[key], "region", move(axis, step))
        sums[source] = (sums[source].astype(F32) + got.astype(F32)).astype(BF16)
    mine = sums[(0, 0)]
    total = mine.astype(F32)
    for d in (1, 3, 2):
        got = lax.ppermute(mine, "ray", [(i, (i + d) % 4) for i in range(4)])
        total = total + got.astype(F32)
    ray_color = color[0:3, 0:64:4].T
    return ray_color, total[None, 0:256], total[None, 256:512], total[512:516].T[None]


def solution(mesh):
    in_specs = (
        P(("ray", "region"), None, None),
        P(("ray", "region"), None),
        P("region", None, None),
        P("region", None, None),
        P("region", None, None),
        P(("ray", "region"), None),
        P(("ray", "region"), None),
        P(("ray", "region"), None),
        P(),
    )
    out_specs = (
        P(("ray", "region"), None),
        P("region", None, None),
        P("region", None, None),
        P("region", None, None),
    )
    return jax.shard_map(local, mesh=mesh, in_specs=in_specs, out_specs=out_specs, check_vma=False)
```

time: 495 us -> 167 us (0.34)
  waiting for transfers between devices: 350 us -> 46.2 us
  matrix products: 62.3 us -> 0 us
  Pallas kernels: 0 us -> 54.2 us
  starting transfers between devices: 0.24 us -> 45.4 us
  blocking collectives: 36.6 us -> 0 us
  local copies, waits for them, and re-layouts: 26.3 us -> 6.8 us
  between operations: 14.3 us -> 0.97 us
  other arithmetic: 4.59 us -> 10.3 us
    reduce_scatter x2 -> x0, waiting for transfers between devices: 170 us -> none  [the longest x1 96.1 us: local(): lax.psum_scatter(pieces[0], 'region', scatter_dimension=0, tiled=True)]
    unnamed x7 -> x0, waiting for transfers between devices: 104 us -> none
    dot_general x7 -> x0, matrix products: 62.3 us -> none  [the longest x1 12.2 us: unshade(): g_one = jnp.einsum('agbpd,agbpe->gde', x, d_one, preferred_element_type=f32)]
    pallas_call x0 -> x4, Pallas kernels: none -> 54.2 us  [the longest x1 28.3 us: local(): pl.pallas_call(backward_kernel, out_shape=(shape((8, 128), F32),) + (shap...]
    ppermute x0 -> x37, waiting for transfers between devices: none -> 46.2 us  [the longest x15 22 us: local(): got = lax.ppermute(sums[key], 'region', move(axis, step))]
    ppermute x0 -> x37, starting transfers between devices: none -> 45.4 us  [the longest x15 24.8 us: local(): held[key] = lax.ppermute(held[source], 'region', move(axis, -step))]
    all_gather x2 -> x0, waiting for transfers between devices: 44 us -> none  [the longest x1 37.5 us: local(): lax.all_gather(weight_two, 'region', axis=0, tiled=True)]
    psum x1 -> x0, waiting for transfers between devices: 32.6 us -> none  [local(): lax.psum((grad_one, grad_two, grad_out), 'ray')]
  transfers between devices with their start and end apart: 6 -> 37, of which waited for: 6 -> 16; matrix products, arithmetic and copies ran while one was open for 10% -> 8% of each run, Pallas kernels for 0% -> 2%
where the time goes in v1:
time: 167 us; the launch traced here: 164 us
  Pallas kernels  54.2 us (32%)
  waiting for transfers between devices  46.2 us (28%)
  starting transfers between devices  45.4 us (27%)
  other arithmetic  10.3 us (6%)
  local copies, waits for them, and re-layouts  6.8 us (4%)
    pallas_call x1, Pallas kernels, local(): pl.pallas_call(backward_kernel, out_shape=(shape((8, 128), F32),) + (shap...  28.3 us
    ppermute x15, starting transfers between devices, local(): held[key] = lax.ppermute(held[source], 'region', move(axis, -step))  24.8 us
    pallas_call x1, Pallas kernels, local(): pl.pallas_call(forward_kernel, out_shape=(shape((8, 128), F32), shape((6,...  22.7 us
    ppermute x15, waiting for transfers between devices, local(): got = lax.ppermute(sums[key], 'region', move(axis, step))  22 us
    ppermute x15, starting transfers between devices, local(): got = lax.ppermute(sums[key], 'region', move(axis, step))  16.2 us
    ppermute x15, waiting for transfers between devices, local(): held[key] = lax.ppermute(held[source], 'region', move(axis, -step))  13.9 us
    convert_element_type x8, other arithmetic, local(): sums[source] = (sums[source].astype(F32) + got.astype(F32)).astype(BF16)  8.46 us
    ppermute x3, waiting for transfers between devices, local(): got = lax.ppermute(mine, 'ray', [(i, (i + d) % 4) for i in range(4)])  6.38 us
  transfers between devices with their start and end apart: 37, of which 16 were waited for; matrix products, arithmetic and copies ran while one was open for 8% of the time, Pallas kernels for 2%

profile of v1, /device:TPU:0, one launch (start us, length us, event | category | flops | bytes accessed | tf_op | source)
XLA Modules:
  0.0 163.8 jit_solution(15004356771601775560)
XLA Ops:
  1.7 4.2 %collective-permute-start.6 = (bf16[528,256]{1,0:T(8,128)(2,1)S(1)}, bf16[528,256]{1,0:T(8,128)(2,1)S(1)}, u32[]{:S(2)}, u32[]{:S(2)}) collective-permute-start(bf16[528,256]{1,0:T(8,128)(2,1)S(1)} %fusion.1.refs_6_.refs_11_), channel_id=1, source_target_pairs={{0,24},{1,25},{2,26},{3,27},{4,28},{5,29},{6,30},{7,31},{8,0},{9,1... | collective-permute-start | bytes 811016 | tf_op jit(solution)/shard_map/ppermute | solution.py:351
  5.9 2.8 %collective-permute-start.3 = (bf16[528,256]{1,0:T(8,128)(2,1)S(1)}, bf16[528,256]{1,0:T(8,128)(2,1)S(1)}, u32[]{:S(2)}, u32[]{:S(2)}) collective-permute-start(bf16[528,256]{1,0:T(8,128)(2,1)S(1)} %fusion.1.refs_6_.refs_11_), channel_id=1, source_target_pairs={{0,6},{1,7},{2,0},{3,1},{4,2},{5,3},{6,4},{7,5},{8,14},{9,15},{10,... | collective-permute-start | bytes 811016 | tf_op jit(solution)/shard_map/ppermute | solution.py:351
  11.4 1.4 copy.13.region
  13.4 1.6 meta.1.own.refs_6_
  15.0 1.4 collective-permute-done.sib.refs_7_
  17.8 3.3 %collective-permute-start.10 = (bf16[528,256]{1,0:T(8,128)(2,1)S(1)}, bf16[528,256]{1,0:T(8,128)(2,1)S(1)}, u32[]{:S(2)}, u32[]{:S(2)}) collective-permute-start(bf16[528,256]{1,0:T(8,128)(2,1)S(1)} %collective-permute-done.6.refs_10_.refs_15_), channel_id=1, source_target_pairs={{0,24},{1,25},{2,26},{3,27},{4,28},{5,29},{6,30},{7,31},{8,0},{9,1... | collective-permute-start | bytes 811016 | tf_op jit(solution)/shard_map/ppermute | solution.py:351
  21.8 2.6 %collective-permute-start.4 = (bf16[528,256]{1,0:T(8,128)(2,1)S(1)}, bf16[528,256]{1,0:T(8,128)(2,1)S(1)}, u32[]{:S(2)}, u32[]{:S(2)}) collective-permute-start(bf16[528,256]{1,0:T(8,128)(2,1)S(1)} %collective-permute-done.3.refs_7_.refs_12_), channel_id=1, source_target_pairs={{0,6},{1,7},{2,0},{3,1},{4,2},{5,3},{6,4},{7,5},{8,14},{9,15},{10,... | collective-permute-start | bytes 811016 | tf_op jit(solution)/shard_map/ppermute | solution.py:351
  24.4 3.9 %collective-permute-done.5.refs_9_.refs_14_ = bf16[528,256]{1,0:T(8,128)(2,1)S(1)} collective-permute-done((bf16[528,256]{1,0:T(8,128)(2,1)S(1)}, bf16[528,256]{1,0:T(8,128)(2,1)S(1)}, u32[]{:S(2)}, u32[]{:S(2)}) %collective-permute-start.5) | collective-permute-done | bytes 270368 | tf_op jit(solution)/shard_map/ppermute | solution.py:351
  28.4 4.9 %collective-permute-done.9.refs_13_.refs_18_ = bf16[528,256]{1,0:T(8,128)(2,1)S(1)} collective-permute-done((bf16[528,256]{1,0:T(8,128)(2,1)S(1)}, bf16[528,256]{1,0:T(8,128)(2,1)S(1)}, u32[]{:S(2)}, u32[]{:S(2)}) %collective-permute-start.9) | collective-permute-done | bytes 270368 | tf_op jit(solution)/shard_map/ppermute | solution.py:351
  33.3 3.3 %collective-permute-start.8 = (bf16[528,256]{1,0:T(8,128)(2,1)S(1)}, bf16[528,256]{1,0:T(8,128)(2,1)S(1)}, u32[]{:S(2)}, u32[]{:S(2)}) collective-permute-start(bf16[528,256]{1,0:T(8,128)(2,1)S(1)} %collective-permute-done.4.refs_8_.refs_13_), channel_id=1, source_target_pairs={{0,24},{1,25},{2,26},{3,27},{4,28},{5,29},{6,30},{7,31},{8,0},{9,1... | collective-permute-start | bytes 811016 | tf_op jit(solution)/shard_map/ppermute | solution.py:351
  37.4 3.7 %collective-permute-start.11 = (bf16[528,256]{1,0:T(8,128)(2,1)S(1)}, bf16[528,256]{1,0:T(8,128)(2,1)}, u32[]{:S(2)}, u32[]{:S(2)}) collective-permute-start(bf16[528,256]{1,0:T(8,128)(2,1)S(1)} %collective-permute-done.10.refs_14_.refs_19_), channel_id=1, source_target_pairs={{0,6},{1,7},{2,0},{3,1},{4,2},{5,3},{6,4},{7,5},{8,14},{9,15},{10,... | collective-permute-start | bytes 811016 | tf_op jit(solution)/shard_map/ppermute | solution.py:351
  41.1 1.5 collective-permute-done.15.refs_19_.refs_24_
  42.6 1.7 %collective-permute-start.17 = (bf16[528,256]{1,0:T(8,128)(2,1)S(1)}, bf16[528,256]{1,0:T(8,128)(2,1)}, u32[]{:S(2)}, u32[]{:S(2)}) collective-permute-start(bf16[528,256]{1,0:T(8,128)(2,1)S(1)} %collective-permute-done.16.refs_21_.refs_26_), channel_id=1, source_target_pairs={{0,2},{1,3},{2,4},{3,5},{4,6},{5,7},{6,0},{7,1},{8,10},{9,11},{10,... | collective-permute-start | bytes 811016 | tf_op jit(solution)/shard_map/ppermute | solution.py:351
  44.3 1.7 %collective-permute-start.12 = (bf16[528,256]{1,0:T(8,128)(2,1)S(1)}, bf16[528,256]{1,0:T(8,128)(2,1)}, u32[]{:S(2)}, u32[]{:S(2)}) collective-permute-start(bf16[528,256]{1,0:T(8,128)(2,1)S(1)} %collective-permute-done.8.refs_12_.refs_17_), channel_id=1, source_target_pairs={{0,24},{1,25},{2,26},{3,27},{4,28},{5,29},{6,30},{7,31},{8,0},{9,1... | collective-permute-start | bytes 811016 | tf_op jit(solution)/shard_map/ppermute | solution.py:351
  46.0 1.7 %plan.1 = (s32[8,128]{1,0:T(8,128)}, s32[8,128]{1,0:T(8,128)}) custom-call(s32[3]{0:T(128)} %pad_add_fusion.place, f32[8,128]{1,0:T(8,128)} %meta.1.own.refs_6_, f32[8,128]{1,0:T(8,128)} %copy-done.14), custom_call_target="tpu_custom_call" | custom-call | tf_op jit(solution)/shard_map/plan/pallas_call | solution.py:363
  47.7 3.5 %collective-permute-done.17.refs_20_.refs_25_ = bf16[528,256]{1,0:T(8,128)(2,1)} collective-permute-done((bf16[528,256]{1,0:T(8,128)(2,1)S(1)}, bf16[528,256]{1,0:T(8,128)(2,1)}, u32[]{:S(2)}, u32[]{:S(2)}) %collective-permute-start.17) | collective-permute-done | bytes 270368 | tf_op jit(solution)/shard_map/ppermute | solution.py:351
  51.3 22.7 %forward.1 = (f32[8,128]{1,0:T(8,128)}, f32[6,64,256]{2,1,0:T(8,128)}, bf16[64,256,256]{2,1,0:T(8,128)(2,1)}, bf16[64,256,256]{2,1,0:T(8,128)(2,1)}) custom-call(s32[8,128]{1,0:T(8,128)} %get-tuple-element.27.refs_0_, s32[8,128]{1,0:T(8,128)} %get-tuple-element.28.refs_1_, bf16[64,128,256]{2,1,0:T(8,128)(2,1)} %refs_2_.3, ...), custom_call_target="tpu_custom_call" | custom-call | tf_op jit(solution)/shard_map/forward/pallas_call | solution.py:372
  74.1 1.4 collective-permute-done.18.refs_5_
  76.1 28.3 %backward.1 = (f32[8,128]{1,0:T(8,128)}, bf16[528,256]{1,0:T(8,128)(2,1)}, bf16[528,256]{1,0:T(8,128)(2,1)}, bf16[528,256]{1,0:T(8,128)(2,1)}, bf16[528,256]{1,0...) custom-call(s32[8,128]{1,0:T(8,128)} %get-tuple-element.27.refs_0_, ...), custom_call_target="tpu_custom_call" | custom-call | tf_op jit(solution)/shard_map/backward/pallas_call | solution.py:396
  104.5 3.9 %collective-permute-start.21 = (bf16[528,256]{1,0:T(8,128)(2,1)}, bf16[528,256]{1,0:T(8,128)(2,1)S(1)}, u32[]{:S(2)}, u32[]{:S(2)}) collective-permute-start(bf16[528,256]{1,0:T(8,128)(2,1)} %get-tuple-element.39), channel_id=1, source_target_pairs={{0,6},{1,7},{2,0},{3,1},{4,2},{5,3},{6,4},{7,5},{8,14},{9,15},{10,... | collective-permute-start | bytes 811016 | tf_op jit(solution)/shard_map/ppermute | solution.py:422
  108.4 3.2 %collective-permute-start.19 = (bf16[528,256]{1,0:T(8,128)(2,1)}, bf16[528,256]{1,0:T(8,128)(2,1)S(1)}, u32[]{:S(2)}, u32[]{:S(2)}) collective-permute-start(bf16[528,256]{1,0:T(8,128)(2,1)} %get-tuple-element.35), channel_id=1, source_target_pairs={{0,24},{1,25},{2,26},{3,27},{4,28},{5,29},{6,30},{7,31},{8,0},{9,1... | collective-permute-start | bytes 811016 | tf_op jit(solution)/shard_map/ppermute | solution.py:422
  111.6 1.6 collective-permute-done.30
  113.2 3.2 %collective-permute-start.26 = (bf16[528,256]{1,0:T(8,128)(2,1)}, bf16[528,256]{1,0:T(8,128)(2,1)S(1)}, u32[]{:S(2)}, u32[]{:S(2)}) collective-permute-start(bf16[528,256]{1,0:T(8,128)(2,1)} %get-tuple-element.44), channel_id=1, source_target_pairs={{0,6},{1,7},{2,0},{3,1},{4,2},{5,3},{6,4},{7,5},{8,14},{9,15},{10,... | collective-permute-start | bytes 811016 | tf_op jit(solution)/shard_map/ppermute | solution.py:422
  120.2 2.7 %collective-permute-done.26 = bf16[528,256]{1,0:T(8,128)(2,1)S(1)} collective-permute-done((bf16[528,256]{1,0:T(8,128)(2,1)}, bf16[528,256]{1,0:T(8,128)(2,1)S(1)}, u32[]{:S(2)}, u32[]{:S(2)}) %collective-permute-start.26) | collective-permute-done | bytes 270368 | tf_op jit(solution)/shard_map/ppermute | solution.py:422
  123.9 3.8 %collective-permute-done.31 = bf16[528,256]{1,0:T(8,128)(2,1)S(1)} collective-permute-done((bf16[528,256]{1,0:T(8,128)(2,1)S(1)}, bf16[528,256]{1,0:T(8,128)(2,1)S(1)}, u32[]{:S(2)}, u32[]{:S(2)}) %collective-permute-start.31) | collective-permute-done | bytes 270368 | tf_op jit(solution)/shard_map/ppermute | solution.py:422
  129.5 1.6 collective-permute-start.29
  135.2 1.9 %collective-permute-start.28 = (bf16[528,256]{1,0:T(8,128)(2,1)S(1)}, bf16[528,256]{1,0:T(8,128)(2,1)S(1)}, u32[]{:S(2)}, u32[]{:S(2)}) collective-permute-start(bf16[528,256]{1,0:T(8,128)(2,1)S(1)} %add_convert_fusion.6), channel_id=1, source_target_pairs={{0,6},{1,7},{2,0},{3,1},{4,2},{5,3},{6,4},{7,5},{8,14},{9,15},{10,... | collective-permute-start | bytes 811016 | tf_op jit(solution)/shard_map/ppermute | solution.py:422
  137.1 4.1 %collective-permute-done.32 = bf16[528,256]{1,0:T(8,128)(2,1)S(1)} collective-permute-done((bf16[528,256]{1,0:T(8,128)(2,1)S(1)}, bf16[528,256]{1,0:T(8,128)(2,1)S(1)}, u32[]{:S(2)}, u32[]{:S(2)}) %collective-permute-start.32) | collective-permute-done | bytes 270368 | tf_op jit(solution)/shard_map/ppermute | solution.py:422
  142.4 7.6 %collective-permute-done.33 = bf16[528,256]{1,0:T(8,128)(2,1)S(1)} collective-permute-done((bf16[528,256]{1,0:T(8,128)(2,1)S(1)}, bf16[528,256]{1,0:T(8,128)(2,1)S(1)}, u32[]{:S(2)}, u32[]{:S(2)}) %collective-permute-start.33) | collective-permute-done | bytes 270368 | tf_op jit(solution)/shard_map/ppermute | solution.py:422
  151.1 2.0 %collective-permute-start.36 = (bf16[528,256]{1,0:T(8,128)(2,1)S(1)}, bf16[528,256]{1,0:T(8,128)(2,1)S(1)}, u32[]{:S(2)}, u32[]{:S(2)}) collective-permute-start(bf16[528,256]{1,0:T(8,128)(2,1)S(1)} %add_convert_fusion), channel_id=1, source_target_pairs={{0,64},{32,96},{64,0},{96,32},{1,65},{33,97},{65,1},{97,33},{2,66}... | collective-permute-start | bytes 811016 | tf_op jit(solution)/shard_map/ppermute | solution.py:427
  155.8 3.4 %collective-permute-done.36 = bf16[528,256]{1,0:T(8,128)(2,1)S(1)} collective-permute-done((bf16[528,256]{1,0:T(8,128)(2,1)S(1)}, bf16[528,256]{1,0:T(8,128)(2,1)S(1)}, u32[]{:S(2)}, u32[]{:S(2)}) %collective-permute-start.36) | collective-permute-done | bytes 270368 | tf_op jit(solution)/shard_map/ppermute | solution.py:427
  159.2 3.0 %collective-permute-done.35 = bf16[528,256]{1,0:T(8,128)(2,1)S(1)} collective-permute-done((bf16[528,256]{1,0:T(8,128)(2,1)S(1)}, bf16[528,256]{1,0:T(8,128)(2,1)S(1)}, u32[]{:S(2)}, u32[]{:S(2)}) %collective-permute-start.35) | collective-permute-done | bytes 270368 | tf_op jit(solution)/shard_map/ppermute | solution.py:427
  (97 shorter events, 25.4 us)
Async XLA Ops:
  0.6 50.6 %collective-permute-start.1 = (bf16[64,128,256]{2,1,0:T(8,128)(2,1)}, bf16[64,128,256]{2,1,0:T(8,128)(2,1)}, u32[]{:S(2)}, u32[]{:S(2)}) collective-permute-start(bf16[64,128,256]{2,1,0:T(8,128)(2,1)} %refs_2_.3), channel_id=1, source_target_pairs={{0,1},{1,0},{2,3},{3,2},{4,5},{5,4},{6,7},{7,6},{8,9},{9,8},{10,11... | collective-permute-start | bytes 12582920 | tf_op jit(solution)/shard_map/ppermute | solution.py:346
  1.7 16.0 %collective-permute-start.6 = (bf16[528,256]{1,0:T(8,128)(2,1)S(1)}, bf16[528,256]{1,0:T(8,128)(2,1)S(1)}, u32[]{:S(2)}, u32[]{:S(2)}) collective-permute-start(bf16[528,256]{1,0:T(8,128)(2,1)S(1)} %fusion.1.refs_6_.refs_11_), channel_id=1, source_target_pairs={{0,24},{1,25},{2,26},{3,27},{4,28},{5,29},{6,30},{7,31},{8,0},{9,1... | collective-permute-start | bytes 811016 | tf_op jit(solution)/shard_map/ppermute | solution.py:351
  5.9 15.1 %collective-permute-start.14 = (bf16[528,256]{1,0:T(8,128)(2,1)S(1)}, bf16[528,256]{1,0:T(8,128)(2,1)S(1)}, u32[]{:S(2)}, u32[]{:S(2)}) collective-permute-start(bf16[528,256]{1,0:T(8,128)(2,1)S(1)} %fusion.1.refs_6_.refs_11_), channel_id=1, source_target_pairs={{0,8},{1,9},{2,10},{3,11},{4,12},{5,13},{6,14},{7,15},{8,16},{9,17... | collective-permute-start | bytes 811016 | tf_op jit(solution)/shard_map/ppermute | solution.py:351
  5.9 15.8 %collective-permute-start.3 = (bf16[528,256]{1,0:T(8,128)(2,1)S(1)}, bf16[528,256]{1,0:T(8,128)(2,1)S(1)}, u32[]{:S(2)}, u32[]{:S(2)}) collective-permute-start(bf16[528,256]{1,0:T(8,128)(2,1)S(1)} %fusion.1.refs_6_.refs_11_), channel_id=1, source_target_pairs={{0,6},{1,7},{2,0},{3,1},{4,2},{5,3},{6,4},{7,5},{8,14},{9,15},{10,... | collective-permute-start | bytes 811016 | tf_op jit(solution)/shard_map/ppermute | solution.py:351
  17.8 10.5 %collective-permute-start.5 = (bf16[528,256]{1,0:T(8,128)(2,1)S(1)}, bf16[528,256]{1,0:T(8,128)(2,1)S(1)}, u32[]{:S(2)}, u32[]{:S(2)}) collective-permute-start(bf16[528,256]{1,0:T(8,128)(2,1)S(1)} %fusion.1.refs_6_.refs_11_), channel_id=1, source_target_pairs={{0,2},{1,3},{2,4},{3,5},{4,6},{5,7},{6,0},{7,1},{8,10},{9,11},{10,... | collective-permute-start | bytes 811016 | tf_op jit(solution)/shard_map/ppermute | solution.py:351
  17.8 10.5 %collective-permute-start.10 = (bf16[528,256]{1,0:T(8,128)(2,1)S(1)}, bf16[528,256]{1,0:T(8,128)(2,1)S(1)}, u32[]{:S(2)}, u32[]{:S(2)}) collective-permute-start(bf16[528,256]{1,0:T(8,128)(2,1)S(1)} %collective-permute-done.6.refs_10_.refs_15_), channel_id=1, source_target_pairs={{0,24},{1,25},{2,26},{3,27},{4,28},{5,29},{6,30},{7,31},{8,0},{9,1... | collective-permute-start | bytes 811016 | tf_op jit(solution)/shard_map/ppermute | solution.py:351
  21.1 12.2 %collective-permute-start.9 = (bf16[528,256]{1,0:T(8,128)(2,1)S(1)}, bf16[528,256]{1,0:T(8,128)(2,1)S(1)}, u32[]{:S(2)}, u32[]{:S(2)}) collective-permute-start(bf16[528,256]{1,0:T(8,128)(2,1)S(1)} %collective-permute-done.6.refs_10_.refs_15_), channel_id=1, source_target_pairs={{0,2},{1,3},{2,4},{3,5},{4,6},{5,7},{6,0},{7,1},{8,10},{9,11},{10,... | collective-permute-start | bytes 811016 | tf_op jit(solution)/shard_map/ppermute | solution.py:351
  21.8 11.6 %collective-permute-start.4 = (bf16[528,256]{1,0:T(8,128)(2,1)S(1)}, bf16[528,256]{1,0:T(8,128)(2,1)S(1)}, u32[]{:S(2)}, u32[]{:S(2)}) collective-permute-start(bf16[528,256]{1,0:T(8,128)(2,1)S(1)} %collective-permute-done.3.refs_7_.refs_12_), channel_id=1, source_target_pairs={{0,6},{1,7},{2,0},{3,1},{4,2},{5,3},{6,4},{7,5},{8,14},{9,15},{10,... | collective-permute-start | bytes 811016 | tf_op jit(solution)/shard_map/ppermute | solution.py:351
  28.3 8.3 %collective-permute-start.7 = (bf16[528,256]{1,0:T(8,128)(2,1)S(1)}, bf16[528,256]{1,0:T(8,128)(2,1)S(1)}, u32[]{:S(2)}, u32[]{:S(2)}) collective-permute-start(bf16[528,256]{1,0:T(8,128)(2,1)S(1)} %collective-permute-done.6.refs_10_.refs_15_), channel_id=1, source_target_pairs={{0,6},{1,7},{2,0},{3,1},{4,2},{5,3},{6,4},{7,5},{8,14},{9,15},{10,... | collective-permute-start | bytes 811016 | tf_op jit(solution)/shard_map/ppermute | solution.py:351
  28.3 9.1 %collective-permute-start.16 = (bf16[528,256]{1,0:T(8,128)(2,1)S(1)}, bf16[528,256]{1,0:T(8,128)(2,1)S(1)}, u32[]{:S(2)}, u32[]{:S(2)}) collective-permute-start(bf16[528,256]{1,0:T(8,128)(2,1)S(1)} %collective-permute-done.5.refs_9_.refs_14_), channel_id=1, source_target_pairs={{0,8},{1,9},{2,10},{3,11},{4,12},{5,13},{6,14},{7,15},{8,16},{9,17... | collective-permute-start | bytes 811016 | tf_op jit(solution)/shard_map/ppermute | solution.py:351
  33.3 9.3 %collective-permute-start.15 = (bf16[528,256]{1,0:T(8,128)(2,1)S(1)}, bf16[528,256]{1,0:T(8,128)(2,1)S(1)}, u32[]{:S(2)}, u32[]{:S(2)}) collective-permute-start(bf16[528,256]{1,0:T(8,128)(2,1)S(1)} %collective-permute-done.3.refs_7_.refs_12_), channel_id=1, source_target_pairs={{0,8},{1,9},{2,10},{3,11},{4,12},{5,13},{6,14},{7,15},{8,16},{9,17... | collective-permute-start | bytes 811016 | tf_op jit(solution)/shard_map/ppermute | solution.py:351
  33.3 10.9 %collective-permute-start.8 = (bf16[528,256]{1,0:T(8,128)(2,1)S(1)}, bf16[528,256]{1,0:T(8,128)(2,1)S(1)}, u32[]{:S(2)}, u32[]{:S(2)}) collective-permute-start(bf16[528,256]{1,0:T(8,128)(2,1)S(1)} %collective-permute-done.4.refs_8_.refs_13_), channel_id=1, source_target_pairs={{0,24},{1,25},{2,26},{3,27},{4,28},{5,29},{6,30},{7,31},{8,0},{9,1... | collective-permute-start | bytes 811016 | tf_op jit(solution)/shard_map/ppermute | solution.py:351
  36.6 11.1 %collective-permute-start.13 = (bf16[528,256]{1,0:T(8,128)(2,1)S(1)}, bf16[528,256]{1,0:T(8,128)(2,1)S(1)}, u32[]{:S(2)}, u32[]{:S(2)}) collective-permute-start(bf16[528,256]{1,0:T(8,128)(2,1)S(1)} %collective-permute-done.10.refs_14_.refs_19_), channel_id=1, source_target_pairs={{0,2},{1,3},{2,4},{3,5},{4,6},{5,7},{6,0},{7,1},{8,10},{9,11},{10,... | collective-permute-start | bytes 811016 | tf_op jit(solution)/shard_map/ppermute | solution.py:351
  37.4 10.3 %collective-permute-start.11 = (bf16[528,256]{1,0:T(8,128)(2,1)S(1)}, bf16[528,256]{1,0:T(8,128)(2,1)}, u32[]{:S(2)}, u32[]{:S(2)}) collective-permute-start(bf16[528,256]{1,0:T(8,128)(2,1)S(1)} %collective-permute-done.10.refs_14_.refs_19_), channel_id=1, source_target_pairs={{0,6},{1,7},{2,0},{3,1},{4,2},{5,3},{6,4},{7,5},{8,14},{9,15},{10,... | collective-permute-start | bytes 811016 | tf_op jit(solution)/shard_map/ppermute | solution.py:351
  42.6 8.6 %collective-permute-start.17 = (bf16[528,256]{1,0:T(8,128)(2,1)S(1)}, bf16[528,256]{1,0:T(8,128)(2,1)}, u32[]{:S(2)}, u32[]{:S(2)}) collective-permute-start(bf16[528,256]{1,0:T(8,128)(2,1)S(1)} %collective-permute-done.16.refs_21_.refs_26_), channel_id=1, source_target_pairs={{0,2},{1,3},{2,4},{3,5},{4,6},{5,7},{6,0},{7,1},{8,10},{9,11},{10,... | collective-permute-start | bytes 811016 | tf_op jit(solution)/shard_map/ppermute | solution.py:351
  104.4 8.8 %collective-permute-start.30 = (bf16[528,256]{1,0:T(8,128)(2,1)}, bf16[528,256]{1,0:T(8,128)(2,1)S(1)}, u32[]{:S(2)}, u32[]{:S(2)}) collective-permute-start(bf16[528,256]{1,0:T(8,128)(2,1)} %get-tuple-element.49), channel_id=1, source_target_pairs={{0,8},{1,9},{2,10},{3,11},{4,12},{5,13},{6,14},{7,15},{8,16},{9,17... | collective-permute-start | bytes 811016 | tf_op jit(solution)/shard_map/ppermute | solution.py:422
  104.5 13.0 %collective-permute-start.21 = (bf16[528,256]{1,0:T(8,128)(2,1)}, bf16[528,256]{1,0:T(8,128)(2,1)S(1)}, u32[]{:S(2)}, u32[]{:S(2)}) collective-permute-start(bf16[528,256]{1,0:T(8,128)(2,1)} %get-tuple-element.39), channel_id=1, source_target_pairs={{0,6},{1,7},{2,0},{3,1},{4,2},{5,3},{6,4},{7,5},{8,14},{9,15},{10,... | collective-permute-start | bytes 811016 | tf_op jit(solution)/shard_map/ppermute | solution.py:422
  108.4 10.7 %collective-permute-start.22 = (bf16[528,256]{1,0:T(8,128)(2,1)}, bf16[528,256]{1,0:T(8,128)(2,1)S(1)}, u32[]{:S(2)}, u32[]{:S(2)}) collective-permute-start(bf16[528,256]{1,0:T(8,128)(2,1)} %get-tuple-element.40), channel_id=1, source_target_pairs={{0,2},{1,3},{2,4},{3,5},{4,6},{5,7},{6,0},{7,1},{8,10},{9,11},{10,... | collective-permute-start | bytes 811016 | tf_op jit(solution)/shard_map/ppermute | solution.py:422
  108.4 33.9 %collective-permute-start.19 = (bf16[528,256]{1,0:T(8,128)(2,1)}, bf16[528,256]{1,0:T(8,128)(2,1)S(1)}, u32[]{:S(2)}, u32[]{:S(2)}) collective-permute-start(bf16[528,256]{1,0:T(8,128)(2,1)} %get-tuple-element.35), channel_id=1, source_target_pairs={{0,24},{1,25},{2,26},{3,27},{4,28},{5,29},{6,30},{7,31},{8,0},{9,1... | collective-permute-start | bytes 811016 | tf_op jit(solution)/shard_map/ppermute | solution.py:422
  111.5 17.9 %collective-permute-start.20 = (bf16[528,256]{1,0:T(8,128)(2,1)}, bf16[528,256]{1,0:T(8,128)(2,1)S(1)}, u32[]{:S(2)}, u32[]{:S(2)}) collective-permute-start(bf16[528,256]{1,0:T(8,128)(2,1)} %get-tuple-element.37), channel_id=1, source_target_pairs={{0,2},{1,3},{2,4},{3,5},{4,6},{5,7},{6,0},{7,1},{8,10},{9,11},{10,... | collective-permute-start | bytes 811016 | tf_op jit(solution)/shard_map/ppermute | solution.py:422
  113.2 9.7 %collective-permute-start.26 = (bf16[528,256]{1,0:T(8,128)(2,1)}, bf16[528,256]{1,0:T(8,128)(2,1)S(1)}, u32[]{:S(2)}, u32[]{:S(2)}) collective-permute-start(bf16[528,256]{1,0:T(8,128)(2,1)} %get-tuple-element.44), channel_id=1, source_target_pairs={{0,6},{1,7},{2,0},{3,1},{4,2},{5,3},{6,4},{7,5},{8,14},{9,15},{10,... | collective-permute-start | bytes 811016 | tf_op jit(solution)/shard_map/ppermute | solution.py:422
  117.4 13.6 %collective-permute-start.24 = (bf16[528,256]{1,0:T(8,128)(2,1)}, bf16[528,256]{1,0:T(8,128)(2,1)S(1)}, u32[]{:S(2)}, u32[]{:S(2)}) collective-permute-start(bf16[528,256]{1,0:T(8,128)(2,1)} %get-tuple-element.41), channel_id=1, source_target_pairs={{0,6},{1,7},{2,0},{3,1},{4,2},{5,3},{6,4},{7,5},{8,14},{9,15},{10,... | collective-permute-start | bytes 811016 | tf_op jit(solution)/shard_map/ppermute | solution.py:422
  119.1 8.6 %collective-permute-start.31 = (bf16[528,256]{1,0:T(8,128)(2,1)S(1)}, bf16[528,256]{1,0:T(8,128)(2,1)S(1)}, u32[]{:S(2)}, u32[]{:S(2)}) collective-permute-start(bf16[528,256]{1,0:T(8,128)(2,1)S(1)} %add_convert_fusion.3), channel_id=1, source_target_pairs={{0,8},{1,9},{2,10},{3,11},{4,12},{5,13},{6,14},{7,15},{8,16},{9,17... | collective-permute-start | bytes 811016 | tf_op jit(solution)/shard_map/ppermute | solution.py:422
  122.9 8.2 %collective-permute-start.23 = (bf16[528,256]{1,0:T(8,128)(2,1)S(1)}, bf16[528,256]{1,0:T(8,128)(2,1)S(1)}, u32[]{:S(2)}, u32[]{:S(2)}) collective-permute-start(bf16[528,256]{1,0:T(8,128)(2,1)S(1)} %add_convert_fusion.11), channel_id=1, source_target_pairs={{0,8},{1,9},{2,10},{3,11},{4,12},{5,13},{6,14},{7,15},{8,16},{9,17... | collective-permute-start | bytes 811016 | tf_op jit(solution)/shard_map/ppermute | solution.py:422
  129.5 7.6 %collective-permute-start.29 = (bf16[528,256]{1,0:T(8,128)(2,1)}, bf16[528,256]{1,0:T(8,128)(2,1)S(1)}, u32[]{:S(2)}, u32[]{:S(2)}) collective-permute-start(bf16[528,256]{1,0:T(8,128)(2,1)} %get-tuple-element.46), channel_id=1, source_target_pairs={{0,24},{1,25},{2,26},{3,27},{4,28},{5,29},{6,30},{7,31},{8,0},{9,1... | collective-permute-start | bytes 811016 | tf_op jit(solution)/shard_map/ppermute | solution.py:422
  131.1 10.1 %collective-permute-start.32 = (bf16[528,256]{1,0:T(8,128)(2,1)S(1)}, bf16[528,256]{1,0:T(8,128)(2,1)S(1)}, u32[]{:S(2)}, u32[]{:S(2)}) collective-permute-start(bf16[528,256]{1,0:T(8,128)(2,1)S(1)} %add_convert_fusion.2), channel_id=1, source_target_pairs={{0,2},{1,3},{2,4},{3,5},{4,6},{5,7},{6,0},{7,1},{8,10},{9,11},{10,... | collective-permute-start | bytes 811016 | tf_op jit(solution)/shard_map/ppermute | solution.py:422
  132.2 10.1 %collective-permute-start.25 = (bf16[528,256]{1,0:T(8,128)(2,1)S(1)}, bf16[528,256]{1,0:T(8,128)(2,1)S(1)}, u32[]{:S(2)}, u32[]{:S(2)}) collective-permute-start(bf16[528,256]{1,0:T(8,128)(2,1)S(1)} %add_convert_fusion.9), channel_id=1, source_target_pairs={{0,8},{1,9},{2,10},{3,11},{4,12},{5,13},{6,14},{7,15},{8,16},{9,17... | collective-permute-start | bytes 811016 | tf_op jit(solution)/shard_map/ppermute | solution.py:422
  135.2 7.2 %collective-permute-start.28 = (bf16[528,256]{1,0:T(8,128)(2,1)S(1)}, bf16[528,256]{1,0:T(8,128)(2,1)S(1)}, u32[]{:S(2)}, u32[]{:S(2)}) collective-permute-start(bf16[528,256]{1,0:T(8,128)(2,1)S(1)} %add_convert_fusion.6), channel_id=1, source_target_pairs={{0,6},{1,7},{2,0},{3,1},{4,2},{5,3},{6,4},{7,5},{8,14},{9,15},{10,... | collective-permute-start | bytes 811016 | tf_op jit(solution)/shard_map/ppermute | solution.py:422
  142.2 7.7 %collective-permute-start.33 = (bf16[528,256]{1,0:T(8,128)(2,1)S(1)}, bf16[528,256]{1,0:T(8,128)(2,1)S(1)}, u32[]{:S(2)}, u32[]{:S(2)}) collective-permute-start(bf16[528,256]{1,0:T(8,128)(2,1)S(1)} %add_convert_fusion.1), channel_id=1, source_target_pairs={{0,2},{1,3},{2,4},{3,5},{4,6},{5,7},{6,0},{7,1},{8,10},{9,11},{10,... | collective-permute-start | bytes 811016 | tf_op jit(solution)/shard_map/ppermute | solution.py:422
  151.1 8.1 %collective-permute-start.36 = (bf16[528,256]{1,0:T(8,128)(2,1)S(1)}, bf16[528,256]{1,0:T(8,128)(2,1)S(1)}, u32[]{:S(2)}, u32[]{:S(2)}) collective-permute-start(bf16[528,256]{1,0:T(8,128)(2,1)S(1)} %add_convert_fusion), channel_id=1, source_target_pairs={{0,64},{32,96},{64,0},{96,32},{1,65},{33,97},{65,1},{97,33},{2,66}... | collective-permute-start | bytes 811016 | tf_op jit(solution)/shard_map/ppermute | solution.py:427
  153.1 9.1 %collective-permute-start.35 = (bf16[528,256]{1,0:T(8,128)(2,1)S(1)}, bf16[528,256]{1,0:T(8,128)(2,1)S(1)}, u32[]{:S(2)}, u32[]{:S(2)}) collective-permute-start(bf16[528,256]{1,0:T(8,128)(2,1)S(1)} %add_convert_fusion), channel_id=1, source_target_pairs={{0,96},{32,0},{64,32},{96,64},{1,97},{33,1},{65,33},{97,65},{2,98}... | collective-permute-start | bytes 811016 | tf_op jit(solution)/shard_map/ppermute | solution.py:427
  154.1 8.2 %collective-permute-start.34 = (bf16[528,256]{1,0:T(8,128)(2,1)S(1)}, bf16[528,256]{1,0:T(8,128)(2,1)S(1)}, u32[]{:S(2)}, u32[]{:S(2)}) collective-permute-start(bf16[528,256]{1,0:T(8,128)(2,1)S(1)} %add_convert_fusion), channel_id=1, source_target_pairs={{0,32},{32,64},{64,96},{96,0},{1,33},{33,65},{65,97},{97,1},{2,34}... | collective-permute-start | bytes 811016 | tf_op jit(solution)/shard_map/ppermute | solution.py:427
  (22 other events, 404.2 us)

commit v2 on v1

v2 whole, which is shorter than its diff:
```python
import functools

import jax
import jax.numpy as jnp
from jax import lax
from jax.experimental import pallas as pl
from jax.experimental.pallas import tpu as pltpu
from jax.sharding import PartitionSpec as P

F32, BF16, I32 = jnp.float32, jnp.bfloat16, jnp.int32
G = 4
NS = 16
NP = 64
ROWS = 528
MIB = 1024 * 1024
HI = lax.Precision.HIGHEST

TREE = (
    ((0, 1), (0, 0), "x", 1),
    ((0, 3), (0, 0), "x", 3),
    ((1, 0), (0, 0), "z", 1),
    ((3, 0), (0, 0), "z", 3),
    ((0, 2), (0, 1), "x", 1),
    ((1, 3), (1, 0), "x", 3),
    ((2, 0), (1, 0), "z", 1),
    ((3, 3), (0, 3), "z", 3),
    ((1, 1), (1, 0), "x", 1),
    ((3, 1), (0, 1), "z", 3),
    ((1, 2), (0, 2), "z", 1),
    ((3, 2), (3, 3), "x", 3),
    ((2, 1), (2, 0), "x", 1),
    ((2, 3), (2, 0), "x", 3),
    ((2, 2), (1, 2), "z", 1),
)


def move(axis, step):
    pairs = []
    for z in range(4):
        for x in range(4):
            for c in range(2):
                z2, x2, c2 = z, x, c
                if axis == "z":
                    z2 = (z + step) % 4
                elif axis == "x":
                    x2 = (x + step) % 4
                else:
                    c2 = 1 - c
                pairs.append((z * 8 + x * 2 + c, z2 * 8 + x2 * 2 + c2))
    return pairs


def iota(shape, dim):
    return lax.broadcasted_iota(I32, shape, dim)


def meta_kernel(owner, region, order, target, delta, out):
    me = lax.axis_index("region")
    spot = region[...]
    slot = jnp.zeros((1, 64), I32)
    for r in range(32):
        slot = jnp.where(spot == r, owner[r], slot)
    dz = ((slot >> 3) - (me >> 3)) & 3
    dx = (((slot >> 1) & 3) - ((me >> 1) & 3)) & 3
    key = (dz * 4 + dx) * 2 + (slot & 1)
    rows = jnp.concatenate([order[...].astype(F32), target[...], jnp.zeros((1, 16), F32)], 0)
    ray = jnp.where((iota((16, 64), 1) >> 2) == iota((16, 64), 0), 1.0, 0.0)
    spread = jnp.dot(rows, ray, precision=HI, preferred_element_type=F32)
    pick = (iota((8, 64), 1) & 3) == iota((8, 64), 0)
    place = jnp.sum(jnp.where(pick, spread, 0.0), 0, keepdims=True)
    top = jnp.concatenate([key.astype(F32), place, spread[4:7], jnp.zeros((3, 64), F32)], 0)
    out[0:8, :] = jnp.concatenate([top, jnp.zeros((8, 64), F32)], 1)
    out[8:72, :] = delta[...].astype(F32)


def both(a, b):
    lane = iota(a.shape, 1)
    return jnp.where(lane < 64, a, pltpu.roll(b, 64, 1))


def plan_kernel(own, sib, table, code_out):
    meta = both(own[0:8], sib[0:8])
    key = meta[0:1].astype(I32)
    rel, valid = key >> 1, (key & 1) == (lax.axis_index("region") & 1)
    hot = (iota((NS, 128), 0) == rel) & valid
    hotf = jnp.where(hot, 1.0, 0.0)
    before = jnp.where(iota((128, 128), 0) < iota((128, 128), 1), 1.0, 0.0)
    cum = jnp.dot(hotf, before, preferred_element_type=F32)
    rank = jnp.sum(hotf * cum, 0, keepdims=True).astype(I32)
    count = jnp.sum(hotf, 1, keepdims=True).astype(I32)
    pairs = ((count + 1) >> 1).astype(F32)
    eye = iota((NS, 128), 0) == iota((NS, 128), 1)
    pairs_row = jnp.sum(jnp.where(eye, pairs, 0.0), 0, keepdims=True)
    ahead = iota((NS, 128), 1) < iota((NS, 128), 0)
    start = jnp.sum(jnp.where(ahead, pairs_row, 0.0), 1, keepdims=True)
    start_row = jnp.sum(jnp.where(eye, start, 0.0), 0, keepdims=True)
    start_j = jnp.sum(hotf * start, 0, keepdims=True).astype(I32)
    code = start_j + (rank >> 1) + (rank & 1) * NP
    code = jnp.where(valid, code, -1)
    square = iota((128, 128), 0) == iota((128, 128), 1)
    code_col = jnp.sum(jnp.where(square, code.astype(F32), 0.0), 1, keepdims=True)
    source = (iota((128, 128), 0) + 1).astype(F32)
    hit = code_col.astype(I32) == iota((128, 128), 1)
    inverse = jnp.sum(jnp.where(hit, source, 0.0), 0, keepdims=True).astype(I32)
    inverse = jnp.maximum(inverse - 1, 0)
    begun = jnp.where(start.astype(I32) <= iota((NS, 128), 1), 1.0, 0.0)
    slot_of = jnp.sum(begun, 0, keepdims=True).astype(I32) - 1
    total = jnp.sum(pairs_row, 1, keepdims=True).astype(I32)
    table[...] = jnp.concatenate(
        [
            inverse,
            slot_of,
            start_row.astype(I32),
            pairs_row.astype(I32),
            jnp.broadcast_to(total, (1, 128)),
            jnp.zeros((3, 128), I32),
        ],
        0,
    )
    code_out[...] = jnp.broadcast_to(code, (8, 128))


def fetch(table, own, sib, xs, sems, groups):
    def step(t, _):
        for g in range(G):
            for h in range(2):
                i = t * G + g
                src = table[0, h * NP + i]
                dst = xs.at[i, pl.ds(128 * h, 128)]

                @pl.when(src < 64)
                def _():
                    pltpu.make_async_copy(own.at[src], dst, sems.at[t]).start()

                @pl.when(src >= 64)
                def _():
                    pltpu.make_async_copy(sib.at[src - 64], dst, sems.at[t]).start()

        return 0

    lax.fori_loop(0, groups, step, 0)


def forward_kernel(*refs):
    table, code, own, sib, m_own, m_sib = refs[:6]
    weights = refs[6 : 6 + NS]
    res, saved, xs, wv, h1, h2 = refs[6 + NS : 12 + NS]
    raw, xsem, wsem = refs[12 + NS :]
    groups = (table[4, 0] + G - 1) // G
    for s in range(NS):
        pltpu.make_async_copy(weights[s], wv.at[s], wsem).start()
    fetch(table, own, sib, xs, xsem, groups)
    raw[...] = jnp.zeros(raw.shape, F32)
    pltpu.make_async_copy(wv, wv, wsem).wait()

    def step(t, _):
        ids = [G * t + g for g in range(G)]
        slots = [table[1, i] for i in ids]
        chunk = xs.at[pl.ds(G * t, G)]
        pltpu.make_async_copy(chunk, chunk, xsem.at[t]).wait()
        pre = [
            jnp.dot(xs[i], wv[s, 0:256], preferred_element_type=F32)
            for i, s in zip(ids, slots)
        ]
        one = [jnp.maximum(p, 0.0).astype(BF16) for p in pre]
        pre = [
            jnp.dot(o, wv[s, 256:512], preferred_element_type=F32) for o, s in zip(one, slots)
        ]
        two = [jnp.maximum(p, 0.0).astype(BF16) for p in pre]
        out = [
            lax.dot_general(
                wv[s, 512:528], o, (((1,), (1,)), ((), ())), preferred_element_type=F32
            )
            for o, s in zip(two, slots)
        ]
        for g, i in enumerate(ids):
            h1[i] = one[g]
            h2[i] = two[g]
            rows = pl.ds(pl.multiple_of(i * 8, 8), 8)
            raw[0, rows, :] = out[g][0:8, 0:128]
            raw[1, rows, :] = out[g][0:8, 128:256]
        return 0

    lax.fori_loop(0, groups, step, 0)

    before = jnp.where(iota((128, 128), 0) < iota((128, 128), 1), 1.0, 0.0)
    spot = code[0:1]
    out = jnp.zeros((4, 128), F32)
    for h in range(2):
        lanes = slice(h * 128, h * 128 + 128)
        pick = spot == iota((NP, 128), 0) + h * NP
        pickb = jnp.where(pick, 1.0, 0.0).astype(BF16)
        deltas = jnp.concatenate([m_own[8:72], m_sib[8:72]], 0).astype(BF16)
        delta = jnp.dot(pickb, deltas, preferred_element_type=F32)
        ch = [raw[h, pl.ds(c, NP, stride=8), :] for c in range(4)]
        sigma = jnp.maximum(ch[0], 0.0) + jnp.log1p(jnp.exp(-jnp.abs(ch[0])))
        rgb = [jax.nn.sigmoid(ch[c]) for c in (1, 2, 3)]
        tau = sigma * delta
        cum = jnp.dot(tau, before, precision=HI, preferred_element_type=F32)
        trans = jnp.exp(-cum)
        opacity = 1.0 - jnp.exp(-tau)
        weight = trans * opacity
        cols = [jnp.sum(weight * rgb[c], 1, keepdims=True) for c in range(3)]
        cols.append(-jnp.sum(tau, 1, keepdims=True))
        out += jnp.concatenate(
            [jnp.sum(jnp.where(pick, col, 0.0), 0, keepdims=True) for col in cols], 0
        )
        keep = rgb + [weight, trans * (1.0 - opacity), delta * jax.nn.sigmoid(ch[0])]
        for k in range(6):
            saved[k, :, lanes] = keep[k]
    res[...] = jnp.concatenate([out, jnp.zeros((4, 128), F32)], 0)


def backward_kernel(*refs):
    table, code, res, res_sib, m_own, m_sib, saved, xs, wv, h1, h2, color_out = refs[:12]
    grads = refs[12 : 12 + NS]
    dr, acc1, acc2, acc3, stage, gsem = refs[12 + NS :]
    groups = (table[4, 0] + G - 1) // G

    meta = both(m_own[0:8], m_sib[0:8])
    parts = res[...] + pltpu.roll(res_sib[...], 64, 1)
    order = meta[1:2]
    square = (128, 128)
    same = (iota(square, 0) >> 2) == (iota(square, 1) >> 2)
    samef = jnp.where(same, 1.0, 0.0)
    eye = iota(square, 0) == iota(square, 1)
    order_col = jnp.sum(jnp.where(eye, order, 0.0), 1, keepdims=True)
    prior = jnp.where(same & (order_col < order), 1.0, 0.0)
    later = jnp.where(same & (order_col > order), 1.0, 0.0)
    ahead = jnp.dot(parts, prior, precision=HI, preferred_element_type=F32)[3:4]
    reach = jnp.exp(ahead)
    shown = parts * reach
    color = jnp.dot(shown, samef, precision=HI, preferred_element_type=F32)
    color_out[...] = color
    gray = color[0:3] - meta[2:5]
    portion = jnp.sum(shown[0:3] * gray, 0, keepdims=True)
    log_cot = jnp.dot(
        jnp.broadcast_to(portion, (8, 128)), later, precision=HI, preferred_element_type=F32
    )[0:1]
    cot = [reach * gray[c : c + 1] for c in range(3)] + [log_cot]

    after = jnp.where(iota(square, 0) > iota(square, 1), 1.0, 0.0)
    spot = code[0:1]
    dr[...] = jnp.zeros(dr.shape, F32)
    for h in range(2):
        lanes = slice(h * 128, h * 128 + 128)
        pick = spot == iota((NP, 128), 0) + h * NP
        col = [jnp.sum(jnp.where(pick, row, 0.0), 1, keepdims=True) for row in cot]
        rgb = [saved[c, :, lanes] for c in range(3)]
        weight = saved[3, :, lanes]
        d_weight = rgb[0] * col[0] + rgb[1] * col[1] + rgb[2] * col[2]
        follow = jnp.dot(d_weight * weight, after, precision=HI, preferred_element_type=F32)
        d_tau = d_weight * saved[4, :, lanes] - col[3] - follow
        dr[h, pl.ds(0, NP, stride=8), :] = d_tau * saved[5, :, lanes]
        for c in range(3):
            d_col = weight * col[c] * rgb[c] * (1.0 - rgb[c])
            dr[h, pl.ds(c + 1, NP, stride=8), :] = d_col

    def send(s):
        pltpu.make_async_copy(stage.at[s], grads[s], gsem).start()

    for s in range(NS):

        @pl.when(table[3, s] == 0)
        def _():
            stage[s] = jnp.zeros((ROWS, 256), BF16)
            send(s)

    def step(t, _):
        ids = [G * t + g for g in range(G)]
        slots = [table[1, i] for i in ids]
        tn, nt = (((0,), (0,)), ((), ())), (((1,), (1,)), ((), ()))
        raws = []
        for i in ids:
            rows = pl.ds(pl.multiple_of(i * 8, 8), 8)
            d_raw = jnp.concatenate([dr[0, rows, :], dr[1, rows, :]], 1)
            raws.append(jnp.concatenate([d_raw, jnp.zeros((8, 256), F32)], 0).astype(BF16))
        two = [h2[i] for i in ids]
        dh = [
            lax.dot_general(r, wv[s, 512:528], tn, preferred_element_type=F32)
            for r, s in zip(raws, slots)
        ]
        d_two = [jnp.where(h > 0, d, 0.0).astype(BF16) for h, d in zip(two, dh)]
        one = [h1[i] for i in ids]
        dh = [
            lax.dot_general(d, wv[s, 256:512], nt, preferred_element_type=F32)
            for d, s in zip(d_two, slots)
        ]
        g3 = [jnp.dot(r, h, preferred_element_type=F32) for r, h in zip(raws, two)]
        g2 = [
            lax.dot_general(h, d, tn, preferred_element_type=F32) for h, d in zip(one, d_two)
        ]
        d_one = [jnp.where(h > 0, d, 0.0).astype(BF16) for h, d in zip(one, dh)]
        g1 = [
            lax.dot_general(xs[i], d, tn, preferred_element_type=F32)
            for i, d in zip(ids, d_one)
        ]
        for g, s in enumerate(slots):
            first = ids[g] == table[2, s]
            acc1[s] = jnp.where(first, 0.0, acc1[s]) + g1[g]
            acc2[s] = jnp.where(first, 0.0, acc2[s]) + g2[g]
            acc3[s] = jnp.where(first, 0.0, acc3[s]) + g3[g]
        return 0

    lax.fori_loop(0, groups, step, 0)
    for s in range(NS):

        @pl.when(table[3, s] > 0)
        def _():
            stage[s, 0:256] = acc1[s].astype(BF16)
            stage[s, 256:512] = acc2[s].astype(BF16)
            stage[s, 512:528] = acc3[s].astype(BF16)
            send(s)

    pltpu.make_async_copy(stage, stage, gsem).wait()


def spec(space):
    return pl.BlockSpec(memory_space=space)


def local(
    features, deltas, weight_one, weight_two, weight_out, target, block_region, seg_order, owner_map
):
    smem, vmem, hbm = spec(pltpu.SMEM), spec(pltpu.VMEM), spec(pl.ANY)
    shape = jax.ShapeDtypeStruct
    def swap(a):
        return lax.ppermute(a, "region", move("core", 1))

    head = jnp.pad(weight_out[0].T, ((0, 12), (0, 0)))
    held = {(0, 0): jnp.concatenate([weight_one[0], weight_two[0], head], 0)}
    for key, source, axis, step in TREE:
        held[key] = lax.ppermute(held[source], "region", move(axis, -step))
    weights = [held[(s // 4, s % 4)] for s in range(NS)]

    meta = pl.pallas_call(
        meta_kernel,
        out_shape=shape((72, 128), F32),
        in_specs=[smem, vmem, vmem, vmem, vmem],
        out_specs=vmem,
        name="meta",
    )(owner_map, block_region.T, seg_order.T, target.T, deltas)
    meta_sib, x_sib = swap(meta), swap(features)
    table, code = pl.pallas_call(
        plan_kernel,
        out_shape=(shape((8, 128), I32), shape((8, 128), I32)),
        in_specs=[vmem, vmem],
        out_specs=(vmem, vmem),
        name="plan",
    )(meta, meta_sib)

    dma = pltpu.SemaphoreType.DMA
    kept = pltpu.VMEM((NP, 256, 256), BF16)
    res, saved, xs, wv, h1, h2 = pl.pallas_call(
        forward_kernel,
        out_shape=(
            shape((8, 128), F32),
            pltpu.VMEM((6, NP, 256), F32),
            kept,
            pltpu.VMEM((NS, ROWS, 256), BF16),
            kept,
            kept,
        ),
        in_specs=[smem, vmem, hbm, hbm, vmem, vmem] + [hbm] * NS,
        out_specs=(vmem,) * 6,
        scratch_shapes=[pltpu.VMEM((2, NP * 8, 128), F32), dma((NP // G,)), dma],
        compiler_params=pltpu.CompilerParams(vmem_limit_bytes=8 * MIB),
        name="forward",
    )(table, code, features, x_sib, meta, meta_sib, *weights)
    res_sib = swap(res)
    color, *grads = pl.pallas_call(
        backward_kernel,
        out_shape=(shape((8, 128), F32),) + (shape((ROWS, 256), BF16),) * NS,
        in_specs=[smem] + [vmem] * 10,
        out_specs=(vmem,) + (hbm,) * NS,
        scratch_shapes=[
            pltpu.VMEM((2, NP * 8, 128), F32),
            pltpu.VMEM((NS, 256, 256), F32),
            pltpu.VMEM((NS, 256, 256), F32),
            pltpu.VMEM((NS, 16, 256), F32),
            pltpu.VMEM((NS, ROWS, 256), BF16),
            dma,
        ],
        compiler_params=pltpu.CompilerParams(vmem_limit_bytes=18 * MIB),
        name="backward",
    )(table, code, res, res_sib, meta, meta_sib, saved, xs, wv, h1, h2)

    sums = {(s // 4, s % 4): grads[s] for s in range(NS)}
    for key, source, axis, step in reversed(TREE):
        got = lax.ppermute(sums[key], "region", move(axis, step))
        sums[source] = (sums[source].astype(F32) + got.astype(F32)).astype(BF16)
    mine = sums[(0, 0)]
    total = mine.astype(F32)
    for d in (1, 3, 2):
        got = lax.ppermute(mine, "ray", [(i, (i + d) % 4) for i in range(4)])
        total = total + got.astype(F32)
    ray_color = color[0:3, 0:64:4].T
    return ray_color, total[None, 0:256], total[None, 256:512], total[512:516].T[None]


def solution(mesh):
    in_specs = (
        P(("ray", "region"), None, None),
        P(("ray", "region"), None),
        P("region", None, None),
        P("region", None, None),
        P("region", None, None),
        P(("ray", "region"), None),
        P(("ray", "region"), None),
        P(("ray", "region"), None),
        P(),
    )
    out_specs = (
        P(("ray", "region"), None),
        P("region", None, None),
        P("region", None, None),
        P("region", None, None),
    )
    return jax.shard_map(local, mesh=mesh, in_specs=in_specs, out_specs=out_specs, check_vma=False)
```

time: 167 us -> 139 us (0.83)
  Pallas kernels: 54.2 us -> 24.3 us
  other arithmetic: 10.3 us -> 2.01 us
  local copies, waits for them, and re-layouts: 6.8 us -> 13.9 us
  waiting for transfers between devices: 46.2 us -> 49.4 us
    pallas_call x1, Pallas kernels: 28.3 us -> 11.1 us  [local(): pl.pallas_call(backward_kernel, out_shape=(shape((8, 128), F32),) + (shap...]
    pallas_call x2, Pallas kernels: 24.3 us -> 11.4 us  [the longest x1 9.88 us: local(): pl.pallas_call(forward_kernel, out_shape=(shape((8, 128), F32), pltpu.VME...]
    convert_element_type x8, other arithmetic: 8.46 us -> 0.87 us  [local(): sums[source] = (sums[source].astype(F32) + got.astype(F32)).astype(BF16)]
    unnamed x37 -> x24, local copies, waits for them, and re-layouts: 4.71 us -> 11.8 us
    ppermute x15, waiting for transfers between devices: 22 us -> 26.5 us  [local(): got = lax.ppermute(sums[key], 'region', move(axis, step))]
    ppermute x4 -> x3, waiting for transfers between devices: 3.97 us -> 2.59 us  [swap(): return lax.ppermute(a, 'region', move('core', 1))]
  transfers between devices with their start and end apart: 37 -> 36, of which waited for: 16 -> 19; matrix products, arithmetic and copies ran while one was open for 8% -> 2% of each run, Pallas kernels for 2% -> 2%
where the time goes in v2:
time: 139 us; the launch traced here: 137 us
  waiting for transfers between devices  49.4 us (36%)
  starting transfers between devices  46.5 us (33%)
  Pallas kernels  24.3 us (17%)
  local copies, waits for them, and re-layouts  13.9 us (10%)
  other arithmetic  2.01 us (1%)
    ppermute x15, waiting for transfers between devices, local(): got = lax.ppermute(sums[key], 'region', move(axis, step))  26.5 us
    ppermute x15, starting transfers between devices, local(): held[key] = lax.ppermute(held[source], 'region', move(axis, -step))  25.1 us
    ppermute x15, starting transfers between devices, local(): got = lax.ppermute(sums[key], 'region', move(axis, step))  16 us
    ppermute x15, waiting for transfers between devices, local(): held[key] = lax.ppermute(held[source], 'region', move(axis, -step))  13.5 us
    unnamed x24, local copies, waits for them, and re-layouts  11.8 us
    pallas_call x1, Pallas kernels, local(): pl.pallas_call(backward_kernel, out_shape=(shape((8, 128), F32),) + (shap...  11.1 us
    pallas_call x1, Pallas kernels, local(): pl.pallas_call(forward_kernel, out_shape=(shape((8, 128), F32), pltpu.VME...  9.88 us
    ppermute x3, waiting for transfers between devices, local(): got = lax.ppermute(mine, 'ray', [(i, (i + d) % 4) for i in range(4)])  6.79 us
  transfers between devices with their start and end apart: 36, of which 19 were waited for; matrix products, arithmetic and copies ran while one was open for 2% of the time, Pallas kernels for 2%

profile of v2, /device:TPU:0, one launch (start us, length us, event | category | flops | bytes accessed | tf_op | source)
XLA Modules:
  0.0 136.9 jit_solution(813164992508507903)
XLA Ops:
  1.7 4.2 %collective-permute-start.5 = (bf16[528,256]{1,0:T(8,128)(2,1)S(1)}, bf16[528,256]{1,0:T(8,128)(2,1)S(1)}, u32[]{:S(2)}, u32[]{:S(2)}) collective-permute-start(bf16[528,256]{1,0:T(8,128)(2,1)S(1)} %fusion.1.refs_6_), channel_id=1, source_target_pairs={{0,24},{1,25},{2,26},{3,27},{4,28},{5,29},{6,30},{7,31},{8,0},{9,1... | collective-permute-start | bytes 811016 | tf_op jit(solution)/shard_map/ppermute | solution.py:333
  5.9 2.8 %collective-permute-start.2 = (bf16[528,256]{1,0:T(8,128)(2,1)S(1)}, bf16[528,256]{1,0:T(8,128)(2,1)S(1)}, u32[]{:S(2)}, u32[]{:S(2)}) collective-permute-start(bf16[528,256]{1,0:T(8,128)(2,1)S(1)} %fusion.1.refs_6_), channel_id=1, source_target_pairs={{0,6},{1,7},{2,0},{3,1},{4,2},{5,3},{6,4},{7,5},{8,14},{9,15},{10,... | collective-permute-start | bytes 811016 | tf_op jit(solution)/shard_map/ppermute | solution.py:333
  12.3 3.7 %collective-permute-start.9 = (bf16[528,256]{1,0:T(8,128)(2,1)S(1)}, bf16[528,256]{1,0:T(8,128)(2,1)S(1)}, u32[]{:S(2)}, u32[]{:S(2)}) collective-permute-start(bf16[528,256]{1,0:T(8,128)(2,1)S(1)} %collective-permute-done.5.refs_10_), channel_id=1, source_target_pairs={{0,24},{1,25},{2,26},{3,27},{4,28},{5,29},{6,30},{7,31},{8,0},{9,1... | collective-permute-start | bytes 811016 | tf_op jit(solution)/shard_map/ppermute | solution.py:333
  17.5 1.7 %collective-permute-start.3 = (bf16[528,256]{1,0:T(8,128)(2,1)S(1)}, bf16[528,256]{1,0:T(8,128)(2,1)S(1)}, u32[]{:S(2)}, u32[]{:S(2)}) collective-permute-start(bf16[528,256]{1,0:T(8,128)(2,1)S(1)} %collective-permute-done.2.refs_7_), channel_id=1, source_target_pairs={{0,6},{1,7},{2,0},{3,1},{4,2},{5,3},{6,4},{7,5},{8,14},{9,15},{10,... | collective-permute-start | bytes 811016 | tf_op jit(solution)/shard_map/ppermute | solution.py:333
  19.3 3.0 %collective-permute-done.4.refs_9_ = bf16[528,256]{1,0:T(8,128)(2,1)S(1)} collective-permute-done((bf16[528,256]{1,0:T(8,128)(2,1)S(1)}, bf16[528,256]{1,0:T(8,128)(2,1)S(1)}, u32[]{:S(2)}, u32[]{:S(2)}) %collective-permute-start.4) | collective-permute-done | bytes 270368 | tf_op jit(solution)/shard_map/ppermute | solution.py:333
  22.2 5.0 %collective-permute-done.8.refs_13_ = bf16[528,256]{1,0:T(8,128)(2,1)S(1)} collective-permute-done((bf16[528,256]{1,0:T(8,128)(2,1)S(1)}, bf16[528,256]{1,0:T(8,128)(2,1)S(1)}, u32[]{:S(2)}, u32[]{:S(2)}) %collective-permute-start.8) | collective-permute-done | bytes 270368 | tf_op jit(solution)/shard_map/ppermute | solution.py:333
  27.2 3.2 %collective-permute-start.7 = (bf16[528,256]{1,0:T(8,128)(2,1)S(1)}, bf16[528,256]{1,0:T(8,128)(2,1)S(1)}, u32[]{:S(2)}, u32[]{:S(2)}) collective-permute-start(bf16[528,256]{1,0:T(8,128)(2,1)S(1)} %collective-permute-done.3.refs_8_), channel_id=1, source_target_pairs={{0,24},{1,25},{2,26},{3,27},{4,28},{5,29},{6,30},{7,31},{8,0},{9,1... | collective-permute-start | bytes 811016 | tf_op jit(solution)/shard_map/ppermute | solution.py:333
  32.3 3.1 %collective-permute-start.10 = (bf16[528,256]{1,0:T(8,128)(2,1)S(1)}, bf16[528,256]{1,0:T(8,128)(2,1)}, u32[]{:S(2)}, u32[]{:S(2)}) collective-permute-start(bf16[528,256]{1,0:T(8,128)(2,1)S(1)} %collective-permute-done.9.refs_14_), channel_id=1, source_target_pairs={{0,6},{1,7},{2,0},{3,1},{4,2},{5,3},{6,4},{7,5},{8,14},{9,15},{10,... | collective-permute-start | bytes 811016 | tf_op jit(solution)/shard_map/ppermute | solution.py:333
  36.6 1.6 %collective-permute-start.16 = (bf16[528,256]{1,0:T(8,128)(2,1)S(1)}, bf16[528,256]{1,0:T(8,128)(2,1)}, u32[]{:S(2)}, u32[]{:S(2)}) collective-permute-start(bf16[528,256]{1,0:T(8,128)(2,1)S(1)} %collective-permute-done.15.refs_21_), channel_id=1, source_target_pairs={{0,2},{1,3},{2,4},{3,5},{4,6},{5,7},{6,0},{7,1},{8,10},{9,11},{10,... | collective-permute-start | bytes 811016 | tf_op jit(solution)/shard_map/ppermute | solution.py:333
  38.2 1.7 %collective-permute-start.11 = (bf16[528,256]{1,0:T(8,128)(2,1)S(1)}, bf16[528,256]{1,0:T(8,128)(2,1)}, u32[]{:S(2)}, u32[]{:S(2)}) collective-permute-start(bf16[528,256]{1,0:T(8,128)(2,1)S(1)} %collective-permute-done.7.refs_12_), channel_id=1, source_target_pairs={{0,24},{1,25},{2,26},{3,27},{4,28},{5,29},{6,30},{7,31},{8,0},{9,1... | collective-permute-start | bytes 811016 | tf_op jit(solution)/shard_map/ppermute | solution.py:333
  39.9 1.8 %plan.1 = (s32[8,128]{1,0:T(8,128)}, s32[8,128]{1,0:T(8,128)}) custom-call(f32[72,128]{1,0:T(8,128)} %meta.1.own.refs_4_, f32[72,128]{1,0:T(8,128)} %copy-done.5), custom_call_target="tpu_custom_call" | custom-call | tf_op jit(solution)/shard_map/plan/pallas_call | solution.py:344
  41.7 3.4 %collective-permute-done.16.refs_20_ = bf16[528,256]{1,0:T(8,128)(2,1)} collective-permute-done((bf16[528,256]{1,0:T(8,128)(2,1)S(1)}, bf16[528,256]{1,0:T(8,128)(2,1)}, u32[]{:S(2)}, u32[]{:S(2)}) %collective-permute-start.16) | collective-permute-done | bytes 270368 | tf_op jit(solution)/shard_map/ppermute | solution.py:333
  45.1 2.2 %copy-done.2 = bf16[64,128,256]{2,1,0:T(8,128)(2,1)S(1)} copy-done((bf16[64,128,256]{2,1,0:T(8,128)(2,1)S(1)}, bf16[64,128,256]{2,1,0:T(8,128)(2,1)}, u32[]{:S(2)}) %copy-start.2) | copy-done | bytes 4194328
  50.2 9.9 %forward.1 = (f32[8,128]{1,0:T(8,128)S(1)}, f32[6,64,256]{2,1,0:T(8,128)S(1)}, bf16[64,256,256]{2,1,0:T(8,128)(2,1)S(1)}, bf16[16,528,256]{2,1,0:T(8,128)(2,1)S(...) custom-call(s32[8,128]{1,0:T(8,128)S(1)} %copy-done.8, s32[8,128]{1,0:T(8,128)S(1)} %copy-done.10, ...), custom_call_target="tpu_custom_call" | custom-call | tf_op jit(solution)/shard_map/forward/pallas_call | solution.py:354
  60.1 3.3 %copy-done = bf16[64,256,256]{2,1,0:T(8,128)(2,1)} copy-done((bf16[64,256,256]{2,1,0:T(8,128)(2,1)}, bf16[64,256,256]{2,1,0:T(8,128)(2,1)S(1)}, u32[]{:S(2)}) %copy-start) | copy-done | bytes 8388632
  64.6 3.4 %copy-done.1 = bf16[64,256,256]{2,1,0:T(8,128)(2,1)S(1)} copy-done((bf16[64,256,256]{2,1,0:T(8,128)(2,1)S(1)}, bf16[64,256,256]{2,1,0:T(8,128)(2,1)}, u32[]{:S(2)}) %copy-start.1) | copy-done | bytes 8388632
  68.0 11.1 %backward.1 = (f32[8,128]{1,0:T(8,128)S(1)}, bf16[528,256]{1,0:T(8,128)(2,1)S(1)}, bf16[528,256]{1,0:T(8,128)(2,1)S(1)}, bf16[528,256]{1,0:T(8,128)(2,1)S(1)}, b...) custom-call(s32[8,128]{1,0:T(8,128)S(1)} %copy-done.9, ...), custom_call_target="tpu_custom_call" | custom-call | tf_op jit(solution)/shard_map/backward/pallas_call | solution.py:371
  79.2 2.0 %collective-permute-start.20 = (bf16[528,256]{1,0:T(8,128)(2,1)S(1)}, bf16[528,256]{1,0:T(8,128)(2,1)S(1)}, u32[]{:S(2)}, u32[]{:S(2)}) collective-permute-start(bf16[528,256]{1,0:T(8,128)(2,1)S(1)} %get-tuple-element.43), channel_id=1, source_target_pairs={{0,6},{1,7},{2,0},{3,1},{4,2},{5,3},{6,4},{7,5},{8,14},{9,15},{10,... | collective-permute-start | bytes 811016 | tf_op jit(solution)/shard_map/ppermute | solution.py:390
  81.5 3.0 %collective-permute-start.18 = (bf16[528,256]{1,0:T(8,128)(2,1)S(1)}, bf16[528,256]{1,0:T(8,128)(2,1)S(1)}, u32[]{:S(2)}, u32[]{:S(2)}) collective-permute-start(bf16[528,256]{1,0:T(8,128)(2,1)S(1)} %get-tuple-element.39), channel_id=1, source_target_pairs={{0,24},{1,25},{2,26},{3,27},{4,28},{5,29},{6,30},{7,31},{8,0},{9,1... | collective-permute-start | bytes 811016 | tf_op jit(solution)/shard_map/ppermute | solution.py:390
  85.4 4.1 %collective-permute-done.29 = bf16[528,256]{1,0:T(8,128)(2,1)S(1)} collective-permute-done((bf16[528,256]{1,0:T(8,128)(2,1)S(1)}, bf16[528,256]{1,0:T(8,128)(2,1)S(1)}, u32[]{:S(2)}, u32[]{:S(2)}) %collective-permute-start.29) | collective-permute-done | bytes 270368 | tf_op jit(solution)/shard_map/ppermute | solution.py:390
  89.5 1.8 %collective-permute-start.25 = (bf16[528,256]{1,0:T(8,128)(2,1)S(1)}, bf16[528,256]{1,0:T(8,128)(2,1)S(1)}, u32[]{:S(2)}, u32[]{:S(2)}) collective-permute-start(bf16[528,256]{1,0:T(8,128)(2,1)S(1)} %get-tuple-element.48), channel_id=1, source_target_pairs={{0,6},{1,7},{2,0},{3,1},{4,2},{5,3},{6,4},{7,5},{8,14},{9,15},{10,... | collective-permute-start | bytes 811016 | tf_op jit(solution)/shard_map/ppermute | solution.py:390
  92.7 6.1 %collective-permute-done.25 = bf16[528,256]{1,0:T(8,128)(2,1)S(1)} collective-permute-done((bf16[528,256]{1,0:T(8,128)(2,1)S(1)}, bf16[528,256]{1,0:T(8,128)(2,1)S(1)}, u32[]{:S(2)}, u32[]{:S(2)}) %collective-permute-start.25) | collective-permute-done | bytes 270368 | tf_op jit(solution)/shard_map/ppermute | solution.py:390
  98.9 2.7 %collective-permute-done.30 = bf16[528,256]{1,0:T(8,128)(2,1)S(1)} collective-permute-done((bf16[528,256]{1,0:T(8,128)(2,1)S(1)}, bf16[528,256]{1,0:T(8,128)(2,1)S(1)}, u32[]{:S(2)}, u32[]{:S(2)}) %collective-permute-start.30) | collective-permute-done | bytes 270368 | tf_op jit(solution)/shard_map/ppermute | solution.py:390
  101.7 2.5 %collective-permute-start.26 = (bf16[528,256]{1,0:T(8,128)(2,1)S(1)}, bf16[528,256]{1,0:T(8,128)(2,1)S(1)}, u32[]{:S(2)}, u32[]{:S(2)}) collective-permute-start(bf16[528,256]{1,0:T(8,128)(2,1)S(1)} %add_convert_fusion.7), channel_id=1, source_target_pairs={{0,24},{1,25},{2,26},{3,27},{4,28},{5,29},{6,30},{7,31},{8,0},{9,1... | collective-permute-start | bytes 811016 | tf_op jit(solution)/shard_map/ppermute | solution.py:390
  105.7 1.8 %collective-permute-done.22 = bf16[528,256]{1,0:T(8,128)(2,1)S(1)} collective-permute-done((bf16[528,256]{1,0:T(8,128)(2,1)S(1)}, bf16[528,256]{1,0:T(8,128)(2,1)S(1)}, u32[]{:S(2)}, u32[]{:S(2)}) %collective-permute-start.22) | collective-permute-done | bytes 270368 | tf_op jit(solution)/shard_map/ppermute | solution.py:390
  107.7 3.4 %collective-permute-done.26 = bf16[528,256]{1,0:T(8,128)(2,1)S(1)} collective-permute-done((bf16[528,256]{1,0:T(8,128)(2,1)S(1)}, bf16[528,256]{1,0:T(8,128)(2,1)S(1)}, u32[]{:S(2)}, u32[]{:S(2)}) %collective-permute-start.26) | collective-permute-done | bytes 270368 | tf_op jit(solution)/shard_map/ppermute | solution.py:390
  112.3 2.2 %collective-permute-done.28 = bf16[528,256]{1,0:T(8,128)(2,1)S(1)} collective-permute-done((bf16[528,256]{1,0:T(8,128)(2,1)S(1)}, bf16[528,256]{1,0:T(8,128)(2,1)S(1)}, u32[]{:S(2)}, u32[]{:S(2)}) %collective-permute-start.28) | collective-permute-done | bytes 270368 | tf_op jit(solution)/shard_map/ppermute | solution.py:390
  114.6 1.6 %collective-permute-start.32 = (bf16[528,256]{1,0:T(8,128)(2,1)S(1)}, bf16[528,256]{1,0:T(8,128)(2,1)S(1)}, u32[]{:S(2)}, u32[]{:S(2)}) collective-permute-start(bf16[528,256]{1,0:T(8,128)(2,1)S(1)} %add_convert_fusion.1), channel_id=1, source_target_pairs={{0,2},{1,3},{2,4},{3,5},{4,6},{5,7},{6,0},{7,1},{8,10},{9,11},{10,... | collective-permute-start | bytes 811016 | tf_op jit(solution)/shard_map/ppermute | solution.py:390
  117.7 4.7 %collective-permute-done.32 = bf16[528,256]{1,0:T(8,128)(2,1)S(1)} collective-permute-done((bf16[528,256]{1,0:T(8,128)(2,1)S(1)}, bf16[528,256]{1,0:T(8,128)(2,1)S(1)}, u32[]{:S(2)}, u32[]{:S(2)}) %collective-permute-start.32) | collective-permute-done | bytes 270368 | tf_op jit(solution)/shard_map/ppermute | solution.py:390
  122.6 3.3 %collective-permute-start.35 = (bf16[528,256]{1,0:T(8,128)(2,1)S(1)}, bf16[528,256]{1,0:T(8,128)(2,1)S(1)}, u32[]{:S(2)}, u32[]{:S(2)}) collective-permute-start(bf16[528,256]{1,0:T(8,128)(2,1)S(1)} %add_convert_fusion), channel_id=1, source_target_pairs={{0,64},{32,96},{64,0},{96,32},{1,65},{33,97},{65,1},{97,33},{2,66}... | collective-permute-start | bytes 811016 | tf_op jit(solution)/shard_map/ppermute | solution.py:395
  128.5 3.6 %collective-permute-done.35 = bf16[528,256]{1,0:T(8,128)(2,1)S(1)} collective-permute-done((bf16[528,256]{1,0:T(8,128)(2,1)S(1)}, bf16[528,256]{1,0:T(8,128)(2,1)S(1)}, u32[]{:S(2)}, u32[]{:S(2)}) %collective-permute-start.35) | collective-permute-done | bytes 270368 | tf_op jit(solution)/shard_map/ppermute | solution.py:395
  133.4 1.9 %collective-permute-done.33 = bf16[528,256]{1,0:T(8,128)(2,1)S(1)} collective-permute-done((bf16[528,256]{1,0:T(8,128)(2,1)S(1)}, bf16[528,256]{1,0:T(8,128)(2,1)S(1)}, u32[]{:S(2)}, u32[]{:S(2)}) %collective-permute-start.33) | collective-permute-done | bytes 270368 | tf_op jit(solution)/shard_map/ppermute | solution.py:395
  (81 shorter events, 26.4 us)
Async XLA Ops:
  0.6 44.5 %collective-permute-start.1 = (bf16[64,128,256]{2,1,0:T(8,128)(2,1)}, bf16[64,128,256]{2,1,0:T(8,128)(2,1)}, u32[]{:S(2)}, u32[]{:S(2)}) collective-permute-start(bf16[64,128,256]{2,1,0:T(8,128)(2,1)} %refs_2_.1), channel_id=1, source_target_pairs={{0,1},{1,0},{2,3},{3,2},{4,5},{5,4},{6,7},{7,6},{8,9},{9,8},{10,11... | collective-permute-start | bytes 12582920 | tf_op jit(solution)/shard_map/ppermute | solution.py:328
  1.7 10.6 %collective-permute-start.5 = (bf16[528,256]{1,0:T(8,128)(2,1)S(1)}, bf16[528,256]{1,0:T(8,128)(2,1)S(1)}, u32[]{:S(2)}, u32[]{:S(2)}) collective-permute-start(bf16[528,256]{1,0:T(8,128)(2,1)S(1)} %fusion.1.refs_6_), channel_id=1, source_target_pairs={{0,24},{1,25},{2,26},{3,27},{4,28},{5,29},{6,30},{7,31},{8,0},{9,1... | collective-permute-start | bytes 811016 | tf_op jit(solution)/shard_map/ppermute | solution.py:333
  5.9 10.1 %collective-permute-start.13 = (bf16[528,256]{1,0:T(8,128)(2,1)S(1)}, bf16[528,256]{1,0:T(8,128)(2,1)S(1)}, u32[]{:S(2)}, u32[]{:S(2)}) collective-permute-start(bf16[528,256]{1,0:T(8,128)(2,1)S(1)} %fusion.1.refs_6_), channel_id=1, source_target_pairs={{0,8},{1,9},{2,10},{3,11},{4,12},{5,13},{6,14},{7,15},{8,16},{9,17... | collective-permute-start | bytes 811016 | tf_op jit(solution)/shard_map/ppermute | solution.py:333
  5.9 11.6 %collective-permute-start.2 = (bf16[528,256]{1,0:T(8,128)(2,1)S(1)}, bf16[528,256]{1,0:T(8,128)(2,1)S(1)}, u32[]{:S(2)}, u32[]{:S(2)}) collective-permute-start(bf16[528,256]{1,0:T(8,128)(2,1)S(1)} %fusion.1.refs_6_), channel_id=1, source_target_pairs={{0,6},{1,7},{2,0},{3,1},{4,2},{5,3},{6,4},{7,5},{8,14},{9,15},{10,... | collective-permute-start | bytes 811016 | tf_op jit(solution)/shard_map/ppermute | solution.py:333
  11.7 10.5 %collective-permute-start.4 = (bf16[528,256]{1,0:T(8,128)(2,1)S(1)}, bf16[528,256]{1,0:T(8,128)(2,1)S(1)}, u32[]{:S(2)}, u32[]{:S(2)}) collective-permute-start(bf16[528,256]{1,0:T(8,128)(2,1)S(1)} %fusion.1.refs_6_), channel_id=1, source_target_pairs={{0,2},{1,3},{2,4},{3,5},{4,6},{5,7},{6,0},{7,1},{8,10},{9,11},{10,... | collective-permute-start | bytes 811016 | tf_op jit(solution)/shard_map/ppermute | solution.py:333
  12.3 9.9 %collective-permute-start.9 = (bf16[528,256]{1,0:T(8,128)(2,1)S(1)}, bf16[528,256]{1,0:T(8,128)(2,1)S(1)}, u32[]{:S(2)}, u32[]{:S(2)}) collective-permute-start(bf16[528,256]{1,0:T(8,128)(2,1)S(1)} %collective-permute-done.5.refs_10_), channel_id=1, source_target_pairs={{0,24},{1,25},{2,26},{3,27},{4,28},{5,29},{6,30},{7,31},{8,0},{9,1... | collective-permute-start | bytes 811016 | tf_op jit(solution)/shard_map/ppermute | solution.py:333
  16.0 11.2 %collective-permute-start.8 = (bf16[528,256]{1,0:T(8,128)(2,1)S(1)}, bf16[528,256]{1,0:T(8,128)(2,1)S(1)}, u32[]{:S(2)}, u32[]{:S(2)}) collective-permute-start(bf16[528,256]{1,0:T(8,128)(2,1)S(1)} %collective-permute-done.5.refs_10_), channel_id=1, source_target_pairs={{0,2},{1,3},{2,4},{3,5},{4,6},{5,7},{6,0},{7,1},{8,10},{9,11},{10,... | collective-permute-start | bytes 811016 | tf_op jit(solution)/shard_map/ppermute | solution.py:333
  17.5 9.7 %collective-permute-start.3 = (bf16[528,256]{1,0:T(8,128)(2,1)S(1)}, bf16[528,256]{1,0:T(8,128)(2,1)S(1)}, u32[]{:S(2)}, u32[]{:S(2)}) collective-permute-start(bf16[528,256]{1,0:T(8,128)(2,1)S(1)} %collective-permute-done.2.refs_7_), channel_id=1, source_target_pairs={{0,6},{1,7},{2,0},{3,1},{4,2},{5,3},{6,4},{7,5},{8,14},{9,15},{10,... | collective-permute-start | bytes 811016 | tf_op jit(solution)/shard_map/ppermute | solution.py:333
  22.2 8.6 %collective-permute-start.6 = (bf16[528,256]{1,0:T(8,128)(2,1)S(1)}, bf16[528,256]{1,0:T(8,128)(2,1)S(1)}, u32[]{:S(2)}, u32[]{:S(2)}) collective-permute-start(bf16[528,256]{1,0:T(8,128)(2,1)S(1)} %collective-permute-done.5.refs_10_), channel_id=1, source_target_pairs={{0,6},{1,7},{2,0},{3,1},{4,2},{5,3},{6,4},{7,5},{8,14},{9,15},{10,... | collective-permute-start | bytes 811016 | tf_op jit(solution)/shard_map/ppermute | solution.py:333
  22.2 10.1 %collective-permute-start.15 = (bf16[528,256]{1,0:T(8,128)(2,1)S(1)}, bf16[528,256]{1,0:T(8,128)(2,1)S(1)}, u32[]{:S(2)}, u32[]{:S(2)}) collective-permute-start(bf16[528,256]{1,0:T(8,128)(2,1)S(1)} %collective-permute-done.4.refs_9_), channel_id=1, source_target_pairs={{0,8},{1,9},{2,10},{3,11},{4,12},{5,13},{6,14},{7,15},{8,16},{9,17... | collective-permute-start | bytes 811016 | tf_op jit(solution)/shard_map/ppermute | solution.py:333
  27.2 9.3 %collective-permute-start.14 = (bf16[528,256]{1,0:T(8,128)(2,1)S(1)}, bf16[528,256]{1,0:T(8,128)(2,1)S(1)}, u32[]{:S(2)}, u32[]{:S(2)}) collective-permute-start(bf16[528,256]{1,0:T(8,128)(2,1)S(1)} %collective-permute-done.2.refs_7_), channel_id=1, source_target_pairs={{0,8},{1,9},{2,10},{3,11},{4,12},{5,13},{6,14},{7,15},{8,16},{9,17... | collective-permute-start | bytes 811016 | tf_op jit(solution)/shard_map/ppermute | solution.py:333
  27.2 11.0 %collective-permute-start.7 = (bf16[528,256]{1,0:T(8,128)(2,1)S(1)}, bf16[528,256]{1,0:T(8,128)(2,1)S(1)}, u32[]{:S(2)}, u32[]{:S(2)}) collective-permute-start(bf16[528,256]{1,0:T(8,128)(2,1)S(1)} %collective-permute-done.3.refs_8_), channel_id=1, source_target_pairs={{0,24},{1,25},{2,26},{3,27},{4,28},{5,29},{6,30},{7,31},{8,0},{9,1... | collective-permute-start | bytes 811016 | tf_op jit(solution)/shard_map/ppermute | solution.py:333
  30.8 10.9 %collective-permute-start.12 = (bf16[528,256]{1,0:T(8,128)(2,1)S(1)}, bf16[528,256]{1,0:T(8,128)(2,1)}, u32[]{:S(2)}, u32[]{:S(2)}) collective-permute-start(bf16[528,256]{1,0:T(8,128)(2,1)S(1)} %collective-permute-done.9.refs_14_), channel_id=1, source_target_pairs={{0,2},{1,3},{2,4},{3,5},{4,6},{5,7},{6,0},{7,1},{8,10},{9,11},{10,... | collective-permute-start | bytes 811016 | tf_op jit(solution)/shard_map/ppermute | solution.py:333
  32.3 9.4 %collective-permute-start.10 = (bf16[528,256]{1,0:T(8,128)(2,1)S(1)}, bf16[528,256]{1,0:T(8,128)(2,1)}, u32[]{:S(2)}, u32[]{:S(2)}) collective-permute-start(bf16[528,256]{1,0:T(8,128)(2,1)S(1)} %collective-permute-done.9.refs_14_), channel_id=1, source_target_pairs={{0,6},{1,7},{2,0},{3,1},{4,2},{5,3},{6,4},{7,5},{8,14},{9,15},{10,... | collective-permute-start | bytes 811016 | tf_op jit(solution)/shard_map/ppermute | solution.py:333
  36.6 8.5 %collective-permute-start.16 = (bf16[528,256]{1,0:T(8,128)(2,1)S(1)}, bf16[528,256]{1,0:T(8,128)(2,1)}, u32[]{:S(2)}, u32[]{:S(2)}) collective-permute-start(bf16[528,256]{1,0:T(8,128)(2,1)S(1)} %collective-permute-done.15.refs_21_), channel_id=1, source_target_pairs={{0,2},{1,3},{2,4},{3,5},{4,6},{5,7},{6,0},{7,1},{8,10},{9,11},{10,... | collective-permute-start | bytes 811016 | tf_op jit(solution)/shard_map/ppermute | solution.py:333
  79.1 10.4 %collective-permute-start.29 = (bf16[528,256]{1,0:T(8,128)(2,1)S(1)}, bf16[528,256]{1,0:T(8,128)(2,1)S(1)}, u32[]{:S(2)}, u32[]{:S(2)}) collective-permute-start(bf16[528,256]{1,0:T(8,128)(2,1)S(1)} %get-tuple-element.53), channel_id=1, source_target_pairs={{0,8},{1,9},{2,10},{3,11},{4,12},{5,13},{6,14},{7,15},{8,16},{9,17... | collective-permute-start | bytes 811016 | tf_op jit(solution)/shard_map/ppermute | solution.py:390
  79.2 12.2 %collective-permute-start.20 = (bf16[528,256]{1,0:T(8,128)(2,1)S(1)}, bf16[528,256]{1,0:T(8,128)(2,1)S(1)}, u32[]{:S(2)}, u32[]{:S(2)}) collective-permute-start(bf16[528,256]{1,0:T(8,128)(2,1)S(1)} %get-tuple-element.43), channel_id=1, source_target_pairs={{0,6},{1,7},{2,0},{3,1},{4,2},{5,3},{6,4},{7,5},{8,14},{9,15},{10,... | collective-permute-start | bytes 811016 | tf_op jit(solution)/shard_map/ppermute | solution.py:390
  81.2 11.3 %collective-permute-start.21 = (bf16[528,256]{1,0:T(8,128)(2,1)S(1)}, bf16[528,256]{1,0:T(8,128)(2,1)S(1)}, u32[]{:S(2)}, u32[]{:S(2)}) collective-permute-start(bf16[528,256]{1,0:T(8,128)(2,1)S(1)} %get-tuple-element.44), channel_id=1, source_target_pairs={{0,2},{1,3},{2,4},{3,5},{4,6},{5,7},{6,0},{7,1},{8,10},{9,11},{10,... | collective-permute-start | bytes 811016 | tf_op jit(solution)/shard_map/ppermute | solution.py:390
  81.5 34.7 %collective-permute-start.18 = (bf16[528,256]{1,0:T(8,128)(2,1)S(1)}, bf16[528,256]{1,0:T(8,128)(2,1)S(1)}, u32[]{:S(2)}, u32[]{:S(2)}) collective-permute-start(bf16[528,256]{1,0:T(8,128)(2,1)S(1)} %get-tuple-element.39), channel_id=1, source_target_pairs={{0,24},{1,25},{2,26},{3,27},{4,28},{5,29},{6,30},{7,31},{8,0},{9,1... | collective-permute-start | bytes 811016 | tf_op jit(solution)/shard_map/ppermute | solution.py:390
  84.5 19.8 %collective-permute-start.19 = (bf16[528,256]{1,0:T(8,128)(2,1)S(1)}, bf16[528,256]{1,0:T(8,128)(2,1)S(1)}, u32[]{:S(2)}, u32[]{:S(2)}) collective-permute-start(bf16[528,256]{1,0:T(8,128)(2,1)S(1)} %get-tuple-element.41), channel_id=1, source_target_pairs={{0,2},{1,3},{2,4},{3,5},{4,6},{5,7},{6,0},{7,1},{8,10},{9,11},{10,... | collective-permute-start | bytes 811016 | tf_op jit(solution)/shard_map/ppermute | solution.py:390
  89.5 9.3 %collective-permute-start.25 = (bf16[528,256]{1,0:T(8,128)(2,1)S(1)}, bf16[528,256]{1,0:T(8,128)(2,1)S(1)}, u32[]{:S(2)}, u32[]{:S(2)}) collective-permute-start(bf16[528,256]{1,0:T(8,128)(2,1)S(1)} %get-tuple-element.48), channel_id=1, source_target_pairs={{0,6},{1,7},{2,0},{3,1},{4,2},{5,3},{6,4},{7,5},{8,14},{9,15},{10,... | collective-permute-start | bytes 811016 | tf_op jit(solution)/shard_map/ppermute | solution.py:390
  91.4 14.3 %collective-permute-start.23 = (bf16[528,256]{1,0:T(8,128)(2,1)S(1)}, bf16[528,256]{1,0:T(8,128)(2,1)S(1)}, u32[]{:S(2)}, u32[]{:S(2)}) collective-permute-start(bf16[528,256]{1,0:T(8,128)(2,1)S(1)} %get-tuple-element.45), channel_id=1, source_target_pairs={{0,6},{1,7},{2,0},{3,1},{4,2},{5,3},{6,4},{7,5},{8,14},{9,15},{10,... | collective-permute-start | bytes 811016 | tf_op jit(solution)/shard_map/ppermute | solution.py:390
  92.5 9.2 %collective-permute-start.30 = (bf16[528,256]{1,0:T(8,128)(2,1)S(1)}, bf16[528,256]{1,0:T(8,128)(2,1)S(1)}, u32[]{:S(2)}, u32[]{:S(2)}) collective-permute-start(bf16[528,256]{1,0:T(8,128)(2,1)S(1)} %add_convert_fusion.3), channel_id=1, source_target_pairs={{0,8},{1,9},{2,10},{3,11},{4,12},{5,13},{6,14},{7,15},{8,16},{9,17... | collective-permute-start | bytes 811016 | tf_op jit(solution)/shard_map/ppermute | solution.py:390
  98.8 8.6 %collective-permute-start.22 = (bf16[528,256]{1,0:T(8,128)(2,1)S(1)}, bf16[528,256]{1,0:T(8,128)(2,1)S(1)}, u32[]{:S(2)}, u32[]{:S(2)}) collective-permute-start(bf16[528,256]{1,0:T(8,128)(2,1)S(1)} %add_convert_fusion.11), channel_id=1, source_target_pairs={{0,8},{1,9},{2,10},{3,11},{4,12},{5,13},{6,14},{7,15},{8,16},{9,17... | collective-permute-start | bytes 811016 | tf_op jit(solution)/shard_map/ppermute | solution.py:390
  101.7 9.4 %collective-permute-start.26 = (bf16[528,256]{1,0:T(8,128)(2,1)S(1)}, bf16[528,256]{1,0:T(8,128)(2,1)S(1)}, u32[]{:S(2)}, u32[]{:S(2)}) collective-permute-start(bf16[528,256]{1,0:T(8,128)(2,1)S(1)} %add_convert_fusion.7), channel_id=1, source_target_pairs={{0,24},{1,25},{2,26},{3,27},{4,28},{5,29},{6,30},{7,31},{8,0},{9,1... | collective-permute-start | bytes 811016 | tf_op jit(solution)/shard_map/ppermute | solution.py:390
  104.2 10.2 %collective-permute-start.28 = (bf16[528,256]{1,0:T(8,128)(2,1)S(1)}, bf16[528,256]{1,0:T(8,128)(2,1)S(1)}, u32[]{:S(2)}, u32[]{:S(2)}) collective-permute-start(bf16[528,256]{1,0:T(8,128)(2,1)S(1)} %get-tuple-element.50), channel_id=1, source_target_pairs={{0,24},{1,25},{2,26},{3,27},{4,28},{5,29},{6,30},{7,31},{8,0},{9,1... | collective-permute-start | bytes 811016 | tf_op jit(solution)/shard_map/ppermute | solution.py:390
  105.7 8.8 %collective-permute-start.31 = (bf16[528,256]{1,0:T(8,128)(2,1)S(1)}, bf16[528,256]{1,0:T(8,128)(2,1)S(1)}, u32[]{:S(2)}, u32[]{:S(2)}) collective-permute-start(bf16[528,256]{1,0:T(8,128)(2,1)S(1)} %add_convert_fusion.2), channel_id=1, source_target_pairs={{0,2},{1,3},{2,4},{3,5},{4,6},{5,7},{6,0},{7,1},{8,10},{9,11},{10,... | collective-permute-start | bytes 811016 | tf_op jit(solution)/shard_map/ppermute | solution.py:390
  107.6 8.6 %collective-permute-start.24 = (bf16[528,256]{1,0:T(8,128)(2,1)S(1)}, bf16[528,256]{1,0:T(8,128)(2,1)S(1)}, u32[]{:S(2)}, u32[]{:S(2)}) collective-permute-start(bf16[528,256]{1,0:T(8,128)(2,1)S(1)} %add_convert_fusion.9), channel_id=1, source_target_pairs={{0,8},{1,9},{2,10},{3,11},{4,12},{5,13},{6,14},{7,15},{8,16},{9,17... | collective-permute-start | bytes 811016 | tf_op jit(solution)/shard_map/ppermute | solution.py:390
  114.6 7.7 %collective-permute-start.32 = (bf16[528,256]{1,0:T(8,128)(2,1)S(1)}, bf16[528,256]{1,0:T(8,128)(2,1)S(1)}, u32[]{:S(2)}, u32[]{:S(2)}) collective-permute-start(bf16[528,256]{1,0:T(8,128)(2,1)S(1)} %add_convert_fusion.1), channel_id=1, source_target_pairs={{0,2},{1,3},{2,4},{3,5},{4,6},{5,7},{6,0},{7,1},{8,10},{9,11},{10,... | collective-permute-start | bytes 811016 | tf_op jit(solution)/shard_map/ppermute | solution.py:390
  122.6 9.5 %collective-permute-start.35 = (bf16[528,256]{1,0:T(8,128)(2,1)S(1)}, bf16[528,256]{1,0:T(8,128)(2,1)S(1)}, u32[]{:S(2)}, u32[]{:S(2)}) collective-permute-start(bf16[528,256]{1,0:T(8,128)(2,1)S(1)} %add_convert_fusion), channel_id=1, source_target_pairs={{0,64},{32,96},{64,0},{96,32},{1,65},{33,97},{65,1},{97,33},{2,66}... | collective-permute-start | bytes 811016 | tf_op jit(solution)/shard_map/ppermute | solution.py:395
  125.8 7.6 %collective-permute-start.34 = (bf16[528,256]{1,0:T(8,128)(2,1)S(1)}, bf16[528,256]{1,0:T(8,128)(2,1)S(1)}, u32[]{:S(2)}, u32[]{:S(2)}) collective-permute-start(bf16[528,256]{1,0:T(8,128)(2,1)S(1)} %add_convert_fusion), channel_id=1, source_target_pairs={{0,96},{32,0},{64,32},{96,64},{1,97},{33,1},{65,33},{97,65},{2,98}... | collective-permute-start | bytes 811016 | tf_op jit(solution)/shard_map/ppermute | solution.py:395
  126.8 8.5 %collective-permute-start.33 = (bf16[528,256]{1,0:T(8,128)(2,1)S(1)}, bf16[528,256]{1,0:T(8,128)(2,1)S(1)}, u32[]{:S(2)}, u32[]{:S(2)}) collective-permute-start(bf16[528,256]{1,0:T(8,128)(2,1)S(1)} %add_convert_fusion), channel_id=1, source_target_pairs={{0,32},{32,64},{64,96},{96,0},{1,33},{33,65},{65,97},{97,1},{2,34}... | collective-permute-start | bytes 811016 | tf_op jit(solution)/shard_map/ppermute | solution.py:395
  (16 other events, 153.5 us)

commit v3 on v2

--- a/solution.py
+++ b/solution.py
@@ -78,7 +78,12 @@
     return jnp.where(lane < 64, a, pltpu.roll(b, 64, 1))
 
 
-def plan_kernel(own, sib, table, code_out):
+def plan_kernel(own, sib, x_own, x_sib, table, info, xa, sems):
+    copies = []
+    for k in range(8):
+        src = (x_own, x_sib)[k // 4].at[pl.ds(k % 4 * 16, 16)]
+        copies.append(pltpu.make_async_copy(src, xa.at[pl.ds(k * 16, 16)], sems.at[k]))
+        copies[k].start()
     meta = both(own[0:8], sib[0:8])
     key = meta[0:1].astype(I32)
     rel, valid = key >> 1, (key & 1) == (lax.axis_index("region") & 1)
@@ -117,49 +122,38 @@
         ],
         0,
     )
-    code_out[...] = jnp.broadcast_to(code, (8, 128))
-
-
-def fetch(table, own, sib, xs, sems, groups):
-    def step(t, _):
-        for g in range(G):
-            for h in range(2):
-                i = t * G + g
-                src = table[0, h * NP + i]
-                dst = xs.at[i, pl.ds(128 * h, 128)]
-
-                @pl.when(src < 64)
-                def _():
-                    pltpu.make_async_copy(own.at[src], dst, sems.at[t]).start()
-
-                @pl.when(src >= 64)
-                def _():
-                    pltpu.make_async_copy(sib.at[src - 64], dst, sems.at[t]).start()
-
-        return 0
-
-    lax.fori_loop(0, groups, step, 0)
+    info[0:8, :] = meta
+    info[8:16, :] = jnp.broadcast_to(code, (8, 128)).astype(F32)
+    info[16:80, :] = own[8:72]
+    info[80:144, :] = sib[8:72]
+    for copy in copies:
+        copy.wait()
+
+
+def samples(table, xa, i):
+    return jnp.concatenate([xa[table[0, i]], xa[table[0, NP + i]]], 0)
 
 
 def forward_kernel(*refs):
-    table, code, own, sib, m_own, m_sib = refs[:6]
-    weights = refs[6 : 6 + NS]
-    res, saved, xs, wv, h1, h2 = refs[6 + NS : 12 + NS]
-    raw, xsem, wsem = refs[12 + NS :]
+    table, info, xa = refs[:3]
+    weights = refs[3 : 3 + NS]
+    res, saved, wv, h1, h2 = refs[3 + NS : 8 + NS]
+    raw, wsem = refs[8 + NS :]
     groups = (table[4, 0] + G - 1) // G
     for s in range(NS):
-        pltpu.make_async_copy(weights[s], wv.at[s], wsem).start()
-    fetch(table, own, sib, xs, xsem, groups)
+        pltpu.make_async_copy(weights[s], wv.at[s], wsem.at[s]).start()
     raw[...] = jnp.zeros(raw.shape, F32)
-    pltpu.make_async_copy(wv, wv, wsem).wait()
-
-    def step(t, _):
+
+    def held(s, _):
+        pltpu.make_async_copy(weights[0], wv.at[s], wsem.at[s]).wait()
+        return 0
+
+    def step(t, ready):
         ids = [G * t + g for g in range(G)]
         slots = [table[1, i] for i in ids]
-        chunk = xs.at[pl.ds(G * t, G)]
-        pltpu.make_async_copy(chunk, chunk, xsem.at[t]).wait()
+        lax.fori_loop(ready, slots[-1] + 1, held, 0)
         pre = [
-            jnp.dot(xs[i], wv[s, 0:256], preferred_element_type=F32)
+            jnp.dot(samples(table, xa, i), wv[s, 0:256], preferred_element_type=F32)
             for i, s in zip(ids, slots)
         ]
         one = [jnp.maximum(p, 0.0).astype(BF16) for p in pre]
@@ -179,18 +173,18 @@
             rows = pl.ds(pl.multiple_of(i * 8, 8), 8)
             raw[0, rows, :] = out[g][0:8, 0:128]
             raw[1, rows, :] = out[g][0:8, 128:256]
-        return 0
-
-    lax.fori_loop(0, groups, step, 0)
+        return slots[-1] + 1
+
+    lax.fori_loop(lax.fori_loop(0, groups, step, 0), NS, held, 0)
 
     before = jnp.where(iota((128, 128), 0) < iota((128, 128), 1), 1.0, 0.0)
-    spot = code[0:1]
+    spot = info[8:9].astype(I32)
     out = jnp.zeros((4, 128), F32)
     for h in range(2):
         lanes = slice(h * 128, h * 128 + 128)
         pick = spot == iota((NP, 128), 0) + h * NP
         pickb = jnp.where(pick, 1.0, 0.0).astype(BF16)
-        deltas = jnp.concatenate([m_own[8:72], m_sib[8:72]], 0).astype(BF16)
+        deltas = info[16:144].astype(BF16)
         delta = jnp.dot(pickb, deltas, preferred_element_type=F32)
         ch = [raw[h, pl.ds(c, NP, stride=8), :] for c in range(4)]
         sigma = jnp.maximum(ch[0], 0.0) + jnp.log1p(jnp.exp(-jnp.abs(ch[0])))
@@ -212,12 +206,12 @@
 
 
 def backward_kernel(*refs):
-    table, code, res, res_sib, m_own, m_sib, saved, xs, wv, h1, h2, color_out = refs[:12]
-    grads = refs[12 : 12 + NS]
-    dr, acc1, acc2, acc3, stage, gsem = refs[12 + NS :]
+    table, info, res, res_sib, xa, saved, wv, h1, h2, color_out = refs[:10]
+    grads = refs[10 : 10 + NS]
+    dr, acc1, acc2, acc3 = refs[10 + NS :]
     groups = (table[4, 0] + G - 1) // G
 
-    meta = both(m_own[0:8], m_sib[0:8])
+    meta = info[0:8]
     parts = res[...] + pltpu.roll(res_sib[...], 64, 1)
     order = meta[1:2]
     square = (128, 128)
@@ -240,7 +234,7 @@
     cot = [reach * gray[c : c + 1] for c in range(3)] + [log_cot]
 
     after = jnp.where(iota(square, 0) > iota(square, 1), 1.0, 0.0)
-    spot = code[0:1]
+    spot = info[8:9].astype(I32)
     dr[...] = jnp.zeros(dr.shape, F32)
     for h in range(2):
         lanes = slice(h * 128, h * 128 + 128)
@@ -256,15 +250,11 @@
             d_col = weight * col[c] * rgb[c] * (1.0 - rgb[c])
             dr[h, pl.ds(c + 1, NP, stride=8), :] = d_col
 
-    def send(s):
-        pltpu.make_async_copy(stage.at[s], grads[s], gsem).start()
-
     for s in range(NS):
 
         @pl.when(table[3, s] == 0)
         def _():
-            stage[s] = jnp.zeros((ROWS, 256), BF16)
-            send(s)
+            grads[s][...] = jnp.zeros((ROWS, 256), BF16)
 
     def step(t, _):
         ids = [G * t + g for g in range(G)]
@@ -292,7 +282,7 @@
         ]
         d_one = [jnp.where(h > 0, d, 0.0).astype(BF16) for h, d in zip(one, dh)]
         g1 = [
-            lax.dot_general(xs[i], d, tn, preferred_element_type=F32)
+            lax.dot_general(samples(table, xa, i), d, tn, preferred_element_type=F32)
             for i, d in zip(ids, d_one)
         ]
         for g, s in enumerate(slots):
@@ -307,12 +297,9 @@
 
         @pl.when(table[3, s] > 0)
         def _():
-            stage[s, 0:256] = acc1[s].astype(BF16)
-            stage[s, 256:512] = acc2[s].astype(BF16)
-            stage[s, 512:528] = acc3[s].astype(BF16)
-            send(s)
-
-    pltpu.make_async_copy(stage, stage, gsem).wait()
+            grads[s][0:256] = acc1[s].astype(BF16)
+            grads[s][256:512] = acc2[s].astype(BF16)
+            grads[s][512:528] = acc3[s].astype(BF16)
 
 
 def spec(space):
@@ -323,13 +310,24 @@
     features, deltas, weight_one, weight_two, weight_out, target, block_region, seg_order, owner_map
 ):
     smem, vmem, hbm = spec(pltpu.SMEM), spec(pltpu.VMEM), spec(pl.ANY)
+    far = spec(pltpu.MemorySpace.HBM)
     shape = jax.ShapeDtypeStruct
+    dma = pltpu.SemaphoreType.DMA
+    limit = pltpu.CompilerParams(vmem_limit_bytes=15 * MIB)
+
+    def away(a):
+        return pltpu.with_memory_space_constraint(a, pltpu.MemorySpace.HBM)
+
     def swap(a):
         return lax.ppermute(a, "region", move("core", 1))
 
     head = jnp.pad(weight_out[0].T, ((0, 12), (0, 0)))
     held = {(0, 0): jnp.concatenate([weight_one[0], weight_two[0], head], 0)}
-    for key, source, axis, step in TREE:
+    x_sib = swap(features)
+    for key, source, axis, step in TREE[:4]:
+        held[key] = lax.ppermute(held[source], "region", move(axis, -step))
+    x_sib, held[(1, 0)] = lax.optimization_barrier((x_sib, held[(1, 0)]))
+    for key, source, axis, step in TREE[4:]:
         held[key] = lax.ppermute(held[source], "region", move(axis, -step))
     weights = [held[(s // 4, s % 4)] for s in range(NS)]
 
@@ -340,50 +338,48 @@
         out_specs=vmem,
         name="meta",
     )(owner_map, block_region.T, seg_order.T, target.T, deltas)
-    meta_sib, x_sib = swap(meta), swap(features)
-    table, code = pl.pallas_call(
+    meta_sib = swap(meta)
+    table, info, xa = pl.pallas_call(
         plan_kernel,
-        out_shape=(shape((8, 128), I32), shape((8, 128), I32)),
-        in_specs=[vmem, vmem],
-        out_specs=(vmem, vmem),
+        out_shape=(shape((8, 128), I32), pltpu.VMEM((144, 128), F32), pltpu.VMEM((128, 128, 256), BF16)),
+        in_specs=[vmem, vmem, far, hbm],
+        out_specs=(vmem,) * 3,
+        scratch_shapes=[dma((8,))],
+        compiler_params=limit,
         name="plan",
-    )(meta, meta_sib)
-
-    dma = pltpu.SemaphoreType.DMA
+    )(meta, meta_sib, away(features), x_sib)
+
     kept = pltpu.VMEM((NP, 256, 256), BF16)
-    res, saved, xs, wv, h1, h2 = pl.pallas_call(
+    res, saved, wv, h1, h2 = pl.pallas_call(
         forward_kernel,
         out_shape=(
             shape((8, 128), F32),
             pltpu.VMEM((6, NP, 256), F32),
-            kept,
             pltpu.VMEM((NS, ROWS, 256), BF16),
             kept,
             kept,
         ),
-        in_specs=[smem, vmem, hbm, hbm, vmem, vmem] + [hbm] * NS,
-        out_specs=(vmem,) * 6,
-        scratch_shapes=[pltpu.VMEM((2, NP * 8, 128), F32), dma((NP // G,)), dma],
-        compiler_params=pltpu.CompilerParams(vmem_limit_bytes=8 * MIB),
+        in_specs=[smem, vmem, vmem] + [hbm] * NS,
+        out_specs=(vmem,) * 5,
+        scratch_shapes=[pltpu.VMEM((2, NP * 8, 128), F32), dma((NS,))],
+        compiler_params=limit,
         name="forward",
-    )(table, code, features, x_sib, meta, meta_sib, *weights)
+    )(table, info, xa, *weights)
     res_sib = swap(res)
     color, *grads = pl.pallas_call(
         backward_kernel,
-        out_shape=(shape((8, 128), F32),) + (shape((ROWS, 256), BF16),) * NS,
-        in_specs=[smem] + [vmem] * 10,
-        out_specs=(vmem,) + (hbm,) * NS,
+        out_shape=(shape((8, 128), F32),) + (pltpu.VMEM((ROWS, 256), BF16),) * NS,
+        in_specs=[smem] + [vmem] * 8,
+        out_specs=(vmem,) * (NS + 1),
         scratch_shapes=[
             pltpu.VMEM((2, NP * 8, 128), F32),
             pltpu.VMEM((NS, 256, 256), F32),
             pltpu.VMEM((NS, 256, 256), F32),
             pltpu.VMEM((NS, 16, 256), F32),
-            pltpu.VMEM((NS, ROWS, 256), BF16),
-            dma,
         ],
-        compiler_params=pltpu.CompilerParams(vmem_limit_bytes=18 * MIB),
+        compiler_params=limit,
         name="backward",
-    )(table, code, res, res_sib, meta, meta_sib, saved, xs, wv, h1, h2)
+    )(table, info, res, res_sib, xa, saved, wv, h1, h2)
 
     sums = {(s // 4, s % 4): grads[s] for s in range(NS)}
     for key, source, axis, step in reversed(TREE):

time: 139 us -> 127 us (0.914); the launches traced: 137 us -> 127 us
  local copies, waits for them, and re-layouts: 13.9 us -> 2.86 us
  starting transfers between devices: 46.5 us -> 51.3 us
  Pallas kernels: 24.3 us -> 22.3 us
  waiting for transfers between devices: 49.4 us -> 47.8 us
    unnamed x24 -> x2, local copies, waits for them, and re-layouts: 11.8 us -> 0.77 us
    ppermute x15, starting transfers between devices: 25.1 us -> 31.1 us  [local(): held[key] = lax.ppermute(held[source], 'region', move(axis, -step))]
    pallas_call x1, Pallas kernels: 9.88 us -> 6.34 us  [local(): pl.pallas_call(forward_kernel, out_shape=(shape((8, 128), F32), pltpu.VME...]
    ppermute x15, waiting for transfers between devices: 13.5 us -> 10.7 us  [local(): held[key] = lax.ppermute(held[source], 'region', move(axis, -step))]
    ppermute x15, waiting for transfers between devices: 26.5 us -> 28.1 us  [local(): got = lax.ppermute(sums[key], 'region', move(axis, step))]
    pallas_call x2, Pallas kernels: 12.9 us -> 14.4 us  [the longest x1 10.9 us: local(): pl.pallas_call(backward_kernel, out_shape=(shape((8, 128), F32),) + (pltp...]
    ppermute x3, waiting for transfers between devices: 2.59 us -> 1.16 us  [swap(): return lax.ppermute(a, 'region', move('core', 1))]
  transfers between devices with their start and end apart: 36 -> 36, of which waited for: 19 -> 18; matrix products, arithmetic and copies ran while one was open for 2% -> 2% of each run, Pallas kernels for 2% -> 4%
where the time goes in v3:
time: 127 us
  starting transfers between devices  51.3 us (40%)
  waiting for transfers between devices  47.8 us (38%)
  Pallas kernels  22.3 us (18%)
  local copies, waits for them, and re-layouts  2.86 us (2%)
  other arithmetic  1.99 us (2%)
    ppermute x15, starting transfers between devices, local(): held[key] = lax.ppermute(held[source], 'region', move(axis, -step))  31.1 us
    ppermute x15, waiting for transfers between devices, local(): got = lax.ppermute(sums[key], 'region', move(axis, step))  28.1 us
    ppermute x15, starting transfers between devices, local(): got = lax.ppermute(sums[key], 'region', move(axis, step))  14.7 us
    pallas_call x1, Pallas kernels, local(): pl.pallas_call(backward_kernel, out_shape=(shape((8, 128), F32),) + (pltp...  10.9 us
    ppermute x15, waiting for transfers between devices, local(): held[key] = lax.ppermute(held[source], 'region', move(axis, -step))  10.7 us
    ppermute x3, waiting for transfers between devices, local(): got = lax.ppermute(mine, 'ray', [(i, (i + d) % 4) for i in range(4)])  7.76 us
    pallas_call x1, Pallas kernels, local(): pl.pallas_call(forward_kernel, out_shape=(shape((8, 128), F32), pltpu.VME...  6.34 us
    ppermute x3, starting transfers between devices, local(): got = lax.ppermute(mine, 'ray', [(i, (i + d) % 4) for i in range(4)])  5.27 us
  transfers between devices with their start and end apart: 36, of which 18 were waited for; matrix products, arithmetic and copies ran while one was open for 2% of the time, Pallas kernels for 4%

profile of v3, /device:TPU:0, one launch (start us, length us, event | category | flops | bytes accessed | tf_op | source)
XLA Modules:
  0.0 127.0 jit_solution(16358064684916728434)
XLA Ops:
  1.7 2.9 %collective-permute-start.3 = (bf16[528,256]{1,0:T(8,128)(2,1)S(1)}, bf16[528,256]{1,0:T(8,128)(2,1)S(1)}, u32[]{:S(2)}, u32[]{:S(2)}) collective-permute-start(bf16[528,256]{1,0:T(8,128)(2,1)S(1)} %fusion.1.refs_3_), channel_id=1, source_target_pairs={{0,6},{1,7},{2,0},{3,1},{4,2},{5,3},{6,4},{7,5},{8,14},{9,15},{10,... | collective-permute-start | bytes 811016 | tf_op jit(solution)/shard_map/ppermute | solution.py:328
  4.6 4.0 %collective-permute-start.2 = (bf16[528,256]{1,0:T(8,128)(2,1)S(1)}, bf16[528,256]{1,0:T(8,128)(2,1)S(1)}, u32[]{:S(2)}, u32[]{:S(2)}) collective-permute-start(bf16[528,256]{1,0:T(8,128)(2,1)S(1)} %fusion.1.refs_3_), channel_id=1, source_target_pairs={{0,24},{1,25},{2,26},{3,27},{4,28},{5,29},{6,30},{7,31},{8,0},{9,1... | collective-permute-start | bytes 811016 | tf_op jit(solution)/shard_map/ppermute | solution.py:328
  8.7 2.4 %collective-permute-done.3.refs_4_ = bf16[528,256]{1,0:T(8,128)(2,1)S(1)} collective-permute-done((bf16[528,256]{1,0:T(8,128)(2,1)S(1)}, bf16[528,256]{1,0:T(8,128)(2,1)S(1)}, u32[]{:S(2)}, u32[]{:S(2)}) %collective-permute-start.3) | collective-permute-done | bytes 270368 | tf_op jit(solution)/shard_map/ppermute | solution.py:328
  11.0 3.7 %collective-permute-start.4 = (bf16[528,256]{1,0:T(8,128)(2,1)S(1)}, bf16[528,256]{1,0:T(8,128)(2,1)S(1)}, u32[]{:S(2)}, u32[]{:S(2)}) collective-permute-start(bf16[528,256]{1,0:T(8,128)(2,1)S(1)} %collective-permute-done.3.refs_4_), channel_id=1, source_target_pairs={{0,6},{1,7},{2,0},{3,1},{4,2},{5,3},{6,4},{7,5},{8,14},{9,15},{10,... | collective-permute-start | bytes 811016 | tf_op jit(solution)/shard_map/ppermute | solution.py:331
  14.7 1.9 %collective-permute-start.15 = (bf16[528,256]{1,0:T(8,128)(2,1)S(1)}, bf16[528,256]{1,0:T(8,128)(2,1)S(1)}, u32[]{:S(2)}, u32[]{:S(2)}) collective-permute-start(bf16[528,256]{1,0:T(8,128)(2,1)S(1)} %collective-permute-done.5.refs_6_), channel_id=1, source_target_pairs={{0,8},{1,9},{2,10},{3,11},{4,12},{5,13},{6,14},{7,15},{8,16},{9,17... | collective-permute-start | bytes 811016 | tf_op jit(solution)/shard_map/ppermute | solution.py:331
  16.7 1.6 %meta.1.own = f32[72,128]{1,0:T(8,128)} custom-call(s32[32]{0:T(128)} %owner.1, s32[1,64]{1,0:T(1,128)} %bitcast.23, s32[4,16]{1,0:T(4,128)} %bitcast.20, f32[3,16]{1,0:T(4,128)} %bitcast.21, bf16[64,128]{1,0:T(8,128)(2,1)} %delta.1), custom_call_target="tpu_custom_call" | custom-call | tf_op jit(solution)/shard_map/meta/pallas_call | solution.py:334
  18.2 2.0 %collective-permute-start.13 = (bf16[528,256]{1,0:T(8,128)(2,1)S(1)}, bf16[528,256]{1,0:T(8,128)(2,1)S(1)}, u32[]{:S(2)}, u32[]{:S(2)}) collective-permute-start(bf16[528,256]{1,0:T(8,128)(2,1)S(1)} %fusion.1.refs_3_), channel_id=1, source_target_pairs={{0,8},{1,9},{2,10},{3,11},{4,12},{5,13},{6,14},{7,15},{8,16},{9,17... | collective-permute-start | bytes 811016 | tf_op jit(solution)/shard_map/ppermute | solution.py:328
  20.3 4.0 %collective-permute-start.7 = (bf16[528,256]{1,0:T(8,128)(2,1)S(1)}, bf16[528,256]{1,0:T(8,128)(2,1)S(1)}, u32[]{:S(2)}, u32[]{:S(2)}) collective-permute-start(bf16[528,256]{1,0:T(8,128)(2,1)S(1)} %collective-permute-done.4.refs_5_), channel_id=1, source_target_pairs={{0,24},{1,25},{2,26},{3,27},{4,28},{5,29},{6,30},{7,31},{8,0},{9,1... | collective-permute-start | bytes 811016 | tf_op jit(solution)/shard_map/ppermute | solution.py:331
  24.4 3.2 %collective-permute-start.9 = (bf16[528,256]{1,0:T(8,128)(2,1)S(1)}, bf16[528,256]{1,0:T(8,128)(2,1)S(1)}, u32[]{:S(2)}, u32[]{:S(2)}) collective-permute-start(bf16[528,256]{1,0:T(8,128)(2,1)S(1)} %collective-permute-done.2.refs_7_), channel_id=1, source_target_pairs={{0,24},{1,25},{2,26},{3,27},{4,28},{5,29},{6,30},{7,31},{8,0},{9,1... | collective-permute-start | bytes 811016 | tf_op jit(solution)/shard_map/ppermute | solution.py:331
  27.6 3.7 %collective-permute-done.7.refs_9_ = bf16[528,256]{1,0:T(8,128)(2,1)S(1)} collective-permute-done((bf16[528,256]{1,0:T(8,128)(2,1)S(1)}, bf16[528,256]{1,0:T(8,128)(2,1)S(1)}, u32[]{:S(2)}, u32[]{:S(2)}) %collective-permute-start.7) | collective-permute-done | bytes 270368 | tf_op jit(solution)/shard_map/ppermute | solution.py:331
  31.3 3.7 %collective-permute-start.11 = (bf16[528,256]{1,0:T(8,128)(2,1)S(1)}, bf16[528,256]{1,0:T(8,128)(2,1)S(1)}, u32[]{:S(2)}, u32[]{:S(2)}) collective-permute-start(bf16[528,256]{1,0:T(8,128)(2,1)S(1)} %collective-permute-done.7.refs_9_), channel_id=1, source_target_pairs={{0,24},{1,25},{2,26},{3,27},{4,28},{5,29},{6,30},{7,31},{8,0},{9,1... | collective-permute-start | bytes 811016 | tf_op jit(solution)/shard_map/ppermute | solution.py:331
  36.4 2.4 %collective-permute-start.6 = (bf16[528,256]{1,0:T(8,128)(2,1)S(1)}, bf16[528,256]{1,0:T(8,128)(2,1)S(1)}, u32[]{:S(2)}, u32[]{:S(2)}) collective-permute-start(bf16[528,256]{1,0:T(8,128)(2,1)S(1)} %collective-permute-done.2.refs_7_), channel_id=1, source_target_pairs={{0,6},{1,7},{2,0},{3,1},{4,2},{5,3},{6,4},{7,5},{8,14},{9,15},{10,... | collective-permute-start | bytes 811016 | tf_op jit(solution)/shard_map/ppermute | solution.py:331
  38.8 3.2 %collective-permute-start.10 = (bf16[528,256]{1,0:T(8,128)(2,1)S(1)}, bf16[528,256]{1,0:T(8,128)(2,1)S(1)}, u32[]{:S(2)}, u32[]{:S(2)}) collective-permute-start(bf16[528,256]{1,0:T(8,128)(2,1)S(1)} %collective-permute-done.9.refs_11_), channel_id=1, source_target_pairs={{0,6},{1,7},{2,0},{3,1},{4,2},{5,3},{6,4},{7,5},{8,14},{9,15},{10,... | collective-permute-start | bytes 811016 | tf_op jit(solution)/shard_map/ppermute | solution.py:331
  42.8 3.5 %plan.1 = (s32[8,128]{1,0:T(8,128)S(1)}, f32[144,128]{1,0:T(8,128)S(1)}, bf16[128,128,256]{2,1,0:T(8,128)(2,1)S(1)}) custom-call(f32[72,128]{1,0:T(8,128)S(1)} %copy-done, f32[72,128]{1,0:T(8,128)S(1)} %collective-permute-done.sib, bf16[64,128,256]{2,1,0:T(8,128)(2,1)} %x_own.1, bf16[64,128,256]{2,1,0:T(8,128)(2,1)} %collective-permute-done.1.x_sib), custom_call_target="tpu_custom_call" | custom-call | tf_op jit(solution)/shard_map/plan/pallas_call | solution.py:342
  47.8 1.7 %collective-permute-done.10.refs_12_ = bf16[528,256]{1,0:T(8,128)(2,1)S(1)} collective-permute-done((bf16[528,256]{1,0:T(8,128)(2,1)S(1)}, bf16[528,256]{1,0:T(8,128)(2,1)S(1)}, u32[]{:S(2)}, u32[]{:S(2)}) %collective-permute-start.10) | collective-permute-done | bytes 270368 | tf_op jit(solution)/shard_map/ppermute | solution.py:331
  49.4 6.3 %forward.1 = (f32[8,128]{1,0:T(8,128)S(1)}, f32[6,64,256]{2,1,0:T(8,128)S(1)}, bf16[16,528,256]{2,1,0:T(8,128)(2,1)S(1)}, bf16[64,256,256]{2,1,0:T(8,128)(2,1)S(1)}, bf16[64,256,256]{2,1,0:T(8,128)(2,1)S(1)}) custom-call(s32[8,128]{1,0:T(8,128)S(1)} %get-tuple-element.32.refs_0_, f32[144,128]{1,0:T(8,128)S(1)} %get-tuple-element.33.refs_1_, ...), custom_call_target="tpu_custom_call" | custom-call | tf_op jit(solution)/shard_map/forward/pallas_call | solution.py:353
  57.0 10.9 %backward.1 = (f32[8,128]{1,0:T(8,128)S(1)}, bf16[528,256]{1,0:T(8,128)(2,1)S(1)}, bf16[528,256]{1,0:T(8,128)(2,1)S(1)}, bf16[528,256]{1,0:T(8,128)(2,1)S(1)}, b...) custom-call(s32[8,128]{1,0:T(8,128)S(1)} %get-tuple-element.32.refs_, ...), custom_call_target="tpu_custom_call" | custom-call | tf_op jit(solution)/shard_map/backward/pallas_call | solution.py:369
  68.0 1.6 %collective-permute-start.20 = (bf16[528,256]{1,0:T(8,128)(2,1)S(1)}, bf16[528,256]{1,0:T(8,128)(2,1)S(1)}, u32[]{:S(2)}, u32[]{:S(2)}) collective-permute-start(bf16[528,256]{1,0:T(8,128)(2,1)S(1)} %get-tuple-element.47), channel_id=1, source_target_pairs={{0,6},{1,7},{2,0},{3,1},{4,2},{5,3},{6,4},{7,5},{8,14},{9,15},{10,... | collective-permute-start | bytes 811016 | tf_op jit(solution)/shard_map/ppermute | solution.py:386
  70.1 3.2 %collective-permute-start.18 = (bf16[528,256]{1,0:T(8,128)(2,1)S(1)}, bf16[528,256]{1,0:T(8,128)(2,1)S(1)}, u32[]{:S(2)}, u32[]{:S(2)}) collective-permute-start(bf16[528,256]{1,0:T(8,128)(2,1)S(1)} %get-tuple-element.43), channel_id=1, source_target_pairs={{0,24},{1,25},{2,26},{3,27},{4,28},{5,29},{6,30},{7,31},{8,0},{9,1... | collective-permute-start | bytes 811016 | tf_op jit(solution)/shard_map/ppermute | solution.py:386
  73.3 3.8 %collective-permute-done.29 = bf16[528,256]{1,0:T(8,128)(2,1)S(1)} collective-permute-done((bf16[528,256]{1,0:T(8,128)(2,1)S(1)}, bf16[528,256]{1,0:T(8,128)(2,1)S(1)}, u32[]{:S(2)}, u32[]{:S(2)}) %collective-permute-start.29) | collective-permute-done | bytes 270368 | tf_op jit(solution)/shard_map/ppermute | solution.py:386
  77.1 2.7 %collective-permute-start.25 = (bf16[528,256]{1,0:T(8,128)(2,1)S(1)}, bf16[528,256]{1,0:T(8,128)(2,1)S(1)}, u32[]{:S(2)}, u32[]{:S(2)}) collective-permute-start(bf16[528,256]{1,0:T(8,128)(2,1)S(1)} %get-tuple-element.52), channel_id=1, source_target_pairs={{0,6},{1,7},{2,0},{3,1},{4,2},{5,3},{6,4},{7,5},{8,14},{9,15},{10,... | collective-permute-start | bytes 811016 | tf_op jit(solution)/shard_map/ppermute | solution.py:386
  81.7 4.9 %collective-permute-done.25 = bf16[528,256]{1,0:T(8,128)(2,1)S(1)} collective-permute-done((bf16[528,256]{1,0:T(8,128)(2,1)S(1)}, bf16[528,256]{1,0:T(8,128)(2,1)S(1)}, u32[]{:S(2)}, u32[]{:S(2)}) %collective-permute-start.25) | collective-permute-done | bytes 270368 | tf_op jit(solution)/shard_map/ppermute | solution.py:386
  86.7 3.2 %collective-permute-done.30 = bf16[528,256]{1,0:T(8,128)(2,1)S(1)} collective-permute-done((bf16[528,256]{1,0:T(8,128)(2,1)S(1)}, bf16[528,256]{1,0:T(8,128)(2,1)S(1)}, u32[]{:S(2)}, u32[]{:S(2)}) %collective-permute-start.30) | collective-permute-done | bytes 270368 | tf_op jit(solution)/shard_map/ppermute | solution.py:386
  89.9 2.8 %collective-permute-start.26 = (bf16[528,256]{1,0:T(8,128)(2,1)S(1)}, bf16[528,256]{1,0:T(8,128)(2,1)S(1)}, u32[]{:S(2)}, u32[]{:S(2)}) collective-permute-start(bf16[528,256]{1,0:T(8,128)(2,1)S(1)} %add_convert_fusion.7), channel_id=1, source_target_pairs={{0,24},{1,25},{2,26},{3,27},{4,28},{5,29},{6,30},{7,31},{8,0},{9,1... | collective-permute-start | bytes 811016 | tf_op jit(solution)/shard_map/ppermute | solution.py:386
  92.9 3.8 %collective-permute-done.22 = bf16[528,256]{1,0:T(8,128)(2,1)S(1)} collective-permute-done((bf16[528,256]{1,0:T(8,128)(2,1)S(1)}, bf16[528,256]{1,0:T(8,128)(2,1)S(1)}, u32[]{:S(2)}, u32[]{:S(2)}) %collective-permute-start.22) | collective-permute-done | bytes 270368 | tf_op jit(solution)/shard_map/ppermute | solution.py:386
  97.0 2.3 %collective-permute-done.26 = bf16[528,256]{1,0:T(8,128)(2,1)S(1)} collective-permute-done((bf16[528,256]{1,0:T(8,128)(2,1)S(1)}, bf16[528,256]{1,0:T(8,128)(2,1)S(1)}, u32[]{:S(2)}, u32[]{:S(2)}) %collective-permute-start.26) | collective-permute-done | bytes 270368 | tf_op jit(solution)/shard_map/ppermute | solution.py:386
  100.8 2.6 %collective-permute-done.28 = bf16[528,256]{1,0:T(8,128)(2,1)S(1)} collective-permute-done((bf16[528,256]{1,0:T(8,128)(2,1)S(1)}, bf16[528,256]{1,0:T(8,128)(2,1)S(1)}, u32[]{:S(2)}, u32[]{:S(2)}) %collective-permute-start.28) | collective-permute-done | bytes 270368 | tf_op jit(solution)/shard_map/ppermute | solution.py:386
  104.3 2.0 %collective-permute-done.24 = bf16[528,256]{1,0:T(8,128)(2,1)S(1)} collective-permute-done((bf16[528,256]{1,0:T(8,128)(2,1)S(1)}, bf16[528,256]{1,0:T(8,128)(2,1)S(1)}, u32[]{:S(2)}, u32[]{:S(2)}) %collective-permute-start.24) | collective-permute-done | bytes 270368 | tf_op jit(solution)/shard_map/ppermute | solution.py:386
  106.3 5.2 %collective-permute-done.32 = bf16[528,256]{1,0:T(8,128)(2,1)S(1)} collective-permute-done((bf16[528,256]{1,0:T(8,128)(2,1)S(1)}, bf16[528,256]{1,0:T(8,128)(2,1)S(1)}, u32[]{:S(2)}, u32[]{:S(2)}) %collective-permute-start.32) | collective-permute-done | bytes 270368 | tf_op jit(solution)/shard_map/ppermute | solution.py:386
  111.8 3.2 %collective-permute-start.35 = (bf16[528,256]{1,0:T(8,128)(2,1)S(1)}, bf16[528,256]{1,0:T(8,128)(2,1)S(1)}, u32[]{:S(2)}, u32[]{:S(2)}) collective-permute-start(bf16[528,256]{1,0:T(8,128)(2,1)S(1)} %add_convert_fusion), channel_id=1, source_target_pairs={{0,64},{32,96},{64,0},{96,32},{1,65},{33,97},{65,1},{97,33},{2,66}... | collective-permute-start | bytes 811016 | tf_op jit(solution)/shard_map/ppermute | solution.py:391
  117.7 4.5 %collective-permute-done.35 = bf16[528,256]{1,0:T(8,128)(2,1)S(1)} collective-permute-done((bf16[528,256]{1,0:T(8,128)(2,1)S(1)}, bf16[528,256]{1,0:T(8,128)(2,1)S(1)}, u32[]{:S(2)}, u32[]{:S(2)}) %collective-permute-start.35) | collective-permute-done | bytes 270368 | tf_op jit(solution)/shard_map/ppermute | solution.py:391
  122.2 3.2 %collective-permute-done.34 = bf16[528,256]{1,0:T(8,128)(2,1)S(1)} collective-permute-done((bf16[528,256]{1,0:T(8,128)(2,1)S(1)}, bf16[528,256]{1,0:T(8,128)(2,1)S(1)}, u32[]{:S(2)}, u32[]{:S(2)}) %collective-permute-start.34) | collective-permute-done | bytes 270368 | tf_op jit(solution)/shard_map/ppermute | solution.py:391
  (59 shorter events, 16.1 us)
Async XLA Ops:
  0.6 23.8 %collective-permute-start.1 = (bf16[64,128,256]{2,1,0:T(8,128)(2,1)}, bf16[64,128,256]{2,1,0:T(8,128)(2,1)}, u32[]{:S(2)}, u32[]{:S(2)}) collective-permute-start(bf16[64,128,256]{2,1,0:T(8,128)(2,1)} %x_own.1), channel_id=1, source_target_pairs={{0,1},{1,0},{2,3},{3,2},{4,5},{5,4},{6,7},{7,6},{8,9},{9,8},{10,11... | collective-permute-start | bytes 12582920 | tf_op jit(solution)/shard_map/ppermute | solution.py:322
  1.7 9.3 %collective-permute-start.3 = (bf16[528,256]{1,0:T(8,128)(2,1)S(1)}, bf16[528,256]{1,0:T(8,128)(2,1)S(1)}, u32[]{:S(2)}, u32[]{:S(2)}) collective-permute-start(bf16[528,256]{1,0:T(8,128)(2,1)S(1)} %fusion.1.refs_3_), channel_id=1, source_target_pairs={{0,6},{1,7},{2,0},{3,1},{4,2},{5,3},{6,4},{7,5},{8,14},{9,15},{10,... | collective-permute-start | bytes 811016 | tf_op jit(solution)/shard_map/ppermute | solution.py:328
  4.6 10.1 %collective-permute-start.5 = (bf16[528,256]{1,0:T(8,128)(2,1)S(1)}, bf16[528,256]{1,0:T(8,128)(2,1)S(1)}, u32[]{:S(2)}, u32[]{:S(2)}) collective-permute-start(bf16[528,256]{1,0:T(8,128)(2,1)S(1)} %fusion.1.refs_3_), channel_id=1, source_target_pairs={{0,2},{1,3},{2,4},{3,5},{4,6},{5,7},{6,0},{7,1},{8,10},{9,11},{10,... | collective-permute-start | bytes 811016 | tf_op jit(solution)/shard_map/ppermute | solution.py:328
  4.6 13.6 %collective-permute-start.2 = (bf16[528,256]{1,0:T(8,128)(2,1)S(1)}, bf16[528,256]{1,0:T(8,128)(2,1)S(1)}, u32[]{:S(2)}, u32[]{:S(2)}) collective-permute-start(bf16[528,256]{1,0:T(8,128)(2,1)S(1)} %fusion.1.refs_3_), channel_id=1, source_target_pairs={{0,24},{1,25},{2,26},{3,27},{4,28},{5,29},{6,30},{7,31},{8,0},{9,1... | collective-permute-start | bytes 811016 | tf_op jit(solution)/shard_map/ppermute | solution.py:328
  11.0 9.3 %collective-permute-start.4 = (bf16[528,256]{1,0:T(8,128)(2,1)S(1)}, bf16[528,256]{1,0:T(8,128)(2,1)S(1)}, u32[]{:S(2)}, u32[]{:S(2)}) collective-permute-start(bf16[528,256]{1,0:T(8,128)(2,1)S(1)} %collective-permute-done.3.refs_4_), channel_id=1, source_target_pairs={{0,6},{1,7},{2,0},{3,1},{4,2},{5,3},{6,4},{7,5},{8,14},{9,15},{10,... | collective-permute-start | bytes 811016 | tf_op jit(solution)/shard_map/ppermute | solution.py:331
  14.7 12.9 %collective-permute-start.15 = (bf16[528,256]{1,0:T(8,128)(2,1)S(1)}, bf16[528,256]{1,0:T(8,128)(2,1)S(1)}, u32[]{:S(2)}, u32[]{:S(2)}) collective-permute-start(bf16[528,256]{1,0:T(8,128)(2,1)S(1)} %collective-permute-done.5.refs_6_), channel_id=1, source_target_pairs={{0,8},{1,9},{2,10},{3,11},{4,12},{5,13},{6,14},{7,15},{8,16},{9,17... | collective-permute-start | bytes 811016 | tf_op jit(solution)/shard_map/ppermute | solution.py:331
  18.2 16.8 %collective-permute-start.13 = (bf16[528,256]{1,0:T(8,128)(2,1)S(1)}, bf16[528,256]{1,0:T(8,128)(2,1)S(1)}, u32[]{:S(2)}, u32[]{:S(2)}) collective-permute-start(bf16[528,256]{1,0:T(8,128)(2,1)S(1)} %fusion.1.refs_3_), channel_id=1, source_target_pairs={{0,8},{1,9},{2,10},{3,11},{4,12},{5,13},{6,14},{7,15},{8,16},{9,17... | collective-permute-start | bytes 811016 | tf_op jit(solution)/shard_map/ppermute | solution.py:328
  20.3 11.0 %collective-permute-start.7 = (bf16[528,256]{1,0:T(8,128)(2,1)S(1)}, bf16[528,256]{1,0:T(8,128)(2,1)S(1)}, u32[]{:S(2)}, u32[]{:S(2)}) collective-permute-start(bf16[528,256]{1,0:T(8,128)(2,1)S(1)} %collective-permute-done.4.refs_5_), channel_id=1, source_target_pairs={{0,24},{1,25},{2,26},{3,27},{4,28},{5,29},{6,30},{7,31},{8,0},{9,1... | collective-permute-start | bytes 811016 | tf_op jit(solution)/shard_map/ppermute | solution.py:331
  24.4 12.0 %collective-permute-start.14 = (bf16[528,256]{1,0:T(8,128)(2,1)S(1)}, bf16[528,256]{1,0:T(8,128)(2,1)S(1)}, u32[]{:S(2)}, u32[]{:S(2)}) collective-permute-start(bf16[528,256]{1,0:T(8,128)(2,1)S(1)} %collective-permute-done.3.refs_4_), channel_id=1, source_target_pairs={{0,8},{1,9},{2,10},{3,11},{4,12},{5,13},{6,14},{7,15},{8,16},{9,17... | collective-permute-start | bytes 811016 | tf_op jit(solution)/shard_map/ppermute | solution.py:331
  24.4 14.4 %collective-permute-start.9 = (bf16[528,256]{1,0:T(8,128)(2,1)S(1)}, bf16[528,256]{1,0:T(8,128)(2,1)S(1)}, u32[]{:S(2)}, u32[]{:S(2)}) collective-permute-start(bf16[528,256]{1,0:T(8,128)(2,1)S(1)} %collective-permute-done.2.refs_7_), channel_id=1, source_target_pairs={{0,24},{1,25},{2,26},{3,27},{4,28},{5,29},{6,30},{7,31},{8,0},{9,1... | collective-permute-start | bytes 811016 | tf_op jit(solution)/shard_map/ppermute | solution.py:331
  27.6 11.2 %collective-permute-start.16 = (bf16[528,256]{1,0:T(8,128)(2,1)S(1)}, bf16[528,256]{1,0:T(8,128)(2,1)S(1)}, u32[]{:S(2)}, u32[]{:S(2)}) collective-permute-start(bf16[528,256]{1,0:T(8,128)(2,1)S(1)} %collective-permute-done.15.refs_18_), channel_id=1, source_target_pairs={{0,2},{1,3},{2,4},{3,5},{4,6},{5,7},{6,0},{7,1},{8,10},{9,11},{10,... | collective-permute-start | bytes 811016 | tf_op jit(solution)/shard_map/ppermute | solution.py:331
  31.3 15.0 %collective-permute-start.11 = (bf16[528,256]{1,0:T(8,128)(2,1)S(1)}, bf16[528,256]{1,0:T(8,128)(2,1)S(1)}, u32[]{:S(2)}, u32[]{:S(2)}) collective-permute-start(bf16[528,256]{1,0:T(8,128)(2,1)S(1)} %collective-permute-done.7.refs_9_), channel_id=1, source_target_pairs={{0,24},{1,25},{2,26},{3,27},{4,28},{5,29},{6,30},{7,31},{8,0},{9,1... | collective-permute-start | bytes 811016 | tf_op jit(solution)/shard_map/ppermute | solution.py:331
  35.0 11.3 %collective-permute-start.8 = (bf16[528,256]{1,0:T(8,128)(2,1)S(1)}, bf16[528,256]{1,0:T(8,128)(2,1)S(1)}, u32[]{:S(2)}, u32[]{:S(2)}) collective-permute-start(bf16[528,256]{1,0:T(8,128)(2,1)S(1)} %collective-permute-done.2.refs_7_), channel_id=1, source_target_pairs={{0,2},{1,3},{2,4},{3,5},{4,6},{5,7},{6,0},{7,1},{8,10},{9,11},{10,... | collective-permute-start | bytes 811016 | tf_op jit(solution)/shard_map/ppermute | solution.py:331
  36.4 9.9 %collective-permute-start.6 = (bf16[528,256]{1,0:T(8,128)(2,1)S(1)}, bf16[528,256]{1,0:T(8,128)(2,1)S(1)}, u32[]{:S(2)}, u32[]{:S(2)}) collective-permute-start(bf16[528,256]{1,0:T(8,128)(2,1)S(1)} %collective-permute-done.2.refs_7_), channel_id=1, source_target_pairs={{0,6},{1,7},{2,0},{3,1},{4,2},{5,3},{6,4},{7,5},{8,14},{9,15},{10,... | collective-permute-start | bytes 811016 | tf_op jit(solution)/shard_map/ppermute | solution.py:331
  38.8 9.0 %collective-permute-start.12 = (bf16[528,256]{1,0:T(8,128)(2,1)S(1)}, bf16[528,256]{1,0:T(8,128)(2,1)S(1)}, u32[]{:S(2)}, u32[]{:S(2)}) collective-permute-start(bf16[528,256]{1,0:T(8,128)(2,1)S(1)} %collective-permute-done.9.refs_11_), channel_id=1, source_target_pairs={{0,2},{1,3},{2,4},{3,5},{4,6},{5,7},{6,0},{7,1},{8,10},{9,11},{10,... | collective-permute-start | bytes 811016 | tf_op jit(solution)/shard_map/ppermute | solution.py:331
  38.8 10.6 %collective-permute-start.10 = (bf16[528,256]{1,0:T(8,128)(2,1)S(1)}, bf16[528,256]{1,0:T(8,128)(2,1)S(1)}, u32[]{:S(2)}, u32[]{:S(2)}) collective-permute-start(bf16[528,256]{1,0:T(8,128)(2,1)S(1)} %collective-permute-done.9.refs_11_), channel_id=1, source_target_pairs={{0,6},{1,7},{2,0},{3,1},{4,2},{5,3},{6,4},{7,5},{8,14},{9,15},{10,... | collective-permute-start | bytes 811016 | tf_op jit(solution)/shard_map/ppermute | solution.py:331
  67.9 9.2 %collective-permute-start.29 = (bf16[528,256]{1,0:T(8,128)(2,1)S(1)}, bf16[528,256]{1,0:T(8,128)(2,1)S(1)}, u32[]{:S(2)}, u32[]{:S(2)}) collective-permute-start(bf16[528,256]{1,0:T(8,128)(2,1)S(1)} %get-tuple-element.57), channel_id=1, source_target_pairs={{0,8},{1,9},{2,10},{3,11},{4,12},{5,13},{6,14},{7,15},{8,16},{9,17... | collective-permute-start | bytes 811016 | tf_op jit(solution)/shard_map/ppermute | solution.py:386
  68.0 11.8 %collective-permute-start.20 = (bf16[528,256]{1,0:T(8,128)(2,1)S(1)}, bf16[528,256]{1,0:T(8,128)(2,1)S(1)}, u32[]{:S(2)}, u32[]{:S(2)}) collective-permute-start(bf16[528,256]{1,0:T(8,128)(2,1)S(1)} %get-tuple-element.47), channel_id=1, source_target_pairs={{0,6},{1,7},{2,0},{3,1},{4,2},{5,3},{6,4},{7,5},{8,14},{9,15},{10,... | collective-permute-start | bytes 811016 | tf_op jit(solution)/shard_map/ppermute | solution.py:386
  69.6 10.6 %collective-permute-start.21 = (bf16[528,256]{1,0:T(8,128)(2,1)S(1)}, bf16[528,256]{1,0:T(8,128)(2,1)S(1)}, u32[]{:S(2)}, u32[]{:S(2)}) collective-permute-start(bf16[528,256]{1,0:T(8,128)(2,1)S(1)} %get-tuple-element.48), channel_id=1, source_target_pairs={{0,2},{1,3},{2,4},{3,5},{4,6},{5,7},{6,0},{7,1},{8,10},{9,11},{10,... | collective-permute-start | bytes 811016 | tf_op jit(solution)/shard_map/ppermute | solution.py:386
  70.1 34.2 %collective-permute-start.18 = (bf16[528,256]{1,0:T(8,128)(2,1)S(1)}, bf16[528,256]{1,0:T(8,128)(2,1)S(1)}, u32[]{:S(2)}, u32[]{:S(2)}) collective-permute-start(bf16[528,256]{1,0:T(8,128)(2,1)S(1)} %get-tuple-element.43), channel_id=1, source_target_pairs={{0,24},{1,25},{2,26},{3,27},{4,28},{5,29},{6,30},{7,31},{8,0},{9,1... | collective-permute-start | bytes 811016 | tf_op jit(solution)/shard_map/ppermute | solution.py:386
  73.3 19.5 %collective-permute-start.19 = (bf16[528,256]{1,0:T(8,128)(2,1)S(1)}, bf16[528,256]{1,0:T(8,128)(2,1)S(1)}, u32[]{:S(2)}, u32[]{:S(2)}) collective-permute-start(bf16[528,256]{1,0:T(8,128)(2,1)S(1)} %get-tuple-element.45), channel_id=1, source_target_pairs={{0,2},{1,3},{2,4},{3,5},{4,6},{5,7},{6,0},{7,1},{8,10},{9,11},{10,... | collective-permute-start | bytes 811016 | tf_op jit(solution)/shard_map/ppermute | solution.py:386
  77.1 9.5 %collective-permute-start.25 = (bf16[528,256]{1,0:T(8,128)(2,1)S(1)}, bf16[528,256]{1,0:T(8,128)(2,1)S(1)}, u32[]{:S(2)}, u32[]{:S(2)}) collective-permute-start(bf16[528,256]{1,0:T(8,128)(2,1)S(1)} %get-tuple-element.52), channel_id=1, source_target_pairs={{0,6},{1,7},{2,0},{3,1},{4,2},{5,3},{6,4},{7,5},{8,14},{9,15},{10,... | collective-permute-start | bytes 811016 | tf_op jit(solution)/shard_map/ppermute | solution.py:386
  79.9 13.0 %collective-permute-start.23 = (bf16[528,256]{1,0:T(8,128)(2,1)S(1)}, bf16[528,256]{1,0:T(8,128)(2,1)S(1)}, u32[]{:S(2)}, u32[]{:S(2)}) collective-permute-start(bf16[528,256]{1,0:T(8,128)(2,1)S(1)} %get-tuple-element.49), channel_id=1, source_target_pairs={{0,6},{1,7},{2,0},{3,1},{4,2},{5,3},{6,4},{7,5},{8,14},{9,15},{10,... | collective-permute-start | bytes 811016 | tf_op jit(solution)/shard_map/ppermute | solution.py:386
  80.1 9.7 %collective-permute-start.30 = (bf16[528,256]{1,0:T(8,128)(2,1)S(1)}, bf16[528,256]{1,0:T(8,128)(2,1)S(1)}, u32[]{:S(2)}, u32[]{:S(2)}) collective-permute-start(bf16[528,256]{1,0:T(8,128)(2,1)S(1)} %add_convert_fusion.3), channel_id=1, source_target_pairs={{0,8},{1,9},{2,10},{3,11},{4,12},{5,13},{6,14},{7,15},{8,16},{9,17... | collective-permute-start | bytes 811016 | tf_op jit(solution)/shard_map/ppermute | solution.py:386
  86.6 10.1 %collective-permute-start.22 = (bf16[528,256]{1,0:T(8,128)(2,1)S(1)}, bf16[528,256]{1,0:T(8,128)(2,1)S(1)}, u32[]{:S(2)}, u32[]{:S(2)}) collective-permute-start(bf16[528,256]{1,0:T(8,128)(2,1)S(1)} %add_convert_fusion.11), channel_id=1, source_target_pairs={{0,8},{1,9},{2,10},{3,11},{4,12},{5,13},{6,14},{7,15},{8,16},{9,17... | collective-permute-start | bytes 811016 | tf_op jit(solution)/shard_map/ppermute | solution.py:386
  89.9 9.4 %collective-permute-start.26 = (bf16[528,256]{1,0:T(8,128)(2,1)S(1)}, bf16[528,256]{1,0:T(8,128)(2,1)S(1)}, u32[]{:S(2)}, u32[]{:S(2)}) collective-permute-start(bf16[528,256]{1,0:T(8,128)(2,1)S(1)} %add_convert_fusion.7), channel_id=1, source_target_pairs={{0,24},{1,25},{2,26},{3,27},{4,28},{5,29},{6,30},{7,31},{8,0},{9,1... | collective-permute-start | bytes 811016 | tf_op jit(solution)/shard_map/ppermute | solution.py:386
  92.8 10.6 %collective-permute-start.28 = (bf16[528,256]{1,0:T(8,128)(2,1)S(1)}, bf16[528,256]{1,0:T(8,128)(2,1)S(1)}, u32[]{:S(2)}, u32[]{:S(2)}) collective-permute-start(bf16[528,256]{1,0:T(8,128)(2,1)S(1)} %get-tuple-element.54), channel_id=1, source_target_pairs={{0,24},{1,25},{2,26},{3,27},{4,28},{5,29},{6,30},{7,31},{8,0},{9,1... | collective-permute-start | bytes 811016 | tf_op jit(solution)/shard_map/ppermute | solution.py:386
  92.9 10.5 %collective-permute-start.31 = (bf16[528,256]{1,0:T(8,128)(2,1)S(1)}, bf16[528,256]{1,0:T(8,128)(2,1)S(1)}, u32[]{:S(2)}, u32[]{:S(2)}) collective-permute-start(bf16[528,256]{1,0:T(8,128)(2,1)S(1)} %add_convert_fusion.2), channel_id=1, source_target_pairs={{0,2},{1,3},{2,4},{3,5},{4,6},{5,7},{6,0},{7,1},{8,10},{9,11},{10,... | collective-permute-start | bytes 811016 | tf_op jit(solution)/shard_map/ppermute | solution.py:386
  96.9 9.4 %collective-permute-start.24 = (bf16[528,256]{1,0:T(8,128)(2,1)S(1)}, bf16[528,256]{1,0:T(8,128)(2,1)S(1)}, u32[]{:S(2)}, u32[]{:S(2)}) collective-permute-start(bf16[528,256]{1,0:T(8,128)(2,1)S(1)} %add_convert_fusion.9), channel_id=1, source_target_pairs={{0,8},{1,9},{2,10},{3,11},{4,12},{5,13},{6,14},{7,15},{8,16},{9,17... | collective-permute-start | bytes 811016 | tf_op jit(solution)/shard_map/ppermute | solution.py:386
  111.8 10.4 %collective-permute-start.35 = (bf16[528,256]{1,0:T(8,128)(2,1)S(1)}, bf16[528,256]{1,0:T(8,128)(2,1)S(1)}, u32[]{:S(2)}, u32[]{:S(2)}) collective-permute-start(bf16[528,256]{1,0:T(8,128)(2,1)S(1)} %add_convert_fusion), channel_id=1, source_target_pairs={{0,64},{32,96},{64,0},{96,32},{1,65},{33,97},{65,1},{97,33},{2,66}... | collective-permute-start | bytes 811016 | tf_op jit(solution)/shard_map/ppermute | solution.py:391
  115.0 10.4 %collective-permute-start.34 = (bf16[528,256]{1,0:T(8,128)(2,1)S(1)}, bf16[528,256]{1,0:T(8,128)(2,1)S(1)}, u32[]{:S(2)}, u32[]{:S(2)}) collective-permute-start(bf16[528,256]{1,0:T(8,128)(2,1)S(1)} %add_convert_fusion), channel_id=1, source_target_pairs={{0,96},{32,0},{64,32},{96,64},{1,97},{33,1},{65,33},{97,65},{2,98}... | collective-permute-start | bytes 811016 | tf_op jit(solution)/shard_map/ppermute | solution.py:391
  116.1 9.4 %collective-permute-start.33 = (bf16[528,256]{1,0:T(8,128)(2,1)S(1)}, bf16[528,256]{1,0:T(8,128)(2,1)S(1)}, u32[]{:S(2)}, u32[]{:S(2)}) collective-permute-start(bf16[528,256]{1,0:T(8,128)(2,1)S(1)} %add_convert_fusion), channel_id=1, source_target_pairs={{0,32},{32,64},{64,96},{96,0},{1,33},{33,65},{65,97},{97,1},{2,34}... | collective-permute-start | bytes 811016 | tf_op jit(solution)/shard_map/ppermute | solution.py:391
  (5 other events, 23.2 us)

commit v4 on v3

--- a/solution.py
+++ b/solution.py
@@ -15,22 +15,39 @@
 MIB = 1024 * 1024
 HI = lax.Precision.HIGHEST
 
-TREE = (
+OUT_TREE = (
     ((0, 1), (0, 0), "x", 1),
+    ((1, 0), (0, 0), "z", 1),
+    ((0, 3), (0, 0), "x", 3),
+    ((3, 0), (0, 0), "z", 3),
+    ((0, 2), (0, 1), "x", 1),
+    ((2, 0), (3, 0), "z", 3),
+    ((1, 1), (1, 0), "x", 1),
+    ((3, 1), (0, 1), "z", 3),
+    ((3, 3), (3, 0), "x", 3),
+    ((1, 3), (0, 3), "z", 1),
+    ((1, 2), (0, 2), "z", 1),
+    ((2, 1), (2, 0), "x", 1),
+    ((3, 2), (0, 2), "z", 3),
+    ((2, 3), (2, 0), "x", 3),
+    ((2, 2), (2, 0), "x", 2),
+)
+BACK_TREE = (
+    ((2, 2), (2, 0), "x", 2),
+    ((1, 3), (0, 3), "z", 1),
+    ((3, 3), (3, 0), "x", 3),
+    ((3, 1), (0, 1), "z", 3),
+    ((1, 1), (1, 0), "x", 1),
+    ((2, 3), (2, 0), "x", 3),
+    ((3, 2), (0, 2), "z", 3),
+    ((2, 1), (2, 0), "x", 1),
+    ((1, 2), (0, 2), "z", 1),
+    ((3, 0), (0, 0), "z", 3),
     ((0, 3), (0, 0), "x", 3),
     ((1, 0), (0, 0), "z", 1),
-    ((3, 0), (0, 0), "z", 3),
-    ((0, 2), (0, 1), "x", 1),
-    ((1, 3), (1, 0), "x", 3),
-    ((2, 0), (1, 0), "z", 1),
-    ((3, 3), (0, 3), "z", 3),
-    ((1, 1), (1, 0), "x", 1),
-    ((3, 1), (0, 1), "z", 3),
-    ((1, 2), (0, 2), "z", 1),
-    ((3, 2), (3, 3), "x", 3),
-    ((2, 1), (2, 0), "x", 1),
-    ((2, 3), (2, 0), "x", 3),
-    ((2, 2), (1, 2), "z", 1),
+    ((0, 1), (0, 0), "x", 1),
+    ((2, 0), (0, 0), "z", 2),
+    ((0, 2), (0, 0), "x", 2),
 )
 
 
@@ -324,10 +341,12 @@
     head = jnp.pad(weight_out[0].T, ((0, 12), (0, 0)))
     held = {(0, 0): jnp.concatenate([weight_one[0], weight_two[0], head], 0)}
     x_sib = swap(features)
-    for key, source, axis, step in TREE[:4]:
+    for key, source, axis, step in OUT_TREE[:4]:
         held[key] = lax.ppermute(held[source], "region", move(axis, -step))
-    x_sib, held[(1, 0)] = lax.optimization_barrier((x_sib, held[(1, 0)]))
-    for key, source, axis, step in TREE[4:]:
+    keys = list(held)
+    x_sib, *values = lax.optimization_barrier((x_sib, *held.values()))
+    held = dict(zip(keys, values))
+    for key, source, axis, step in OUT_TREE[4:]:
         held[key] = lax.ppermute(held[source], "region", move(axis, -step))
     weights = [held[(s // 4, s % 4)] for s in range(NS)]
 
@@ -382,7 +401,7 @@
     )(table, info, res, res_sib, xa, saved, wv, h1, h2)
 
     sums = {(s // 4, s % 4): grads[s] for s in range(NS)}
-    for key, source, axis, step in reversed(TREE):
+    for key, source, axis, step in BACK_TREE:
         got = lax.ppermute(sums[key], "region", move(axis, step))
         sums[source] = (sums[source].astype(F32) + got.astype(F32)).astype(BF16)
     mine = sums[(0, 0)]

time: 127 us -> 137 us (1.079)
  the two profiles are of different devices: /device:TPU:0 before, /device:TPU:38 now
where the time goes in v4:
time: 137 us; the launch traced here: 135 us
  waiting for transfers between devices  71.4 us (52%)
  starting transfers between devices  31.1 us (23%)
  Pallas kernels  22.7 us (17%)
  local copies, waits for them, and re-layouts  7.03 us (5%)
  other arithmetic  1.96 us (1%)
    ppermute x15, waiting for transfers between devices, local(): got = lax.ppermute(sums[key], 'region', move(axis, step))  36.7 us
    ppermute x15, waiting for transfers between devices, local(): held[key] = lax.ppermute(held[source], 'region', move(axis, -step))  27.3 us
    ppermute x15, starting transfers between devices, local(): held[key] = lax.ppermute(held[source], 'region', move(axis, -step))  14.3 us
    pallas_call x1, Pallas kernels, local(): pl.pallas_call(backward_kernel, out_shape=(shape((8, 128), F32),) + (pltp...  12 us
    ppermute x15, starting transfers between devices, local(): got = lax.ppermute(sums[key], 'region', move(axis, step))  11.3 us
    pallas_call x1, Pallas kernels, local(): pl.pallas_call(forward_kernel, out_shape=(shape((8, 128), F32), pltpu.VME...  6.9 us
    ppermute x3, waiting for transfers between devices, local(): got = lax.ppermute(mine, 'ray', [(i, (i + d) % 4) for i in range(4)])  6.03 us
    ppermute x3, starting transfers between devices, local(): got = lax.ppermute(mine, 'ray', [(i, (i + d) % 4) for i in range(4)])  5.3 us
  transfers between devices with their start and end apart: 36, of which 22 were waited for; matrix products, arithmetic and copies ran while one was open for 2% of the time, Pallas kernels for 3%

profile of v4, /device:TPU:38, one launch (start us, length us, event | category | flops | bytes accessed | tf_op | source)
XLA Modules:
  0.0 135.0 jit_solution(17853643171437984151)
XLA Ops:
  1.7 2.0 %collective-permute-start.5 = (bf16[528,256]{1,0:T(8,128)(2,1)S(1)}, bf16[528,256]{1,0:T(8,128)(2,1)S(1)}, u32[]{:S(2)}, u32[]{:S(2)}) collective-permute-start(bf16[528,256]{1,0:T(8,128)(2,1)S(1)} %fusion.1.refs_3_), channel_id=1, source_target_pairs={{0,8},{1,9},{2,10},{3,11},{4,12},{5,13},{6,14},{7,15},{8,16},{9,17... | collective-permute-start | bytes 811016 | tf_op jit(solution)/shard_map/ppermute | solution.py:345
  4.3 1.5 %collective-permute-start.2 = (bf16[528,256]{1,0:T(8,128)(2,1)S(1)}, bf16[528,256]{1,0:T(8,128)(2,1)S(1)}, u32[]{:S(2)}, u32[]{:S(2)}) collective-permute-start(bf16[528,256]{1,0:T(8,128)(2,1)S(1)} %fusion.1.refs_3_), channel_id=1, source_target_pairs={{0,6},{1,7},{2,0},{3,1},{4,2},{5,3},{6,4},{7,5},{8,14},{9,15},{10,... | collective-permute-start | bytes 811016 | tf_op jit(solution)/shard_map/ppermute | solution.py:345
  5.9 4.8 %collective-permute-done.5.refs_15_ = bf16[528,256]{1,0:T(8,128)(2,1)S(1)} collective-permute-done((bf16[528,256]{1,0:T(8,128)(2,1)S(1)}, bf16[528,256]{1,0:T(8,128)(2,1)S(1)}, u32[]{:S(2)}, u32[]{:S(2)}) %collective-permute-start.5) | collective-permute-done | bytes 270368 | tf_op jit(solution)/shard_map/ppermute | solution.py:345
  10.7 1.6 %collective-permute-done.4.refs_6_ = bf16[528,256]{1,0:T(8,128)(2,1)S(1)} collective-permute-done((bf16[528,256]{1,0:T(8,128)(2,1)S(1)}, bf16[528,256]{1,0:T(8,128)(2,1)S(1)}, u32[]{:S(2)}, u32[]{:S(2)}) %collective-permute-start.4) | collective-permute-done | bytes 270368 | tf_op jit(solution)/shard_map/ppermute | solution.py:345
  13.7 2.0 %copy-done = bf16[64,128,256]{2,1,0:T(8,128)(2,1)} copy-done((bf16[64,128,256]{2,1,0:T(8,128)(2,1)}, bf16[64,128,256]{2,1,0:T(8,128)(2,1)S(1)}, u32[]{:S(2)}) %copy-start) | copy-done | bytes 4194328
  15.7 2.3 %collective-permute-start.9 = (bf16[528,256]{1,0:T(8,128)(2,1)S(1)}, bf16[528,256]{1,0:T(8,128)(2,1)S(1)}, u32[]{:S(2)}, u32[]{:S(2)}) collective-permute-start(bf16[528,256]{1,0:T(8,128)(2,1)S(1)} %collective-permute-done.4.refs_6_), channel_id=1, source_target_pairs={{0,24},{1,25},{2,26},{3,27},{4,28},{5,29},{6,30},{7,31},{8,0},{9,1... | collective-permute-start | bytes 811016 | tf_op jit(solution)/shard_map/ppermute | solution.py:350
  18.0 1.6 %meta.1.own = f32[72,128]{1,0:T(8,128)} custom-call(s32[32]{0:T(128)} %owner.1, s32[1,64]{1,0:T(1,128)} %bitcast.23, s32[4,16]{1,0:T(4,128)} %bitcast.20, f32[3,16]{1,0:T(4,128)} %bitcast.21, bf16[64,128]{1,0:T(8,128)(2,1)} %delta.1), custom_call_target="tpu_custom_call" | custom-call | tf_op jit(solution)/shard_map/meta/pallas_call | solution.py:353
  23.1 1.6 %collective-permute-start.16 = (bf16[528,256]{1,0:T(8,128)(2,1)S(1)}, bf16[528,256]{1,0:T(8,128)(2,1)S(1)}, u32[]{:S(2)}, u32[]{:S(2)}) collective-permute-start(bf16[528,256]{1,0:T(8,128)(2,1)S(1)} %collective-permute-done.5.refs_15_), channel_id=1, source_target_pairs={{0,2},{1,3},{2,4},{3,5},{4,6},{5,7},{6,0},{7,1},{8,10},{9,11},{10,... | collective-permute-start | bytes 811016 | tf_op jit(solution)/shard_map/ppermute | solution.py:350
  24.6 5.4 %collective-permute-done.6.refs_5_ = bf16[528,256]{1,0:T(8,128)(2,1)S(1)} collective-permute-done((bf16[528,256]{1,0:T(8,128)(2,1)S(1)}, bf16[528,256]{1,0:T(8,128)(2,1)S(1)}, u32[]{:S(2)}, u32[]{:S(2)}) %collective-permute-start.6) | collective-permute-done | bytes 270368 | tf_op jit(solution)/shard_map/ppermute | solution.py:350
  30.1 5.4 %collective-permute-done.7.refs_8_ = bf16[528,256]{1,0:T(8,128)(2,1)S(1)} collective-permute-done((bf16[528,256]{1,0:T(8,128)(2,1)S(1)}, bf16[528,256]{1,0:T(8,128)(2,1)S(1)}, u32[]{:S(2)}, u32[]{:S(2)}) %collective-permute-start.7) | collective-permute-done | bytes 270368 | tf_op jit(solution)/shard_map/ppermute | solution.py:350
  35.5 1.7 %collective-permute-start.8 = (bf16[528,256]{1,0:T(8,128)(2,1)S(1)}, bf16[528,256]{1,0:T(8,128)(2,1)S(1)}, u32[]{:S(2)}, u32[]{:S(2)}) collective-permute-start(bf16[528,256]{1,0:T(8,128)(2,1)S(1)} %collective-permute-done.6.refs_5_), channel_id=1, source_target_pairs={{0,24},{1,25},{2,26},{3,27},{4,28},{5,29},{6,30},{7,31},{8,0},{9,1... | collective-permute-start | bytes 811016 | tf_op jit(solution)/shard_map/ppermute | solution.py:350
  37.2 2.3 %collective-permute-start.12 = (bf16[528,256]{1,0:T(8,128)(2,1)S(1)}, bf16[528,256]{1,0:T(8,128)(2,1)S(1)}, u32[]{:S(2)}, u32[]{:S(2)}) collective-permute-start(bf16[528,256]{1,0:T(8,128)(2,1)S(1)} %collective-permute-done.10.refs_11_), channel_id=1, source_target_pairs={{0,4},{1,5},{2,6},{3,7},{4,0},{5,1},{6,2},{7,3},{8,12},{9,13},{10,... | collective-permute-start | bytes 811016 | tf_op jit(solution)/shard_map/ppermute | solution.py:350
  39.5 2.2 %copy-done.1 = bf16[64,128,256]{2,1,0:T(8,128)(2,1)S(1)} copy-done((bf16[64,128,256]{2,1,0:T(8,128)(2,1)S(1)}, bf16[64,128,256]{2,1,0:T(8,128)(2,1)}, u32[]{:S(2)}) %copy-start.1) | copy-done | bytes 4194328
  42.4 2.2 %plan.1 = (s32[8,128]{1,0:T(8,128)S(1)}, f32[144,128]{1,0:T(8,128)S(1)}, bf16[128,128,256]{2,1,0:T(8,128)(2,1)S(1)}) custom-call(f32[72,128]{1,0:T(8,128)S(1)} %copy-done.2, f32[72,128]{1,0:T(8,128)S(1)} %collective-permute-done.sib, bf16[64,128,256]{2,1,0:T(8,128)(2,1)} %x_own.1, bf16[64,128,256]{2,1,0:T(8,128)(2,1)S(1)} %copy-done.1), custom_call_target="tpu_custom_call" | custom-call | tf_op jit(solution)/shard_map/plan/pallas_call | solution.py:361
  44.7 1.9 %collective-permute-done.13.refs_14_ = bf16[528,256]{1,0:T(8,128)(2,1)S(1)} collective-permute-done((bf16[528,256]{1,0:T(8,128)(2,1)S(1)}, bf16[528,256]{1,0:T(8,128)(2,1)S(1)}, u32[]{:S(2)}, u32[]{:S(2)}) %collective-permute-start.13) | collective-permute-done | bytes 270368 | tf_op jit(solution)/shard_map/ppermute | solution.py:350
  46.6 1.6 %collective-permute-done.12.refs_13_ = bf16[528,256]{1,0:T(8,128)(2,1)S(1)} collective-permute-done((bf16[528,256]{1,0:T(8,128)(2,1)S(1)}, bf16[528,256]{1,0:T(8,128)(2,1)S(1)}, u32[]{:S(2)}, u32[]{:S(2)}) %collective-permute-start.12) | collective-permute-done | bytes 270368 | tf_op jit(solution)/shard_map/ppermute | solution.py:350
  48.2 4.2 %collective-permute-done.11.refs_12_ = bf16[528,256]{1,0:T(8,128)(2,1)S(1)} collective-permute-done((bf16[528,256]{1,0:T(8,128)(2,1)S(1)}, bf16[528,256]{1,0:T(8,128)(2,1)S(1)}, u32[]{:S(2)}, u32[]{:S(2)}) %collective-permute-start.11) | collective-permute-done | bytes 270368 | tf_op jit(solution)/shard_map/ppermute | solution.py:350
  52.4 6.9 %forward.1 = (f32[8,128]{1,0:T(8,128)S(1)}, f32[6,64,256]{2,1,0:T(8,128)S(1)}, bf16[16,528,256]{2,1,0:T(8,128)(2,1)S(1)}, bf16[64,256,256]{2,1,0:T(8,128)(2,1)S(1)}, bf16[64,256,256]{2,1,0:T(8,128)(2,1)S(1)}) custom-call(s32[8,128]{1,0:T(8,128)S(1)} %get-tuple-element.36.refs_0_, f32[144,128]{1,0:T(8,128)S(1)} %get-tuple-element.37.refs_1_, ...), custom_call_target="tpu_custom_call" | custom-call | tf_op jit(solution)/shard_map/forward/pallas_call | solution.py:372
  60.5 12.0 %backward.1 = (f32[8,128]{1,0:T(8,128)S(1)}, bf16[528,256]{1,0:T(8,128)(2,1)S(1)}, bf16[528,256]{1,0:T(8,128)(2,1)S(1)}, bf16[528,256]{1,0:T(8,128)(2,1)S(1)}, b...) custom-call(s32[8,128]{1,0:T(8,128)S(1)} %get-tuple-element.36.refs_, ...), custom_call_target="tpu_custom_call" | custom-call | tf_op jit(solution)/shard_map/backward/pallas_call | solution.py:388
  74.6 2.1 %collective-permute-start.28 = (bf16[528,256]{1,0:T(8,128)(2,1)S(1)}, bf16[528,256]{1,0:T(8,128)(2,1)S(1)}, u32[]{:S(2)}, u32[]{:S(2)}) collective-permute-start(bf16[528,256]{1,0:T(8,128)(2,1)S(1)} %get-tuple-element.62), channel_id=1, source_target_pairs={{0,2},{1,3},{2,4},{3,5},{4,6},{5,7},{6,0},{7,1},{8,10},{9,11},{10,... | collective-permute-start | bytes 811016 | tf_op jit(solution)/shard_map/ppermute | solution.py:405
  77.3 6.3 %collective-permute-done.26 = bf16[528,256]{1,0:T(8,128)(2,1)S(1)} collective-permute-done((bf16[528,256]{1,0:T(8,128)(2,1)S(1)}, bf16[528,256]{1,0:T(8,128)(2,1)S(1)}, u32[]{:S(2)}, u32[]{:S(2)}) %collective-permute-start.26) | collective-permute-done | bytes 270368 | tf_op jit(solution)/shard_map/ppermute | solution.py:405
  84.7 2.8 %collective-permute-done.27 = bf16[528,256]{1,0:T(8,128)(2,1)S(1)} collective-permute-done((bf16[528,256]{1,0:T(8,128)(2,1)S(1)}, bf16[528,256]{1,0:T(8,128)(2,1)S(1)}, u32[]{:S(2)}, u32[]{:S(2)}) %collective-permute-start.27) | collective-permute-done | bytes 270368 | tf_op jit(solution)/shard_map/ppermute | solution.py:405
  88.3 4.8 %collective-permute-done.18 = bf16[528,256]{1,0:T(8,128)(2,1)S(1)} collective-permute-done((bf16[528,256]{1,0:T(8,128)(2,1)S(1)}, bf16[528,256]{1,0:T(8,128)(2,1)S(1)}, u32[]{:S(2)}, u32[]{:S(2)}) %collective-permute-start.18) | collective-permute-done | bytes 270368 | tf_op jit(solution)/shard_map/ppermute | solution.py:405
  93.6 1.7 %collective-permute-start.19 = (bf16[528,256]{1,0:T(8,128)(2,1)S(1)}, bf16[528,256]{1,0:T(8,128)(2,1)S(1)}, u32[]{:S(2)}, u32[]{:S(2)}) collective-permute-start(bf16[528,256]{1,0:T(8,128)(2,1)S(1)} %add_convert_fusion.14), channel_id=1, source_target_pairs={{0,24},{1,25},{2,26},{3,27},{4,28},{5,29},{6,30},{7,31},{8,0},{9,1... | collective-permute-start | bytes 811016 | tf_op jit(solution)/shard_map/ppermute | solution.py:405
  95.6 1.2 collective-permute-done.24
  97.3 5.4 %collective-permute-done.30 = bf16[528,256]{1,0:T(8,128)(2,1)S(1)} collective-permute-done((bf16[528,256]{1,0:T(8,128)(2,1)S(1)}, bf16[528,256]{1,0:T(8,128)(2,1)S(1)}, u32[]{:S(2)}, u32[]{:S(2)}) %collective-permute-start.30) | collective-permute-done | bytes 270368 | tf_op jit(solution)/shard_map/ppermute | solution.py:405
  102.6 1.4 %collective-permute-start.25 = (bf16[528,256]{1,0:T(8,128)(2,1)S(1)}, bf16[528,256]{1,0:T(8,128)(2,1)S(1)}, u32[]{:S(2)}, u32[]{:S(2)}) collective-permute-start(bf16[528,256]{1,0:T(8,128)(2,1)S(1)} %add_convert_fusion.8), channel_id=1, source_target_pairs={{0,2},{1,3},{2,4},{3,5},{4,6},{5,7},{6,0},{7,1},{8,10},{9,11},{10,... | collective-permute-start | bytes 811016 | tf_op jit(solution)/shard_map/ppermute | solution.py:405
  104.9 8.2 %collective-permute-done.19 = bf16[528,256]{1,0:T(8,128)(2,1)S(1)} collective-permute-done((bf16[528,256]{1,0:T(8,128)(2,1)S(1)}, bf16[528,256]{1,0:T(8,128)(2,1)S(1)}, u32[]{:S(2)}, u32[]{:S(2)}) %collective-permute-start.19) | collective-permute-done | bytes 270368 | tf_op jit(solution)/shard_map/ppermute | solution.py:405
  113.2 7.9 %collective-permute-done.32 = bf16[528,256]{1,0:T(8,128)(2,1)S(1)} collective-permute-done((bf16[528,256]{1,0:T(8,128)(2,1)S(1)}, bf16[528,256]{1,0:T(8,128)(2,1)S(1)}, u32[]{:S(2)}, u32[]{:S(2)}) %collective-permute-start.32) | collective-permute-done | bytes 270368 | tf_op jit(solution)/shard_map/ppermute | solution.py:405
  121.4 3.3 %collective-permute-start.35 = (bf16[528,256]{1,0:T(8,128)(2,1)S(1)}, bf16[528,256]{1,0:T(8,128)(2,1)S(1)}, u32[]{:S(2)}, u32[]{:S(2)}) collective-permute-start(bf16[528,256]{1,0:T(8,128)(2,1)S(1)} %add_convert_fusion), channel_id=1, source_target_pairs={{0,64},{32,96},{64,0},{96,32},{1,65},{33,97},{65,1},{97,33},{2,66}... | collective-permute-start | bytes 811016 | tf_op jit(solution)/shard_map/ppermute | solution.py:410
  127.4 2.1 %collective-permute-done.35 = bf16[528,256]{1,0:T(8,128)(2,1)S(1)} collective-permute-done((bf16[528,256]{1,0:T(8,128)(2,1)S(1)}, bf16[528,256]{1,0:T(8,128)(2,1)S(1)}, u32[]{:S(2)}, u32[]{:S(2)}) %collective-permute-start.35) | collective-permute-done | bytes 270368 | tf_op jit(solution)/shard_map/ppermute | solution.py:410
  129.4 3.3 %collective-permute-done.34 = bf16[528,256]{1,0:T(8,128)(2,1)S(1)} collective-permute-done((bf16[528,256]{1,0:T(8,128)(2,1)S(1)}, bf16[528,256]{1,0:T(8,128)(2,1)S(1)}, u32[]{:S(2)}, u32[]{:S(2)}) %collective-permute-start.34) | collective-permute-done | bytes 270368 | tf_op jit(solution)/shard_map/ppermute | solution.py:410
  (62 shorter events, 20.4 us)
Async XLA Ops:
  0.6 13.1 %collective-permute-start.1 = (bf16[64,128,256]{2,1,0:T(8,128)(2,1)}, bf16[64,128,256]{2,1,0:T(8,128)(2,1)S(1)}, u32[]{:S(2)}, u32[]{:S(2)}) collective-permute-start(bf16[64,128,256]{2,1,0:T(8,128)(2,1)} %x_own.1), channel_id=1, source_target_pairs={{0,1},{1,0},{2,3},{3,2},{4,5},{5,4},{6,7},{7,6},{8,9},{9,8},{10,11... | collective-permute-start | bytes 12582920 | tf_op jit(solution)/shard_map/ppermute | solution.py:339
  1.7 8.9 %collective-permute-start.5 = (bf16[528,256]{1,0:T(8,128)(2,1)S(1)}, bf16[528,256]{1,0:T(8,128)(2,1)S(1)}, u32[]{:S(2)}, u32[]{:S(2)}) collective-permute-start(bf16[528,256]{1,0:T(8,128)(2,1)S(1)} %fusion.1.refs_3_), channel_id=1, source_target_pairs={{0,8},{1,9},{2,10},{3,11},{4,12},{5,13},{6,14},{7,15},{8,16},{9,17... | collective-permute-start | bytes 811016 | tf_op jit(solution)/shard_map/ppermute | solution.py:345
  3.7 8.6 %collective-permute-start.4 = (bf16[528,256]{1,0:T(8,128)(2,1)S(1)}, bf16[528,256]{1,0:T(8,128)(2,1)S(1)}, u32[]{:S(2)}, u32[]{:S(2)}) collective-permute-start(bf16[528,256]{1,0:T(8,128)(2,1)S(1)} %fusion.1.refs_3_), channel_id=1, source_target_pairs={{0,2},{1,3},{2,4},{3,5},{4,6},{5,7},{6,0},{7,1},{8,10},{9,11},{10,... | collective-permute-start | bytes 811016 | tf_op jit(solution)/shard_map/ppermute | solution.py:345
  4.2 8.3 %collective-permute-start.3 = (bf16[528,256]{1,0:T(8,128)(2,1)S(1)}, bf16[528,256]{1,0:T(8,128)(2,1)S(1)}, u32[]{:S(2)}, u32[]{:S(2)}) collective-permute-start(bf16[528,256]{1,0:T(8,128)(2,1)S(1)} %fusion.1.refs_3_), channel_id=1, source_target_pairs={{0,24},{1,25},{2,26},{3,27},{4,28},{5,29},{6,30},{7,31},{8,0},{9,1... | collective-permute-start | bytes 811016 | tf_op jit(solution)/shard_map/ppermute | solution.py:345
  4.3 9.4 %collective-permute-start.2 = (bf16[528,256]{1,0:T(8,128)(2,1)S(1)}, bf16[528,256]{1,0:T(8,128)(2,1)S(1)}, u32[]{:S(2)}, u32[]{:S(2)}) collective-permute-start(bf16[528,256]{1,0:T(8,128)(2,1)S(1)} %fusion.1.refs_3_), channel_id=1, source_target_pairs={{0,6},{1,7},{2,0},{3,1},{4,2},{5,3},{6,4},{7,5},{8,14},{9,15},{10,... | collective-permute-start | bytes 811016 | tf_op jit(solution)/shard_map/ppermute | solution.py:345
  19.6 10.5 %collective-permute-start.6 = (bf16[528,256]{1,0:T(8,128)(2,1)S(1)}, bf16[528,256]{1,0:T(8,128)(2,1)S(1)}, u32[]{:S(2)}, u32[]{:S(2)}) collective-permute-start(bf16[528,256]{1,0:T(8,128)(2,1)S(1)} %collective-permute-done.2.refs_4_), channel_id=1, source_target_pairs={{0,6},{1,7},{2,0},{3,1},{4,2},{5,3},{6,4},{7,5},{8,14},{9,15},{10,... | collective-permute-start | bytes 811016 | tf_op jit(solution)/shard_map/ppermute | solution.py:350
  19.9 15.6 %collective-permute-start.7 = (bf16[528,256]{1,0:T(8,128)(2,1)S(1)}, bf16[528,256]{1,0:T(8,128)(2,1)S(1)}, u32[]{:S(2)}, u32[]{:S(2)}) collective-permute-start(bf16[528,256]{1,0:T(8,128)(2,1)S(1)} %collective-permute-done.3.refs_7_), channel_id=1, source_target_pairs={{0,6},{1,7},{2,0},{3,1},{4,2},{5,3},{6,4},{7,5},{8,14},{9,15},{10,... | collective-permute-start | bytes 811016 | tf_op jit(solution)/shard_map/ppermute | solution.py:350
  20.8 16.4 %collective-permute-start.10 = (bf16[528,256]{1,0:T(8,128)(2,1)S(1)}, bf16[528,256]{1,0:T(8,128)(2,1)S(1)}, u32[]{:S(2)}, u32[]{:S(2)}) collective-permute-start(bf16[528,256]{1,0:T(8,128)(2,1)S(1)} %collective-permute-done.5.refs_15_), channel_id=1, source_target_pairs={{0,8},{1,9},{2,10},{3,11},{4,12},{5,13},{6,14},{7,15},{8,16},{9,17... | collective-permute-start | bytes 811016 | tf_op jit(solution)/shard_map/ppermute | solution.py:350
  21.0 16.1 %collective-permute-start.14 = (bf16[528,256]{1,0:T(8,128)(2,1)S(1)}, bf16[528,256]{1,0:T(8,128)(2,1)S(1)}, u32[]{:S(2)}, u32[]{:S(2)}) collective-permute-start(bf16[528,256]{1,0:T(8,128)(2,1)S(1)} %collective-permute-done.2.refs_4_), channel_id=1, source_target_pairs={{0,8},{1,9},{2,10},{3,11},{4,12},{5,13},{6,14},{7,15},{8,16},{9,17... | collective-permute-start | bytes 811016 | tf_op jit(solution)/shard_map/ppermute | solution.py:350
  23.1 16.4 %collective-permute-start.16 = (bf16[528,256]{1,0:T(8,128)(2,1)S(1)}, bf16[528,256]{1,0:T(8,128)(2,1)S(1)}, u32[]{:S(2)}, u32[]{:S(2)}) collective-permute-start(bf16[528,256]{1,0:T(8,128)(2,1)S(1)} %collective-permute-done.5.refs_15_), channel_id=1, source_target_pairs={{0,2},{1,3},{2,4},{3,5},{4,6},{5,7},{6,0},{7,1},{8,10},{9,11},{10,... | collective-permute-start | bytes 811016 | tf_op jit(solution)/shard_map/ppermute | solution.py:350
  30.1 14.6 %collective-permute-start.15 = (bf16[528,256]{1,0:T(8,128)(2,1)S(1)}, bf16[528,256]{1,0:T(8,128)(2,1)S(1)}, u32[]{:S(2)}, u32[]{:S(2)}) collective-permute-start(bf16[528,256]{1,0:T(8,128)(2,1)S(1)} %collective-permute-done.6.refs_5_), channel_id=1, source_target_pairs={{0,8},{1,9},{2,10},{3,11},{4,12},{5,13},{6,14},{7,15},{8,16},{9,17... | collective-permute-start | bytes 811016 | tf_op jit(solution)/shard_map/ppermute | solution.py:350
  35.5 9.2 %collective-permute-start.8 = (bf16[528,256]{1,0:T(8,128)(2,1)S(1)}, bf16[528,256]{1,0:T(8,128)(2,1)S(1)}, u32[]{:S(2)}, u32[]{:S(2)}) collective-permute-start(bf16[528,256]{1,0:T(8,128)(2,1)S(1)} %collective-permute-done.6.refs_5_), channel_id=1, source_target_pairs={{0,24},{1,25},{2,26},{3,27},{4,28},{5,29},{6,30},{7,31},{8,0},{9,1... | collective-permute-start | bytes 811016 | tf_op jit(solution)/shard_map/ppermute | solution.py:350
  37.2 9.4 %collective-permute-start.13 = (bf16[528,256]{1,0:T(8,128)(2,1)S(1)}, bf16[528,256]{1,0:T(8,128)(2,1)S(1)}, u32[]{:S(2)}, u32[]{:S(2)}) collective-permute-start(bf16[528,256]{1,0:T(8,128)(2,1)S(1)} %collective-permute-done.10.refs_11_), channel_id=1, source_target_pairs={{0,2},{1,3},{2,4},{3,5},{4,6},{5,7},{6,0},{7,1},{8,10},{9,11},{10,... | collective-permute-start | bytes 811016 | tf_op jit(solution)/shard_map/ppermute | solution.py:350
  37.2 11.0 %collective-permute-start.12 = (bf16[528,256]{1,0:T(8,128)(2,1)S(1)}, bf16[528,256]{1,0:T(8,128)(2,1)S(1)}, u32[]{:S(2)}, u32[]{:S(2)}) collective-permute-start(bf16[528,256]{1,0:T(8,128)(2,1)S(1)} %collective-permute-done.10.refs_11_), channel_id=1, source_target_pairs={{0,4},{1,5},{2,6},{3,7},{4,0},{5,1},{6,2},{7,3},{8,12},{9,13},{10,... | collective-permute-start | bytes 811016 | tf_op jit(solution)/shard_map/ppermute | solution.py:350
  39.5 12.9 %collective-permute-start.11 = (bf16[528,256]{1,0:T(8,128)(2,1)S(1)}, bf16[528,256]{1,0:T(8,128)(2,1)S(1)}, u32[]{:S(2)}, u32[]{:S(2)}) collective-permute-start(bf16[528,256]{1,0:T(8,128)(2,1)S(1)} %collective-permute-done.10.refs_11_), channel_id=1, source_target_pairs={{0,6},{1,7},{2,0},{3,1},{4,2},{5,3},{6,4},{7,5},{8,14},{9,15},{10,... | collective-permute-start | bytes 811016 | tf_op jit(solution)/shard_map/ppermute | solution.py:350
  72.5 11.0 %collective-permute-start.26 = (bf16[528,256]{1,0:T(8,128)(2,1)S(1)}, bf16[528,256]{1,0:T(8,128)(2,1)S(1)}, u32[]{:S(2)}, u32[]{:S(2)}) collective-permute-start(bf16[528,256]{1,0:T(8,128)(2,1)S(1)} %get-tuple-element.60), channel_id=1, source_target_pairs={{0,4},{1,5},{2,6},{3,7},{4,0},{5,1},{6,2},{7,3},{8,12},{9,13},{10,... | collective-permute-start | bytes 811016 | tf_op jit(solution)/shard_map/ppermute | solution.py:405
  73.4 14.0 %collective-permute-start.27 = (bf16[528,256]{1,0:T(8,128)(2,1)S(1)}, bf16[528,256]{1,0:T(8,128)(2,1)S(1)}, u32[]{:S(2)}, u32[]{:S(2)}) collective-permute-start(bf16[528,256]{1,0:T(8,128)(2,1)S(1)} %get-tuple-element.61), channel_id=1, source_target_pairs={{0,6},{1,7},{2,0},{3,1},{4,2},{5,3},{6,4},{7,5},{8,14},{9,15},{10,... | collective-permute-start | bytes 811016 | tf_op jit(solution)/shard_map/ppermute | solution.py:405
  74.6 13.3 %collective-permute-start.28 = (bf16[528,256]{1,0:T(8,128)(2,1)S(1)}, bf16[528,256]{1,0:T(8,128)(2,1)S(1)}, u32[]{:S(2)}, u32[]{:S(2)}) collective-permute-start(bf16[528,256]{1,0:T(8,128)(2,1)S(1)} %get-tuple-element.62), channel_id=1, source_target_pairs={{0,2},{1,3},{2,4},{3,5},{4,6},{5,7},{6,0},{7,1},{8,10},{9,11},{10,... | collective-permute-start | bytes 811016 | tf_op jit(solution)/shard_map/ppermute | solution.py:405
  76.7 16.5 %collective-permute-start.18 = (bf16[528,256]{1,0:T(8,128)(2,1)S(1)}, bf16[528,256]{1,0:T(8,128)(2,1)S(1)}, u32[]{:S(2)}, u32[]{:S(2)}) collective-permute-start(bf16[528,256]{1,0:T(8,128)(2,1)S(1)} %get-tuple-element.52), channel_id=1, source_target_pairs={{0,6},{1,7},{2,0},{3,1},{4,2},{5,3},{6,4},{7,5},{8,14},{9,15},{10,... | collective-permute-start | bytes 811016 | tf_op jit(solution)/shard_map/ppermute | solution.py:405
  76.7 16.9 %collective-permute-start.20 = (bf16[528,256]{1,0:T(8,128)(2,1)S(1)}, bf16[528,256]{1,0:T(8,128)(2,1)S(1)}, u32[]{:S(2)}, u32[]{:S(2)}) collective-permute-start(bf16[528,256]{1,0:T(8,128)(2,1)S(1)} %get-tuple-element.54), channel_id=1, source_target_pairs={{0,8},{1,9},{2,10},{3,11},{4,12},{5,13},{6,14},{7,15},{8,16},{9,17... | collective-permute-start | bytes 811016 | tf_op jit(solution)/shard_map/ppermute | solution.py:405
  83.6 11.8 %collective-permute-start.22 = (bf16[528,256]{1,0:T(8,128)(2,1)S(1)}, bf16[528,256]{1,0:T(8,128)(2,1)S(1)}, u32[]{:S(2)}, u32[]{:S(2)}) collective-permute-start(bf16[528,256]{1,0:T(8,128)(2,1)S(1)} %get-tuple-element.56), channel_id=1, source_target_pairs={{0,2},{1,3},{2,4},{3,5},{4,6},{5,7},{6,0},{7,1},{8,10},{9,11},{10,... | collective-permute-start | bytes 811016 | tf_op jit(solution)/shard_map/ppermute | solution.py:405
  87.5 9.4 %collective-permute-start.24 = (bf16[528,256]{1,0:T(8,128)(2,1)S(1)}, bf16[528,256]{1,0:T(8,128)(2,1)S(1)}, u32[]{:S(2)}, u32[]{:S(2)}) collective-permute-start(bf16[528,256]{1,0:T(8,128)(2,1)S(1)} %get-tuple-element.58), channel_id=1, source_target_pairs={{0,24},{1,25},{2,26},{3,27},{4,28},{5,29},{6,30},{7,31},{8,0},{9,1... | collective-permute-start | bytes 811016 | tf_op jit(solution)/shard_map/ppermute | solution.py:405
  87.9 14.7 %collective-permute-start.30 = (bf16[528,256]{1,0:T(8,128)(2,1)S(1)}, bf16[528,256]{1,0:T(8,128)(2,1)S(1)}, u32[]{:S(2)}, u32[]{:S(2)}) collective-permute-start(bf16[528,256]{1,0:T(8,128)(2,1)S(1)} %get-tuple-element.64), channel_id=1, source_target_pairs={{0,24},{1,25},{2,26},{3,27},{4,28},{5,29},{6,30},{7,31},{8,0},{9,1... | collective-permute-start | bytes 811016 | tf_op jit(solution)/shard_map/ppermute | solution.py:405
  93.2 10.8 %collective-permute-start.31 = (bf16[528,256]{1,0:T(8,128)(2,1)S(1)}, bf16[528,256]{1,0:T(8,128)(2,1)S(1)}, u32[]{:S(2)}, u32[]{:S(2)}) collective-permute-start(bf16[528,256]{1,0:T(8,128)(2,1)S(1)} %get-tuple-element.65), channel_id=1, source_target_pairs={{0,8},{1,9},{2,10},{3,11},{4,12},{5,13},{6,14},{7,15},{8,16},{9,17... | collective-permute-start | bytes 811016 | tf_op jit(solution)/shard_map/ppermute | solution.py:405
  93.6 19.5 %collective-permute-start.19 = (bf16[528,256]{1,0:T(8,128)(2,1)S(1)}, bf16[528,256]{1,0:T(8,128)(2,1)S(1)}, u32[]{:S(2)}, u32[]{:S(2)}) collective-permute-start(bf16[528,256]{1,0:T(8,128)(2,1)S(1)} %add_convert_fusion.14), channel_id=1, source_target_pairs={{0,24},{1,25},{2,26},{3,27},{4,28},{5,29},{6,30},{7,31},{8,0},{9,1... | collective-permute-start | bytes 811016 | tf_op jit(solution)/shard_map/ppermute | solution.py:405
  95.4 17.7 %collective-permute-start.21 = (bf16[528,256]{1,0:T(8,128)(2,1)S(1)}, bf16[528,256]{1,0:T(8,128)(2,1)S(1)}, u32[]{:S(2)}, u32[]{:S(2)}) collective-permute-start(bf16[528,256]{1,0:T(8,128)(2,1)S(1)} %add_convert_fusion.12), channel_id=1, source_target_pairs={{0,6},{1,7},{2,0},{3,1},{4,2},{5,3},{6,4},{7,5},{8,14},{9,15},{10,... | collective-permute-start | bytes 811016 | tf_op jit(solution)/shard_map/ppermute | solution.py:405
  96.8 16.3 %collective-permute-start.23 = (bf16[528,256]{1,0:T(8,128)(2,1)S(1)}, bf16[528,256]{1,0:T(8,128)(2,1)S(1)}, u32[]{:S(2)}, u32[]{:S(2)}) collective-permute-start(bf16[528,256]{1,0:T(8,128)(2,1)S(1)} %add_convert_fusion.10), channel_id=1, source_target_pairs={{0,8},{1,9},{2,10},{3,11},{4,12},{5,13},{6,14},{7,15},{8,16},{9,17... | collective-permute-start | bytes 811016 | tf_op jit(solution)/shard_map/ppermute | solution.py:405
  102.6 10.6 %collective-permute-start.25 = (bf16[528,256]{1,0:T(8,128)(2,1)S(1)}, bf16[528,256]{1,0:T(8,128)(2,1)S(1)}, u32[]{:S(2)}, u32[]{:S(2)}) collective-permute-start(bf16[528,256]{1,0:T(8,128)(2,1)S(1)} %add_convert_fusion.8), channel_id=1, source_target_pairs={{0,2},{1,3},{2,4},{3,5},{4,6},{5,7},{6,0},{7,1},{8,10},{9,11},{10,... | collective-permute-start | bytes 811016 | tf_op jit(solution)/shard_map/ppermute | solution.py:405
  104.0 9.2 %collective-permute-start.29 = (bf16[528,256]{1,0:T(8,128)(2,1)S(1)}, bf16[528,256]{1,0:T(8,128)(2,1)S(1)}, u32[]{:S(2)}, u32[]{:S(2)}) collective-permute-start(bf16[528,256]{1,0:T(8,128)(2,1)S(1)} %add_convert_fusion.4), channel_id=1, source_target_pairs={{0,16},{1,17},{2,18},{3,19},{4,20},{5,21},{6,22},{7,23},{8,24},{9,... | collective-permute-start | bytes 811016 | tf_op jit(solution)/shard_map/ppermute | solution.py:405
  113.2 8.0 %collective-permute-start.32 = (bf16[528,256]{1,0:T(8,128)(2,1)S(1)}, bf16[528,256]{1,0:T(8,128)(2,1)S(1)}, u32[]{:S(2)}, u32[]{:S(2)}) collective-permute-start(bf16[528,256]{1,0:T(8,128)(2,1)S(1)} %add_convert_fusion.1), channel_id=1, source_target_pairs={{0,4},{1,5},{2,6},{3,7},{4,0},{5,1},{6,2},{7,3},{8,12},{9,13},{10,... | collective-permute-start | bytes 811016 | tf_op jit(solution)/shard_map/ppermute | solution.py:405
  121.4 8.0 %collective-permute-start.35 = (bf16[528,256]{1,0:T(8,128)(2,1)S(1)}, bf16[528,256]{1,0:T(8,128)(2,1)S(1)}, u32[]{:S(2)}, u32[]{:S(2)}) collective-permute-start(bf16[528,256]{1,0:T(8,128)(2,1)S(1)} %add_convert_fusion), channel_id=1, source_target_pairs={{0,64},{32,96},{64,0},{96,32},{1,65},{33,97},{65,1},{97,33},{2,66}... | collective-permute-start | bytes 811016 | tf_op jit(solution)/shard_map/ppermute | solution.py:410
  124.7 8.1 %collective-permute-start.34 = (bf16[528,256]{1,0:T(8,128)(2,1)S(1)}, bf16[528,256]{1,0:T(8,128)(2,1)S(1)}, u32[]{:S(2)}, u32[]{:S(2)}) collective-permute-start(bf16[528,256]{1,0:T(8,128)(2,1)S(1)} %add_convert_fusion), channel_id=1, source_target_pairs={{0,96},{32,0},{64,32},{96,64},{1,97},{33,1},{65,33},{97,65},{2,98}... | collective-permute-start | bytes 811016 | tf_op jit(solution)/shard_map/ppermute | solution.py:410
  (7 other events, 22.6 us)

commit v5 on v3

--- a/solution.py
+++ b/solution.py
@@ -10,28 +10,35 @@
 F32, BF16, I32 = jnp.float32, jnp.bfloat16, jnp.int32
 G = 4
 NS = 16
-NP = 64
+NA, NB = 48, 24
+NP = NA + NB
 ROWS = 528
 MIB = 1024 * 1024
 HI = lax.Precision.HIGHEST
 
 TREE = (
     ((0, 1), (0, 0), "x", 1),
+    ((1, 0), (0, 0), "z", 1),
     ((0, 3), (0, 0), "x", 3),
-    ((1, 0), (0, 0), "z", 1),
     ((3, 0), (0, 0), "z", 3),
     ((0, 2), (0, 1), "x", 1),
-    ((1, 3), (1, 0), "x", 3),
-    ((2, 0), (1, 0), "z", 1),
-    ((3, 3), (0, 3), "z", 3),
+    ((2, 0), (3, 0), "z", 3),
     ((1, 1), (1, 0), "x", 1),
     ((3, 1), (0, 1), "z", 3),
+    ((3, 3), (3, 0), "x", 3),
+    ((1, 3), (0, 3), "z", 1),
     ((1, 2), (0, 2), "z", 1),
-    ((3, 2), (3, 3), "x", 3),
     ((2, 1), (2, 0), "x", 1),
+    ((3, 2), (0, 2), "z", 3),
     ((2, 3), (2, 0), "x", 3),
-    ((2, 2), (1, 2), "z", 1),
+    ((2, 2), (2, 0), "x", 2),
 )
+
+
+NEAR = ((0, 0), (0, 1), (1, 0), (0, 3), (3, 0), (0, 2), (2, 0), (1, 1), (3, 1), (3, 3), (1, 3))
+FAR = ((1, 2), (2, 1), (3, 2), (2, 3), (2, 2))
+SLOTS = NEAR + FAR
+NN, NF = len(NEAR), len(FAR)
 
 
 def move(axis, step):
@@ -62,7 +69,10 @@
         slot = jnp.where(spot == r, owner[r], slot)
     dz = ((slot >> 3) - (me >> 3)) & 3
     dx = (((slot >> 1) & 3) - ((me >> 1) & 3)) & 3
-    key = (dz * 4 + dx) * 2 + (slot & 1)
+    rel = jnp.zeros((1, 64), I32)
+    for k, (a, b) in enumerate(SLOTS):
+        rel = jnp.where((dz == a) & (dx == b), k, rel)
+    key = rel * 2 + (slot & 1)
     rows = jnp.concatenate([order[...].astype(F32), target[...], jnp.zeros((1, 16), F32)], 0)
     ray = jnp.where((iota((16, 64), 1) >> 2) == iota((16, 64), 0), 1.0, 0.0)
     spread = jnp.dot(rows, ray, precision=HI, preferred_element_type=F32)
@@ -96,29 +106,39 @@
     pairs = ((count + 1) >> 1).astype(F32)
     eye = iota((NS, 128), 0) == iota((NS, 128), 1)
     pairs_row = jnp.sum(jnp.where(eye, pairs, 0.0), 0, keepdims=True)
-    ahead = iota((NS, 128), 1) < iota((NS, 128), 0)
+    row, lane = iota((NS, 128), 0), iota((NS, 128), 1)
+    ahead = (lane < row) & ((lane >= NN) == (row >= NN))
     start = jnp.sum(jnp.where(ahead, pairs_row, 0.0), 1, keepdims=True)
+    start = start + jnp.where(row[:, 0:1] >= NN, float(NA), 0.0)
     start_row = jnp.sum(jnp.where(eye, start, 0.0), 0, keepdims=True)
     start_j = jnp.sum(hotf * start, 0, keepdims=True).astype(I32)
-    code = start_j + (rank >> 1) + (rank & 1) * NP
+    code = start_j * 2 + rank
     code = jnp.where(valid, code, -1)
     square = iota((128, 128), 0) == iota((128, 128), 1)
     code_col = jnp.sum(jnp.where(square, code.astype(F32), 0.0), 1, keepdims=True)
     source = (iota((128, 128), 0) + 1).astype(F32)
-    hit = code_col.astype(I32) == iota((128, 128), 1)
-    inverse = jnp.sum(jnp.where(hit, source, 0.0), 0, keepdims=True).astype(I32)
-    inverse = jnp.maximum(inverse - 1, 0)
+    inverse = []
+    for h in range(2):
+        hit = code_col.astype(I32) == iota((128, 128), 1) * 2 + h
+        found = jnp.sum(jnp.where(hit, source, 0.0), 0, keepdims=True).astype(I32)
+        inverse.append(jnp.maximum(found - 1, 0))
     begun = jnp.where(start.astype(I32) <= iota((NS, 128), 1), 1.0, 0.0)
     slot_of = jnp.sum(begun, 0, keepdims=True).astype(I32) - 1
-    total = jnp.sum(pairs_row, 1, keepdims=True).astype(I32)
+    near = iota((1, 128), 1) < NN
+    totals = [
+        jnp.sum(jnp.where(near == side, pairs_row, 0.0), 1, keepdims=True).astype(I32)
+        for side in (True, False)
+    ]
     table[...] = jnp.concatenate(
         [
-            inverse,
+            inverse[0],
             slot_of,
             start_row.astype(I32),
             pairs_row.astype(I32),
-            jnp.broadcast_to(total, (1, 128)),
-            jnp.zeros((3, 128), I32),
+            jnp.broadcast_to(totals[0], (1, 128)),
+            jnp.broadcast_to(totals[1], (1, 128)),
+            inverse[1],
+            jnp.zeros((1, 128), I32),
         ],
         0,
     )
@@ -131,16 +151,12 @@
 
 
 def samples(table, xa, i):
-    return jnp.concatenate([xa[table[0, i]], xa[table[0, NP + i]]], 0)
-
-
-def forward_kernel(*refs):
-    table, info, xa = refs[:3]
-    weights = refs[3 : 3 + NS]
-    res, saved, wv, h1, h2 = refs[3 + NS : 8 + NS]
-    raw, wsem = refs[8 + NS :]
-    groups = (table[4, 0] + G - 1) // G
-    for s in range(NS):
+    return jnp.concatenate([xa[table[0, i]], xa[table[6, i]]], 0)
+
+
+def shade(table, xa, weights, wv, h1, h2, raw, wsem, first, base, total):
+    count = len(weights)
+    for s in range(count):
         pltpu.make_async_copy(weights[s], wv.at[s], wsem.at[s]).start()
     raw[...] = jnp.zeros(raw.shape, F32)
 
@@ -150,10 +166,10 @@
 
     def step(t, ready):
         ids = [G * t + g for g in range(G)]
-        slots = [table[1, i] for i in ids]
+        slots = [table[1, base + i] - first for i in ids]
         lax.fori_loop(ready, slots[-1] + 1, held, 0)
         pre = [
-            jnp.dot(samples(table, xa, i), wv[s, 0:256], preferred_element_type=F32)
+            jnp.dot(samples(table, xa, base + i), wv[s, 0:256], preferred_element_type=F32)
             for i, s in zip(ids, slots)
         ]
         one = [jnp.maximum(p, 0.0).astype(BF16) for p in pre]
@@ -175,18 +191,36 @@
             raw[1, rows, :] = out[g][0:8, 128:256]
         return slots[-1] + 1
 
-    lax.fori_loop(lax.fori_loop(0, groups, step, 0), NS, held, 0)
+    done = lax.fori_loop(0, (total + G - 1) // G, step, 0)
+    lax.fori_loop(done, count, held, 0)
+
+
+def forward_near_kernel(*refs):
+    table, xa = refs[:2]
+    raw, wv, h1, h2, wsem = refs[2 + NN :]
+    shade(table, xa, refs[2 : 2 + NN], wv, h1, h2, raw, wsem, 0, 0, table[4, 0])
+
+
+def forward_far_kernel(*refs):
+    table, info, xa, raw_near = refs[:4]
+    res, saved, wv, h1, h2, raw, wsem = refs[4 + NF :]
+    shade(table, xa, refs[4 : 4 + NF], wv, h1, h2, raw, wsem, NN, NA, table[5, 0])
 
     before = jnp.where(iota((128, 128), 0) < iota((128, 128), 1), 1.0, 0.0)
     spot = info[8:9].astype(I32)
     out = jnp.zeros((4, 128), F32)
     for h in range(2):
         lanes = slice(h * 128, h * 128 + 128)
-        pick = spot == iota((NP, 128), 0) + h * NP
+        pick = spot == iota((NP, 128), 0) * 2 + h
         pickb = jnp.where(pick, 1.0, 0.0).astype(BF16)
         deltas = info[16:144].astype(BF16)
         delta = jnp.dot(pickb, deltas, preferred_element_type=F32)
-        ch = [raw[h, pl.ds(c, NP, stride=8), :] for c in range(4)]
+        ch = [
+            jnp.concatenate(
+                [raw_near[h, pl.ds(c, NA, stride=8), :], raw[h, pl.ds(c, NB, stride=8), :]], 0
+            )
+            for c in range(4)
+        ]
         sigma = jnp.maximum(ch[0], 0.0) + jnp.log1p(jnp.exp(-jnp.abs(ch[0])))
         rgb = [jax.nn.sigmoid(ch[c]) for c in (1, 2, 3)]
         tau = sigma * delta
@@ -205,11 +239,10 @@
     res[...] = jnp.concatenate([out, jnp.zeros((4, 128), F32)], 0)
 
 
-def backward_kernel(*refs):
-    table, info, res, res_sib, xa, saved, wv, h1, h2, color_out = refs[:10]
-    grads = refs[10 : 10 + NS]
-    dr, acc1, acc2, acc3 = refs[10 + NS :]
-    groups = (table[4, 0] + G - 1) // G
+def backward_far_kernel(*refs):
+    table, info, res, res_sib, xa, saved, wv, h1, h2, color_out, dr = refs[:11]
+    grads = refs[11 : 11 + NF]
+    accs = refs[11 + NF :]
 
     meta = info[0:8]
     parts = res[...] + pltpu.roll(res_sib[...], 64, 1)
@@ -238,7 +271,7 @@
     dr[...] = jnp.zeros(dr.shape, F32)
     for h in range(2):
         lanes = slice(h * 128, h * 128 + 128)
-        pick = spot == iota((NP, 128), 0) + h * NP
+        pick = spot == iota((NP, 128), 0) * 2 + h
         col = [jnp.sum(jnp.where(pick, row, 0.0), 1, keepdims=True) for row in cot]
         rgb = [saved[c, :, lanes] for c in range(3)]
         weight = saved[3, :, lanes]
@@ -250,19 +283,30 @@
             d_col = weight * col[c] * rgb[c] * (1.0 - rgb[c])
             dr[h, pl.ds(c + 1, NP, stride=8), :] = d_col
 
-    for s in range(NS):
-
-        @pl.when(table[3, s] == 0)
+    gradients(table, dr, xa, wv, h1, h2, grads, accs, NN, NA, table[5, 0])
+
+
+def backward_near_kernel(*refs):
+    table, dr, xa, wv, h1, h2 = refs[:6]
+    grads = refs[6 : 6 + NN]
+    gradients(table, dr, xa, wv, h1, h2, grads, refs[6 + NN :], 0, 0, table[4, 0])
+
+
+def gradients(table, dr, xa, wv, h1, h2, grads, accs, first, base, total):
+    acc1, acc2, acc3 = accs
+    for s in range(len(grads)):
+
+        @pl.when(table[3, first + s] == 0)
         def _():
             grads[s][...] = jnp.zeros((ROWS, 256), BF16)
 
     def step(t, _):
         ids = [G * t + g for g in range(G)]
-        slots = [table[1, i] for i in ids]
+        slots = [table[1, base + i] - first for i in ids]
         tn, nt = (((0,), (0,)), ((), ())), (((1,), (1,)), ((), ()))
         raws = []
         for i in ids:
-            rows = pl.ds(pl.multiple_of(i * 8, 8), 8)
+            rows = pl.ds(pl.multiple_of((base + i) * 8, 8), 8)
             d_raw = jnp.concatenate([dr[0, rows, :], dr[1, rows, :]], 1)
             raws.append(jnp.concatenate([d_raw, jnp.zeros((8, 256), F32)], 0).astype(BF16))
         two = [h2[i] for i in ids]
@@ -282,24 +326,28 @@
         ]
         d_one = [jnp.where(h > 0, d, 0.0).astype(BF16) for h, d in zip(one, dh)]
         g1 = [
-            lax.dot_general(samples(table, xa, i), d, tn, preferred_element_type=F32)
+            lax.dot_general(samples(table, xa, base + i), d, tn, preferred_element_type=F32)
             for i, d in zip(ids, d_one)
         ]
         for g, s in enumerate(slots):
-            first = ids[g] == table[2, s]
-            acc1[s] = jnp.where(first, 0.0, acc1[s]) + g1[g]
-            acc2[s] = jnp.where(first, 0.0, acc2[s]) + g2[g]
-            acc3[s] = jnp.where(first, 0.0, acc3[s]) + g3[g]
+            begins = base + ids[g] == table[2, first + s]
+            acc1[s] = jnp.where(begins, 0.0, acc1[s]) + g1[g]
+            acc2[s] = jnp.where(begins, 0.0, acc2[s]) + g2[g]
+            acc3[s] = jnp.where(begins, 0.0, acc3[s]) + g3[g]
         return 0
 
-    lax.fori_loop(0, groups, step, 0)
-    for s in range(NS):
-
-        @pl.when(table[3, s] > 0)
+    lax.fori_loop(0, (total + G - 1) // G, step, 0)
+    for s in range(len(grads)):
+
+        @pl.when(table[3, first + s] > 0)
         def _():
             grads[s][0:256] = acc1[s].astype(BF16)
             grads[s][256:512] = acc2[s].astype(BF16)
             grads[s][512:528] = acc3[s].astype(BF16)
+
+
+def cost(us):
+    return pl.CostEstimate(flops=int(us * 1e9), bytes_accessed=0, transcendentals=0)
 
 
 def spec(space):
@@ -313,7 +361,7 @@
     far = spec(pltpu.MemorySpace.HBM)
     shape = jax.ShapeDtypeStruct
     dma = pltpu.SemaphoreType.DMA
-    limit = pltpu.CompilerParams(vmem_limit_bytes=15 * MIB)
+    limit = pltpu.CompilerParams(vmem_limit_bytes=10 * MIB)
 
     def away(a):
         return pltpu.with_memory_space_constraint(a, pltpu.MemorySpace.HBM)
@@ -329,13 +377,14 @@
     x_sib, held[(1, 0)] = lax.optimization_barrier((x_sib, held[(1, 0)]))
     for key, source, axis, step in TREE[4:]:
         held[key] = lax.ppermute(held[source], "region", move(axis, -step))
-    weights = [held[(s // 4, s % 4)] for s in range(NS)]
+    weights = [held[key] for key in SLOTS]
 
     meta = pl.pallas_call(
         meta_kernel,
         out_shape=shape((72, 128), F32),
         in_specs=[smem, vmem, vmem, vmem, vmem],
         out_specs=vmem,
+        cost_estimate=cost(1.5),
         name="meta",
     )(owner_map, block_region.T, seg_order.T, target.T, deltas)
     meta_sib = swap(meta)
@@ -346,42 +395,76 @@
         out_specs=(vmem,) * 3,
         scratch_shapes=[dma((8,))],
         compiler_params=limit,
+        cost_estimate=cost(3),
         name="plan",
     )(meta, meta_sib, away(features), x_sib)
 
-    kept = pltpu.VMEM((NP, 256, 256), BF16)
-    res, saved, wv, h1, h2 = pl.pallas_call(
-        forward_kernel,
+    def kept(n):
+        return pltpu.VMEM((n, 256, 256), BF16)
+
+    raw, *near = pl.pallas_call(
+        forward_near_kernel,
+        out_shape=(
+            pltpu.VMEM((2, NA * 8, 128), F32),
+            pltpu.VMEM((NN, ROWS, 256), BF16),
+            kept(NA),
+            kept(NA),
+        ),
+        in_specs=[smem, vmem] + [hbm] * NN,
+        out_specs=(vmem,) * 4,
+        scratch_shapes=[dma((NN,))],
+        compiler_params=limit,
+        cost_estimate=cost(4.5),
+        name="forward_near",
+    )(table, xa, *weights[:NN])
+    res, saved, *far_side = pl.pallas_call(
+        forward_far_kernel,
         out_shape=(
             shape((8, 128), F32),
             pltpu.VMEM((6, NP, 256), F32),
-            pltpu.VMEM((NS, ROWS, 256), BF16),
-            kept,
-            kept,
+            pltpu.VMEM((NF, ROWS, 256), BF16),
+            kept(NB),
+            kept(NB),
         ),
-        in_specs=[smem, vmem, vmem] + [hbm] * NS,
+        in_specs=[smem, vmem, vmem, vmem] + [hbm] * NF,
         out_specs=(vmem,) * 5,
-        scratch_shapes=[pltpu.VMEM((2, NP * 8, 128), F32), dma((NS,))],
+        scratch_shapes=[pltpu.VMEM((2, NB * 8, 128), F32), dma((NF,))],
         compiler_params=limit,
-        name="forward",
-    )(table, info, xa, *weights)
+        cost_estimate=cost(3),
+        name="forward_far",
+    )(table, info, xa, raw, *weights[NN:])
     res_sib = swap(res)
-    color, *grads = pl.pallas_call(
-        backward_kernel,
-        out_shape=(shape((8, 128), F32),) + (pltpu.VMEM((ROWS, 256), BF16),) * NS,
+    def accs(n):
+        return [
+            pltpu.VMEM((n, 256, 256), F32),
+            pltpu.VMEM((n, 256, 256), F32),
+            pltpu.VMEM((n, 16, 256), F32),
+        ]
+
+    color, dr, *far_grads = pl.pallas_call(
+        backward_far_kernel,
+        out_shape=(shape((8, 128), F32), pltpu.VMEM((2, NP * 8, 128), F32))
+        + (pltpu.VMEM((ROWS, 256), BF16),) * NF,
         in_specs=[smem] + [vmem] * 8,
-        out_specs=(vmem,) * (NS + 1),
-        scratch_shapes=[
-            pltpu.VMEM((2, NP * 8, 128), F32),
-            pltpu.VMEM((NS, 256, 256), F32),
-            pltpu.VMEM((NS, 256, 256), F32),
-            pltpu.VMEM((NS, 16, 256), F32),
-        ],
+        out_specs=(vmem,) * (NF + 2),
+        scratch_shapes=accs(NF),
         compiler_params=limit,
-        name="backward",
-    )(table, info, res, res_sib, xa, saved, wv, h1, h2)
-
-    sums = {(s // 4, s % 4): grads[s] for s in range(NS)}
+        cost_estimate=cost(5.6),
+        name="backward_far",
+    )(table, info, res, res_sib, xa, saved, *far_side)
+    near_grads = pl.pallas_call(
+        backward_near_kernel,
+        out_shape=(pltpu.VMEM((ROWS, 256), BF16),) * NN,
+        in_specs=[smem] + [vmem] * 5,
+        out_specs=(vmem,) * NN,
+        scratch_shapes=accs(NN),
+        compiler_params=limit,
+        cost_estimate=cost(7.6),
+        name="backward_near",
+    )(table, dr, xa, *near)
+    grads = list(near_grads) + far_grads
+
+    sums = dict(zip(SLOTS, grads))
     for key, source, axis, step in reversed(TREE):
         got = lax.ppermute(sums[key], "region", move(axis, step))
         sums[source] = (sums[source].astype(F32) + got.astype(F32)).astype(BF16)

time: 127 us -> 117 us (0.921)
  waiting for transfers between devices: 47.8 us -> 35.3 us
  Pallas kernels: 22.3 us -> 26.9 us
  starting transfers between devices: 51.3 us -> 49 us
    ppermute x15, waiting for transfers between devices: 28.1 us -> 15.2 us  [local(): got = lax.ppermute(sums[key], 'region', move(axis, step))]
    ppermute x15, starting transfers between devices: 31.1 us -> 19 us  [local(): held[key] = lax.ppermute(held[source], 'region', move(axis, -step))]
    ppermute x15, starting transfers between devices: 14.7 us -> 24 us  [local(): got = lax.ppermute(sums[key], 'region', move(axis, step))]
    pallas_call x2 -> x4, Pallas kernels: 17.2 us -> 21.9 us  [the longest x1 8.73 us: local(): pl.pallas_call(backward_near_kernel, out_shape=(pltpu.VMEM((ROWS, 256), B...]
  transfers between devices with their start and end apart: 36 -> 36, of which waited for: 18 -> 14; matrix products, arithmetic and copies ran while one was open for 2% -> 2% of each run, Pallas kernels for 4% -> 16%
where the time goes in v5:
time: 117 us
  starting transfers between devices  49 us (42%)
  waiting for transfers between devices  35.3 us (30%)
  Pallas kernels  26.9 us (23%)
  local copies, waits for them, and re-layouts  2.86 us (2%)
  other arithmetic  1.99 us (2%)
    ppermute x15, starting transfers between devices, local(): got = lax.ppermute(sums[key], 'region', move(axis, step))  24 us
    ppermute x15, starting transfers between devices, local(): held[key] = lax.ppermute(held[source], 'region', move(axis, -step))  19 us
    ppermute x15, waiting for transfers between devices, local(): got = lax.ppermute(sums[key], 'region', move(axis, step))  15.2 us
    ppermute x15, waiting for transfers between devices, local(): held[key] = lax.ppermute(held[source], 'region', move(axis, -step))  11.9 us
    pallas_call x1, Pallas kernels, local(): pl.pallas_call(backward_near_kernel, out_shape=(pltpu.VMEM((ROWS, 256), B...  8.73 us
    ppermute x3, waiting for transfers between devices, local(): got = lax.ppermute(mine, 'ray', [(i, (i + d) % 4) for i in range(4)])  6.99 us
    ppermute x3, starting transfers between devices, local(): got = lax.ppermute(mine, 'ray', [(i, (i + d) % 4) for i in range(4)])  5.9 us
    pallas_call x1, Pallas kernels, local(): pl.pallas_call(forward_near_kernel, out_shape=(pltpu.VMEM((2, NA * 8, 128...  5.04 us
  transfers between devices with their start and end apart: 36, of which 14 were waited for; matrix products, arithmetic and copies ran while one was open for 2% of the time, Pallas kernels for 16%

profile of v5, /device:TPU:0, one launch (start us, length us, event | category | flops | bytes accessed | tf_op | source)
XLA Modules:
  0.0 116.9 jit_solution(5390180019961002156)
XLA Ops:
  1.7 2.1 %collective-permute-start.5 = (bf16[528,256]{1,0:T(8,128)(2,1)S(1)}, bf16[528,256]{1,0:T(8,128)(2,1)S(1)}, u32[]{:S(2)}, u32[]{:S(2)}) collective-permute-start(bf16[528,256]{1,0:T(8,128)(2,1)S(1)} %fusion.1.refs_2_), channel_id=1, source_target_pairs={{0,8},{1,9},{2,10},{3,11},{4,12},{5,13},{6,14},{7,15},{8,16},{9,17... | collective-permute-start | bytes 811016 | tf_op jit(solution)/shard_map/ppermute | solution.py:376
  3.8 2.8 %collective-permute-start.3 = (bf16[528,256]{1,0:T(8,128)(2,1)S(1)}, bf16[528,256]{1,0:T(8,128)(2,1)S(1)}, u32[]{:S(2)}, u32[]{:S(2)}) collective-permute-start(bf16[528,256]{1,0:T(8,128)(2,1)S(1)} %fusion.1.refs_2_), channel_id=1, source_target_pairs={{0,6},{1,7},{2,0},{3,1},{4,2},{5,3},{6,4},{7,5},{8,14},{9,15},{10,... | collective-permute-start | bytes 811016 | tf_op jit(solution)/shard_map/ppermute | solution.py:376
  6.6 2.2 %collective-permute-start.2 = (bf16[528,256]{1,0:T(8,128)(2,1)S(1)}, bf16[528,256]{1,0:T(8,128)(2,1)S(1)}, u32[]{:S(2)}, u32[]{:S(2)}) collective-permute-start(bf16[528,256]{1,0:T(8,128)(2,1)S(1)} %fusion.1.refs_2_), channel_id=1, source_target_pairs={{0,24},{1,25},{2,26},{3,27},{4,28},{5,29},{6,30},{7,31},{8,0},{9,1... | collective-permute-start | bytes 811016 | tf_op jit(solution)/shard_map/ppermute | solution.py:376
  8.8 4.3 %collective-permute-done.5.refs_6_ = bf16[528,256]{1,0:T(8,128)(2,1)S(1)} collective-permute-done((bf16[528,256]{1,0:T(8,128)(2,1)S(1)}, bf16[528,256]{1,0:T(8,128)(2,1)S(1)}, u32[]{:S(2)}, u32[]{:S(2)}) %collective-permute-start.5) | collective-permute-done | bytes 270368 | tf_op jit(solution)/shard_map/ppermute | solution.py:376
  14.6 1.6 %meta.1.own = f32[72,128]{1,0:T(8,128)} custom-call(s32[32]{0:T(128)} %owner.1, s32[1,64]{1,0:T(1,128)} %bitcast.23, s32[4,16]{1,0:T(4,128)} %bitcast.21, f32[3,16]{1,0:T(4,128)} %bitcast.22, bf16[64,128]{1,0:T(8,128)(2,1)} %delta.1), custom_call_target="tpu_custom_call" | custom-call | flops 1500000000 | tf_op jit(solution)/shard_map/meta/pallas_call | solution.py:382
  16.8 1.6 %collective-permute-start.9 = (bf16[528,256]{1,0:T(8,128)(2,1)S(1)}, bf16[528,256]{1,0:T(8,128)(2,1)S(1)}, u32[]{:S(2)}, u32[]{:S(2)}) collective-permute-start(bf16[528,256]{1,0:T(8,128)(2,1)S(1)} %collective-permute-done.3.refs_3_), channel_id=1, source_target_pairs={{0,8},{1,9},{2,10},{3,11},{4,12},{5,13},{6,14},{7,15},{8,16},{9,17... | collective-permute-start | bytes 811016 | tf_op jit(solution)/shard_map/ppermute | solution.py:379
  18.4 1.5 %collective-permute-start.6 = (bf16[528,256]{1,0:T(8,128)(2,1)S(1)}, bf16[528,256]{1,0:T(8,128)(2,1)S(1)}, u32[]{:S(2)}, u32[]{:S(2)}) collective-permute-start(bf16[528,256]{1,0:T(8,128)(2,1)S(1)} %collective-permute-done.3.refs_3_), channel_id=1, source_target_pairs={{0,6},{1,7},{2,0},{3,1},{4,2},{5,3},{6,4},{7,5},{8,14},{9,15},{10,... | collective-permute-start | bytes 811016 | tf_op jit(solution)/shard_map/ppermute | solution.py:379
  19.9 1.6 %collective-permute-start.11 = (bf16[528,256]{1,0:T(8,128)(2,1)S(1)}, bf16[528,256]{1,0:T(8,128)(2,1)S(1)}, u32[]{:S(2)}, u32[]{:S(2)}) collective-permute-start(bf16[528,256]{1,0:T(8,128)(2,1)S(1)} %collective-permute-done.4.refs_5_), channel_id=1, source_target_pairs={{0,24},{1,25},{2,26},{3,27},{4,28},{5,29},{6,30},{7,31},{8,0},{9,1... | collective-permute-start | bytes 811016 | tf_op jit(solution)/shard_map/ppermute | solution.py:379
  21.5 2.5 %collective-permute-done.10.refs_11_ = bf16[528,256]{1,0:T(8,128)(2,1)S(1)} collective-permute-done((bf16[528,256]{1,0:T(8,128)(2,1)S(1)}, bf16[528,256]{1,0:T(8,128)(2,1)S(1)}, u32[]{:S(2)}, u32[]{:S(2)}) %collective-permute-start.10) | collective-permute-done | bytes 270368 | tf_op jit(solution)/shard_map/ppermute | solution.py:379
  24.9 3.5 %plan.1 = (s32[8,128]{1,0:T(8,128)S(1)}, f32[144,128]{1,0:T(8,128)S(1)}, bf16[128,128,256]{2,1,0:T(8,128)(2,1)S(1)}) custom-call(f32[72,128]{1,0:T(8,128)S(1)} %copy-done, f32[72,128]{1,0:T(8,128)S(1)} %collective-permute-done.sib, bf16[64,128,256]{2,1,0:T(8,128)(2,1)} %x_own.1, bf16[64,128,256]{2,1,0:T(8,128)(2,1)} %collective-permute-done.1.x_sib), custom_call_target="tpu_custom_call" | custom-call | flops 3000000000 | tf_op jit(solution)/shard_map/plan/pallas_call | solution.py:391
  32.0 1.7 %collective-permute-start.13 = (bf16[528,256]{1,0:T(8,128)(2,1)S(1)}, bf16[528,256]{1,0:T(8,128)(2,1)S(1)}, u32[]{:S(2)}, u32[]{:S(2)}) collective-permute-start(bf16[528,256]{1,0:T(8,128)(2,1)S(1)} %collective-permute-done.7.refs_8_), channel_id=1, source_target_pairs={{0,6},{1,7},{2,0},{3,1},{4,2},{5,3},{6,4},{7,5},{8,14},{9,15},{10,... | collective-permute-start | bytes 811016 | tf_op jit(solution)/shard_map/ppermute | solution.py:379
  33.8 3.2 %collective-permute-done.8.refs_9_ = bf16[528,256]{1,0:T(8,128)(2,1)S(1)} collective-permute-done((bf16[528,256]{1,0:T(8,128)(2,1)S(1)}, bf16[528,256]{1,0:T(8,128)(2,1)S(1)}, u32[]{:S(2)}, u32[]{:S(2)}) %collective-permute-start.8) | collective-permute-done | bytes 270368 | tf_op jit(solution)/shard_map/ppermute | solution.py:379
  38.1 5.0 %forward_near.1 = (f32[2,384,128]{2,1,0:T(8,128)S(1)}, bf16[11,528,256]{2,1,0:T(8,128)(2,1)S(1)}, bf16[48,256,256]{2,1,0:T(8,128)(2,1)S(1)}, bf16[48,256,256]{2,1,0:T(8,128)(2,1)S(1)}) custom-call(s32[8,128]{1,0:T(8,128)S(1)} %get-tuple-element.37.refs_0_, bf16[128,128,256]{2,1,0:T(8,128)(2,1)S(1)} %get-tuple-element.39.refs_1_.refs_2_.refs_4_, ...), custom_call_target="tpu_custom_call" | custom-call | flops 4499999744 | tf_op jit(solution)/shard_map/forward_near/pallas_call | solution.py:405
  43.5 3.1 %forward_far.1 = (f32[8,128]{1,0:T(8,128)S(1)}, f32[6,72,256]{2,1,0:T(8,128)S(1)}, bf16[5,528,256]{2,1,0:T(8,128)(2,1)S(1)}, bf16[24,256,256]{2,1,0:T(8,128)(2,1)S(1)}, bf16[24,256,256]{2,1,0:T(8,128)(2,1)S(1)}) custom-call(s32[8,128]{1,0:T(8,128)S(1)} %get-tuple-element.37.refs_0_, f32[144,128]{1,0:T(8,128)S(1)} %get-tuple-element.38.refs_1_, ...), custom_call_target="tpu_custom_call" | custom-call | flops 3000000000 | tf_op jit(solution)/shard_map/forward_far/pallas_call | solution.py:420
  47.9 5.0 %backward_far.1 = (f32[8,128]{1,0:T(8,128)S(1)}, f32[2,576,128]{2,1,0:T(8,128)S(1)}, bf16[528,256]{1,0:T(8,128)(2,1)S(1)}, bf16[528,256]{1,0:T(8,128)(2,1)S(1)},...) custom-call(s32[8,128]{1,0:T(8,128)S(1)} %get-tuple-element.37.refs_0_, ...), custom_call_target="tpu_custom_call" | custom-call | flops 5600000000 | tf_op jit(solution)/shard_map/backward_far/pallas_call | solution.py:444
  52.9 2.8 %collective-permute-start.19 = (bf16[528,256]{1,0:T(8,128)(2,1)S(1)}, bf16[528,256]{1,0:T(8,128)(2,1)S(1)}, u32[]{:S(2)}, u32[]{:S(2)}) collective-permute-start(bf16[528,256]{1,0:T(8,128)(2,1)S(1)} %get-tuple-element.56), channel_id=1, source_target_pairs={{0,4},{1,5},{2,6},{3,7},{4,0},{5,1},{6,2},{7,3},{8,12},{9,13},{10,... | collective-permute-start | bytes 811016 | tf_op jit(solution)/shard_map/ppermute | solution.py:469
  55.7 2.0 %collective-permute-start.20 = (bf16[528,256]{1,0:T(8,128)(2,1)S(1)}, bf16[528,256]{1,0:T(8,128)(2,1)S(1)}, u32[]{:S(2)}, u32[]{:S(2)}) collective-permute-start(bf16[528,256]{1,0:T(8,128)(2,1)S(1)} %get-tuple-element.57), channel_id=1, source_target_pairs={{0,6},{1,7},{2,0},{3,1},{4,2},{5,3},{6,4},{7,5},{8,14},{9,15},{10,... | collective-permute-start | bytes 811016 | tf_op jit(solution)/shard_map/ppermute | solution.py:469
  57.9 8.7 %backward_near.1 = (bf16[528,256]{1,0:T(8,128)(2,1)S(1)}, bf16[528,256]{1,0:T(8,128)(2,1)S(1)}, bf16[528,256]{1,0:T(8,128)(2,1)S(1)}, bf16[528,256]{1,0:T(8,128)...) custom-call(s32[8,128]{1,0:T(8,128)S(1)} %get-tuple-element.37.refs_, ...), custom_call_target="tpu_custom_call" | custom-call | flops 7600000000 | tf_op jit(solution)/shard_map/backward_near/pallas_call | solution.py:455
  68.1 2.6 %collective-permute-start.18 = (bf16[528,256]{1,0:T(8,128)(2,1)S(1)}, bf16[528,256]{1,0:T(8,128)(2,1)S(1)}, u32[]{:S(2)}, u32[]{:S(2)}) collective-permute-start(bf16[528,256]{1,0:T(8,128)(2,1)S(1)} %get-tuple-element.54), channel_id=1, source_target_pairs={{0,6},{1,7},{2,0},{3,1},{4,2},{5,3},{6,4},{7,5},{8,14},{9,15},{10,... | collective-permute-start | bytes 811016 | tf_op jit(solution)/shard_map/ppermute | solution.py:469
  70.7 2.7 %collective-permute-start.29 = (bf16[528,256]{1,0:T(8,128)(2,1)S(1)}, bf16[528,256]{1,0:T(8,128)(2,1)S(1)}, u32[]{:S(2)}, u32[]{:S(2)}) collective-permute-start(bf16[528,256]{1,0:T(8,128)(2,1)S(1)} %get-tuple-element.66), channel_id=1, source_target_pairs={{0,24},{1,25},{2,26},{3,27},{4,28},{5,29},{6,30},{7,31},{8,0},{9,1... | collective-permute-start | bytes 811016 | tf_op jit(solution)/shard_map/ppermute | solution.py:469
  74.7 2.7 %collective-permute-start.28 = (bf16[528,256]{1,0:T(8,128)(2,1)S(1)}, bf16[528,256]{1,0:T(8,128)(2,1)S(1)}, u32[]{:S(2)}, u32[]{:S(2)}) collective-permute-start(bf16[528,256]{1,0:T(8,128)(2,1)S(1)} %get-tuple-element.64), channel_id=1, source_target_pairs={{0,24},{1,25},{2,26},{3,27},{4,28},{5,29},{6,30},{7,31},{8,0},{9,1... | collective-permute-start | bytes 811016 | tf_op jit(solution)/shard_map/ppermute | solution.py:469
  77.4 3.1 %collective-permute-done.29 = bf16[528,256]{1,0:T(8,128)(2,1)S(1)} collective-permute-done((bf16[528,256]{1,0:T(8,128)(2,1)S(1)}, bf16[528,256]{1,0:T(8,128)(2,1)S(1)}, u32[]{:S(2)}, u32[]{:S(2)}) %collective-permute-start.29) | collective-permute-done | bytes 270368 | tf_op jit(solution)/shard_map/ppermute | solution.py:469
  80.5 1.8 %collective-permute-start.25 = (bf16[528,256]{1,0:T(8,128)(2,1)S(1)}, bf16[528,256]{1,0:T(8,128)(2,1)S(1)}, u32[]{:S(2)}, u32[]{:S(2)}) collective-permute-start(bf16[528,256]{1,0:T(8,128)(2,1)S(1)} %add_convert_fusion.8), channel_id=1, source_target_pairs={{0,6},{1,7},{2,0},{3,1},{4,2},{5,3},{6,4},{7,5},{8,14},{9,15},{10,... | collective-permute-start | bytes 811016 | tf_op jit(solution)/shard_map/ppermute | solution.py:469
  82.3 3.5 %collective-permute-start.22 = (bf16[528,256]{1,0:T(8,128)(2,1)S(1)}, bf16[528,256]{1,0:T(8,128)(2,1)S(1)}, u32[]{:S(2)}, u32[]{:S(2)}) collective-permute-start(bf16[528,256]{1,0:T(8,128)(2,1)S(1)} %add_convert_fusion.11), channel_id=1, source_target_pairs={{0,24},{1,25},{2,26},{3,27},{4,28},{5,29},{6,30},{7,31},{8,0},{9,1... | collective-permute-start | bytes 811016 | tf_op jit(solution)/shard_map/ppermute | solution.py:469
  86.4 3.9 %collective-permute-done.22 = bf16[528,256]{1,0:T(8,128)(2,1)S(1)} collective-permute-done((bf16[528,256]{1,0:T(8,128)(2,1)S(1)}, bf16[528,256]{1,0:T(8,128)(2,1)S(1)}, u32[]{:S(2)}, u32[]{:S(2)}) %collective-permute-start.22) | collective-permute-done | bytes 270368 | tf_op jit(solution)/shard_map/ppermute | solution.py:469
  90.4 3.3 %collective-permute-start.23 = (bf16[528,256]{1,0:T(8,128)(2,1)S(1)}, bf16[528,256]{1,0:T(8,128)(2,1)S(1)}, u32[]{:S(2)}, u32[]{:S(2)}) collective-permute-start(bf16[528,256]{1,0:T(8,128)(2,1)S(1)} %add_convert_fusion.10), channel_id=1, source_target_pairs={{0,24},{1,25},{2,26},{3,27},{4,28},{5,29},{6,30},{7,31},{8,0},{9,1... | collective-permute-start | bytes 811016 | tf_op jit(solution)/shard_map/ppermute | solution.py:469
  94.4 3.2 %collective-permute-done.23 = bf16[528,256]{1,0:T(8,128)(2,1)S(1)} collective-permute-done((bf16[528,256]{1,0:T(8,128)(2,1)S(1)}, bf16[528,256]{1,0:T(8,128)(2,1)S(1)}, u32[]{:S(2)}, u32[]{:S(2)}) %collective-permute-start.23) | collective-permute-done | bytes 270368 | tf_op jit(solution)/shard_map/ppermute | solution.py:469
  97.7 3.9 %collective-permute-done.32 = bf16[528,256]{1,0:T(8,128)(2,1)S(1)} collective-permute-done((bf16[528,256]{1,0:T(8,128)(2,1)S(1)}, bf16[528,256]{1,0:T(8,128)(2,1)S(1)}, u32[]{:S(2)}, u32[]{:S(2)}) %collective-permute-start.32) | collective-permute-done | bytes 270368 | tf_op jit(solution)/shard_map/ppermute | solution.py:469
  101.7 3.3 %collective-permute-start.35 = (bf16[528,256]{1,0:T(8,128)(2,1)S(1)}, bf16[528,256]{1,0:T(8,128)(2,1)S(1)}, u32[]{:S(2)}, u32[]{:S(2)}) collective-permute-start(bf16[528,256]{1,0:T(8,128)(2,1)S(1)} %add_convert_fusion), channel_id=1, source_target_pairs={{0,64},{32,96},{64,0},{96,32},{1,65},{33,97},{65,1},{97,33},{2,66}... | collective-permute-start | bytes 811016 | tf_op jit(solution)/shard_map/ppermute | solution.py:474
  105.1 2.6 %collective-permute-start.34 = (bf16[528,256]{1,0:T(8,128)(2,1)S(1)}, bf16[528,256]{1,0:T(8,128)(2,1)S(1)}, u32[]{:S(2)}, u32[]{:S(2)}) collective-permute-start(bf16[528,256]{1,0:T(8,128)(2,1)S(1)} %add_convert_fusion), channel_id=1, source_target_pairs={{0,96},{32,0},{64,32},{96,64},{1,97},{33,1},{65,33},{97,65},{2,98}... | collective-permute-start | bytes 811016 | tf_op jit(solution)/shard_map/ppermute | solution.py:474
  108.3 3.2 %collective-permute-done.35 = bf16[528,256]{1,0:T(8,128)(2,1)S(1)} collective-permute-done((bf16[528,256]{1,0:T(8,128)(2,1)S(1)}, bf16[528,256]{1,0:T(8,128)(2,1)S(1)}, u32[]{:S(2)}, u32[]{:S(2)}) %collective-permute-start.35) | collective-permute-done | bytes 270368 | tf_op jit(solution)/shard_map/ppermute | solution.py:474
  111.5 3.0 %collective-permute-done.34 = bf16[528,256]{1,0:T(8,128)(2,1)S(1)} collective-permute-done((bf16[528,256]{1,0:T(8,128)(2,1)S(1)}, bf16[528,256]{1,0:T(8,128)(2,1)S(1)}, u32[]{:S(2)}, u32[]{:S(2)}) %collective-permute-start.34) | collective-permute-done | bytes 270368 | tf_op jit(solution)/shard_map/ppermute | solution.py:474
  (60 shorter events, 18.1 us)
Async XLA Ops:
  0.6 16.2 %collective-permute-start.1 = (bf16[64,128,256]{2,1,0:T(8,128)(2,1)}, bf16[64,128,256]{2,1,0:T(8,128)(2,1)}, u32[]{:S(2)}, u32[]{:S(2)}) collective-permute-start(bf16[64,128,256]{2,1,0:T(8,128)(2,1)} %x_own.1), channel_id=1, source_target_pairs={{0,1},{1,0},{2,3},{3,2},{4,5},{5,4},{6,7},{7,6},{8,9},{9,8},{10,11... | collective-permute-start | bytes 12582920 | tf_op jit(solution)/shard_map/ppermute | solution.py:370
  1.7 11.3 %collective-permute-start.5 = (bf16[528,256]{1,0:T(8,128)(2,1)S(1)}, bf16[528,256]{1,0:T(8,128)(2,1)S(1)}, u32[]{:S(2)}, u32[]{:S(2)}) collective-permute-start(bf16[528,256]{1,0:T(8,128)(2,1)S(1)} %fusion.1.refs_2_), channel_id=1, source_target_pairs={{0,8},{1,9},{2,10},{3,11},{4,12},{5,13},{6,14},{7,15},{8,16},{9,17... | collective-permute-start | bytes 811016 | tf_op jit(solution)/shard_map/ppermute | solution.py:376
  3.8 12.3 %collective-permute-start.3 = (bf16[528,256]{1,0:T(8,128)(2,1)S(1)}, bf16[528,256]{1,0:T(8,128)(2,1)S(1)}, u32[]{:S(2)}, u32[]{:S(2)}) collective-permute-start(bf16[528,256]{1,0:T(8,128)(2,1)S(1)} %fusion.1.refs_2_), channel_id=1, source_target_pairs={{0,6},{1,7},{2,0},{3,1},{4,2},{5,3},{6,4},{7,5},{8,14},{9,15},{10,... | collective-permute-start | bytes 811016 | tf_op jit(solution)/shard_map/ppermute | solution.py:376
  6.6 9.6 %collective-permute-start.2 = (bf16[528,256]{1,0:T(8,128)(2,1)S(1)}, bf16[528,256]{1,0:T(8,128)(2,1)S(1)}, u32[]{:S(2)}, u32[]{:S(2)}) collective-permute-start(bf16[528,256]{1,0:T(8,128)(2,1)S(1)} %fusion.1.refs_2_), channel_id=1, source_target_pairs={{0,24},{1,25},{2,26},{3,27},{4,28},{5,29},{6,30},{7,31},{8,0},{9,1... | collective-permute-start | bytes 811016 | tf_op jit(solution)/shard_map/ppermute | solution.py:376
  8.8 11.2 %collective-permute-start.4 = (bf16[528,256]{1,0:T(8,128)(2,1)S(1)}, bf16[528,256]{1,0:T(8,128)(2,1)S(1)}, u32[]{:S(2)}, u32[]{:S(2)}) collective-permute-start(bf16[528,256]{1,0:T(8,128)(2,1)S(1)} %fusion.1.refs_2_), channel_id=1, source_target_pairs={{0,2},{1,3},{2,4},{3,5},{4,6},{5,7},{6,0},{7,1},{8,10},{9,11},{10,... | collective-permute-start | bytes 811016 | tf_op jit(solution)/shard_map/ppermute | solution.py:376
  13.1 11.0 %collective-permute-start.10 = (bf16[528,256]{1,0:T(8,128)(2,1)S(1)}, bf16[528,256]{1,0:T(8,128)(2,1)S(1)}, u32[]{:S(2)}, u32[]{:S(2)}) collective-permute-start(bf16[528,256]{1,0:T(8,128)(2,1)S(1)} %collective-permute-done.5.refs_6_), channel_id=1, source_target_pairs={{0,2},{1,3},{2,4},{3,5},{4,6},{5,7},{6,0},{7,1},{8,10},{9,11},{10,... | collective-permute-start | bytes 811016 | tf_op jit(solution)/shard_map/ppermute | solution.py:379
  16.1 12.2 %collective-permute-start.7 = (bf16[528,256]{1,0:T(8,128)(2,1)S(1)}, bf16[528,256]{1,0:T(8,128)(2,1)S(1)}, u32[]{:S(2)}, u32[]{:S(2)}) collective-permute-start(bf16[528,256]{1,0:T(8,128)(2,1)S(1)} %collective-permute-done.5.refs_6_), channel_id=1, source_target_pairs={{0,8},{1,9},{2,10},{3,11},{4,12},{5,13},{6,14},{7,15},{8,16},{9,17... | collective-permute-start | bytes 811016 | tf_op jit(solution)/shard_map/ppermute | solution.py:379
  16.8 15.2 %collective-permute-start.9 = (bf16[528,256]{1,0:T(8,128)(2,1)S(1)}, bf16[528,256]{1,0:T(8,128)(2,1)S(1)}, u32[]{:S(2)}, u32[]{:S(2)}) collective-permute-start(bf16[528,256]{1,0:T(8,128)(2,1)S(1)} %collective-permute-done.3.refs_3_), channel_id=1, source_target_pairs={{0,8},{1,9},{2,10},{3,11},{4,12},{5,13},{6,14},{7,15},{8,16},{9,17... | collective-permute-start | bytes 811016 | tf_op jit(solution)/shard_map/ppermute | solution.py:379
  18.4 15.4 %collective-permute-start.6 = (bf16[528,256]{1,0:T(8,128)(2,1)S(1)}, bf16[528,256]{1,0:T(8,128)(2,1)S(1)}, u32[]{:S(2)}, u32[]{:S(2)}) collective-permute-start(bf16[528,256]{1,0:T(8,128)(2,1)S(1)} %collective-permute-done.3.refs_3_), channel_id=1, source_target_pairs={{0,6},{1,7},{2,0},{3,1},{4,2},{5,3},{6,4},{7,5},{8,14},{9,15},{10,... | collective-permute-start | bytes 811016 | tf_op jit(solution)/shard_map/ppermute | solution.py:379
  19.9 9.6 %collective-permute-start.11 = (bf16[528,256]{1,0:T(8,128)(2,1)S(1)}, bf16[528,256]{1,0:T(8,128)(2,1)S(1)}, u32[]{:S(2)}, u32[]{:S(2)}) collective-permute-start(bf16[528,256]{1,0:T(8,128)(2,1)S(1)} %collective-permute-done.4.refs_5_), channel_id=1, source_target_pairs={{0,24},{1,25},{2,26},{3,27},{4,28},{5,29},{6,30},{7,31},{8,0},{9,1... | collective-permute-start | bytes 811016 | tf_op jit(solution)/shard_map/ppermute | solution.py:379
  24.1 12.9 %collective-permute-start.8 = (bf16[528,256]{1,0:T(8,128)(2,1)S(1)}, bf16[528,256]{1,0:T(8,128)(2,1)S(1)}, u32[]{:S(2)}, u32[]{:S(2)}) collective-permute-start(bf16[528,256]{1,0:T(8,128)(2,1)S(1)} %collective-permute-done.2.refs_4_), channel_id=1, source_target_pairs={{0,6},{1,7},{2,0},{3,1},{4,2},{5,3},{6,4},{7,5},{8,14},{9,15},{10,... | collective-permute-start | bytes 811016 | tf_op jit(solution)/shard_map/ppermute | solution.py:379
  28.4 14.8 %collective-permute-start.16 = (bf16[528,256]{1,0:T(8,128)(2,1)S(1)}, bf16[528,256]{1,0:T(8,128)(2,1)S(1)}, u32[]{:S(2)}, u32[]{:S(2)}) collective-permute-start(bf16[528,256]{1,0:T(8,128)(2,1)S(1)} %collective-permute-done.7.refs_8_), channel_id=1, source_target_pairs={{0,4},{1,5},{2,6},{3,7},{4,0},{5,1},{6,2},{7,3},{8,12},{9,13},{10,... | collective-permute-start | bytes 811016 | tf_op jit(solution)/shard_map/ppermute | solution.py:379
  29.6 13.6 %collective-permute-start.15 = (bf16[528,256]{1,0:T(8,128)(2,1)S(1)}, bf16[528,256]{1,0:T(8,128)(2,1)S(1)}, u32[]{:S(2)}, u32[]{:S(2)}) collective-permute-start(bf16[528,256]{1,0:T(8,128)(2,1)S(1)} %collective-permute-done.7.refs_8_), channel_id=1, source_target_pairs={{0,2},{1,3},{2,4},{3,5},{4,6},{5,7},{6,0},{7,1},{8,10},{9,11},{10,... | collective-permute-start | bytes 811016 | tf_op jit(solution)/shard_map/ppermute | solution.py:379
  32.0 11.5 %collective-permute-start.13 = (bf16[528,256]{1,0:T(8,128)(2,1)S(1)}, bf16[528,256]{1,0:T(8,128)(2,1)S(1)}, u32[]{:S(2)}, u32[]{:S(2)}) collective-permute-start(bf16[528,256]{1,0:T(8,128)(2,1)S(1)} %collective-permute-done.7.refs_8_), channel_id=1, source_target_pairs={{0,6},{1,7},{2,0},{3,1},{4,2},{5,3},{6,4},{7,5},{8,14},{9,15},{10,... | collective-permute-start | bytes 811016 | tf_op jit(solution)/shard_map/ppermute | solution.py:379
  33.8 9.7 %collective-permute-start.14 = (bf16[528,256]{1,0:T(8,128)(2,1)S(1)}, bf16[528,256]{1,0:T(8,128)(2,1)S(1)}, u32[]{:S(2)}, u32[]{:S(2)}) collective-permute-start(bf16[528,256]{1,0:T(8,128)(2,1)S(1)} %collective-permute-done.6.refs_7_), channel_id=1, source_target_pairs={{0,8},{1,9},{2,10},{3,11},{4,12},{5,13},{6,14},{7,15},{8,16},{9,17... | collective-permute-start | bytes 811016 | tf_op jit(solution)/shard_map/ppermute | solution.py:379
  52.9 17.8 %collective-permute-start.19 = (bf16[528,256]{1,0:T(8,128)(2,1)S(1)}, bf16[528,256]{1,0:T(8,128)(2,1)S(1)}, u32[]{:S(2)}, u32[]{:S(2)}) collective-permute-start(bf16[528,256]{1,0:T(8,128)(2,1)S(1)} %get-tuple-element.56), channel_id=1, source_target_pairs={{0,4},{1,5},{2,6},{3,7},{4,0},{5,1},{6,2},{7,3},{8,12},{9,13},{10,... | collective-permute-start | bytes 811016 | tf_op jit(solution)/shard_map/ppermute | solution.py:469
  55.7 15.0 %collective-permute-start.20 = (bf16[528,256]{1,0:T(8,128)(2,1)S(1)}, bf16[528,256]{1,0:T(8,128)(2,1)S(1)}, u32[]{:S(2)}, u32[]{:S(2)}) collective-permute-start(bf16[528,256]{1,0:T(8,128)(2,1)S(1)} %get-tuple-element.57), channel_id=1, source_target_pairs={{0,6},{1,7},{2,0},{3,1},{4,2},{5,3},{6,4},{7,5},{8,14},{9,15},{10,... | collective-permute-start | bytes 811016 | tf_op jit(solution)/shard_map/ppermute | solution.py:469
  57.7 15.7 %collective-permute-start.21 = (bf16[528,256]{1,0:T(8,128)(2,1)S(1)}, bf16[528,256]{1,0:T(8,128)(2,1)S(1)}, u32[]{:S(2)}, u32[]{:S(2)}) collective-permute-start(bf16[528,256]{1,0:T(8,128)(2,1)S(1)} %get-tuple-element.58), channel_id=1, source_target_pairs={{0,2},{1,3},{2,4},{3,5},{4,6},{5,7},{6,0},{7,1},{8,10},{9,11},{10,... | collective-permute-start | bytes 811016 | tf_op jit(solution)/shard_map/ppermute | solution.py:469
  66.7 8.0 %collective-permute-start.24 = (bf16[528,256]{1,0:T(8,128)(2,1)S(1)}, bf16[528,256]{1,0:T(8,128)(2,1)S(1)}, u32[]{:S(2)}, u32[]{:S(2)}) collective-permute-start(bf16[528,256]{1,0:T(8,128)(2,1)S(1)} %get-tuple-element.60), channel_id=1, source_target_pairs={{0,8},{1,9},{2,10},{3,11},{4,12},{5,13},{6,14},{7,15},{8,16},{9,17... | collective-permute-start | bytes 811016 | tf_op jit(solution)/shard_map/ppermute | solution.py:469
  68.1 18.3 %collective-permute-start.18 = (bf16[528,256]{1,0:T(8,128)(2,1)S(1)}, bf16[528,256]{1,0:T(8,128)(2,1)S(1)}, u32[]{:S(2)}, u32[]{:S(2)}) collective-permute-start(bf16[528,256]{1,0:T(8,128)(2,1)S(1)} %get-tuple-element.54), channel_id=1, source_target_pairs={{0,6},{1,7},{2,0},{3,1},{4,2},{5,3},{6,4},{7,5},{8,14},{9,15},{10,... | collective-permute-start | bytes 811016 | tf_op jit(solution)/shard_map/ppermute | solution.py:469
  70.7 15.3 %collective-permute-start.26 = (bf16[528,256]{1,0:T(8,128)(2,1)S(1)}, bf16[528,256]{1,0:T(8,128)(2,1)S(1)}, u32[]{:S(2)}, u32[]{:S(2)}) collective-permute-start(bf16[528,256]{1,0:T(8,128)(2,1)S(1)} %get-tuple-element.62), channel_id=1, source_target_pairs={{0,2},{1,3},{2,4},{3,5},{4,6},{5,7},{6,0},{7,1},{8,10},{9,11},{10,... | collective-permute-start | bytes 811016 | tf_op jit(solution)/shard_map/ppermute | solution.py:469
  70.7 9.8 %collective-permute-start.29 = (bf16[528,256]{1,0:T(8,128)(2,1)S(1)}, bf16[528,256]{1,0:T(8,128)(2,1)S(1)}, u32[]{:S(2)}, u32[]{:S(2)}) collective-permute-start(bf16[528,256]{1,0:T(8,128)(2,1)S(1)} %get-tuple-element.66), channel_id=1, source_target_pairs={{0,24},{1,25},{2,26},{3,27},{4,28},{5,29},{6,30},{7,31},{8,0},{9,1... | collective-permute-start | bytes 811016 | tf_op jit(solution)/shard_map/ppermute | solution.py:469
  73.4 8.9 %collective-permute-start.30 = (bf16[528,256]{1,0:T(8,128)(2,1)S(1)}, bf16[528,256]{1,0:T(8,128)(2,1)S(1)}, u32[]{:S(2)}, u32[]{:S(2)}) collective-permute-start(bf16[528,256]{1,0:T(8,128)(2,1)S(1)} %get-tuple-element.67), channel_id=1, source_target_pairs={{0,8},{1,9},{2,10},{3,11},{4,12},{5,13},{6,14},{7,15},{8,16},{9,17... | collective-permute-start | bytes 811016 | tf_op jit(solution)/shard_map/ppermute | solution.py:469
  74.7 19.0 %collective-permute-start.28 = (bf16[528,256]{1,0:T(8,128)(2,1)S(1)}, bf16[528,256]{1,0:T(8,128)(2,1)S(1)}, u32[]{:S(2)}, u32[]{:S(2)}) collective-permute-start(bf16[528,256]{1,0:T(8,128)(2,1)S(1)} %get-tuple-element.64), channel_id=1, source_target_pairs={{0,24},{1,25},{2,26},{3,27},{4,28},{5,29},{6,30},{7,31},{8,0},{9,1... | collective-permute-start | bytes 811016 | tf_op jit(solution)/shard_map/ppermute | solution.py:469
  80.5 13.9 %collective-permute-start.25 = (bf16[528,256]{1,0:T(8,128)(2,1)S(1)}, bf16[528,256]{1,0:T(8,128)(2,1)S(1)}, u32[]{:S(2)}, u32[]{:S(2)}) collective-permute-start(bf16[528,256]{1,0:T(8,128)(2,1)S(1)} %add_convert_fusion.8), channel_id=1, source_target_pairs={{0,6},{1,7},{2,0},{3,1},{4,2},{5,3},{6,4},{7,5},{8,14},{9,15},{10,... | collective-permute-start | bytes 811016 | tf_op jit(solution)/shard_map/ppermute | solution.py:469
  82.3 8.0 %collective-permute-start.22 = (bf16[528,256]{1,0:T(8,128)(2,1)S(1)}, bf16[528,256]{1,0:T(8,128)(2,1)S(1)}, u32[]{:S(2)}, u32[]{:S(2)}) collective-permute-start(bf16[528,256]{1,0:T(8,128)(2,1)S(1)} %add_convert_fusion.11), channel_id=1, source_target_pairs={{0,24},{1,25},{2,26},{3,27},{4,28},{5,29},{6,30},{7,31},{8,0},{9,1... | collective-permute-start | bytes 811016 | tf_op jit(solution)/shard_map/ppermute | solution.py:469
  86.0 7.7 %collective-permute-start.31 = (bf16[528,256]{1,0:T(8,128)(2,1)S(1)}, bf16[528,256]{1,0:T(8,128)(2,1)S(1)}, u32[]{:S(2)}, u32[]{:S(2)}) collective-permute-start(bf16[528,256]{1,0:T(8,128)(2,1)S(1)} %add_convert_fusion.2), channel_id=1, source_target_pairs={{0,2},{1,3},{2,4},{3,5},{4,6},{5,7},{6,0},{7,1},{8,10},{9,11},{10,... | collective-permute-start | bytes 811016 | tf_op jit(solution)/shard_map/ppermute | solution.py:469
  86.3 8.1 %collective-permute-start.27 = (bf16[528,256]{1,0:T(8,128)(2,1)S(1)}, bf16[528,256]{1,0:T(8,128)(2,1)S(1)}, u32[]{:S(2)}, u32[]{:S(2)}) collective-permute-start(bf16[528,256]{1,0:T(8,128)(2,1)S(1)} %add_convert_fusion.6), channel_id=1, source_target_pairs={{0,8},{1,9},{2,10},{3,11},{4,12},{5,13},{6,14},{7,15},{8,16},{9,17... | collective-permute-start | bytes 811016 | tf_op jit(solution)/shard_map/ppermute | solution.py:469
  93.8 7.7 %collective-permute-start.32 = (bf16[528,256]{1,0:T(8,128)(2,1)S(1)}, bf16[528,256]{1,0:T(8,128)(2,1)S(1)}, u32[]{:S(2)}, u32[]{:S(2)}) collective-permute-start(bf16[528,256]{1,0:T(8,128)(2,1)S(1)} %add_convert_fusion.1), channel_id=1, source_target_pairs={{0,2},{1,3},{2,4},{3,5},{4,6},{5,7},{6,0},{7,1},{8,10},{9,11},{10,... | collective-permute-start | bytes 811016 | tf_op jit(solution)/shard_map/ppermute | solution.py:469
  101.7 9.7 %collective-permute-start.35 = (bf16[528,256]{1,0:T(8,128)(2,1)S(1)}, bf16[528,256]{1,0:T(8,128)(2,1)S(1)}, u32[]{:S(2)}, u32[]{:S(2)}) collective-permute-start(bf16[528,256]{1,0:T(8,128)(2,1)S(1)} %add_convert_fusion), channel_id=1, source_target_pairs={{0,64},{32,96},{64,0},{96,32},{1,65},{33,97},{65,1},{97,33},{2,66}... | collective-permute-start | bytes 811016 | tf_op jit(solution)/shard_map/ppermute | solution.py:474
  105.1 9.4 %collective-permute-start.34 = (bf16[528,256]{1,0:T(8,128)(2,1)S(1)}, bf16[528,256]{1,0:T(8,128)(2,1)S(1)}, u32[]{:S(2)}, u32[]{:S(2)}) collective-permute-start(bf16[528,256]{1,0:T(8,128)(2,1)S(1)} %add_convert_fusion), channel_id=1, source_target_pairs={{0,96},{32,0},{64,32},{96,64},{1,97},{33,1},{65,33},{97,65},{2,98}... | collective-permute-start | bytes 811016 | tf_op jit(solution)/shard_map/ppermute | solution.py:474
  107.6 7.7 %collective-permute-start.33 = (bf16[528,256]{1,0:T(8,128)(2,1)S(1)}, bf16[528,256]{1,0:T(8,128)(2,1)S(1)}, u32[]{:S(2)}, u32[]{:S(2)}) collective-permute-start(bf16[528,256]{1,0:T(8,128)(2,1)S(1)} %add_convert_fusion), channel_id=1, source_target_pairs={{0,32},{32,64},{64,96},{96,0},{1,33},{33,65},{65,97},{97,1},{2,34}... | collective-permute-start | bytes 811016 | tf_op jit(solution)/shard_map/ppermute | solution.py:474
  (5 other events, 18.1 us)

commit v6 on v5

--- a/solution.py
+++ b/solution.py
@@ -469,12 +469,19 @@
         got = lax.ppermute(sums[key], "region", move(axis, step))
         sums[source] = (sums[source].astype(F32) + got.astype(F32)).astype(BF16)
     mine = sums[(0, 0)]
-    total = mine.astype(F32)
+    parts = [mine]
     for d in (1, 3, 2):
-        got = lax.ppermute(mine, "ray", [(i, (i + d) % 4) for i in range(4)])
-        total = total + got.astype(F32)
+        parts.append(lax.ppermute(mine, "ray", [(i, (i + d) % 4) for i in range(4)]))
+
+    def ray_sum(rows):
+        first, *others = [part[rows].astype(F32) for part in parts]
+        for other in others:
+            first = first + other
+        return first
+
     ray_color = color[0:3, 0:64:4].T
-    return ray_color, total[None, 0:256], total[None, 256:512], total[512:516].T[None]
+    grad_out = ray_sum(slice(512, 516)).T
+    return ray_color, ray_sum(slice(0, 256))[None], ray_sum(slice(256, 512))[None], grad_out[None]
 
 
 def solution(mesh):

time: 117 us -> 118 us (level)
  local copies, waits for them, and re-layouts: 2.86 us -> 1.44 us
  other arithmetic: 1.99 us -> 3.36 us
  starting transfers between devices: 49 us -> 50.2 us
    broadcast_in_dim x0 -> x2, other arithmetic: none -> 1.51 us  [the longest x1 0.91 us: local(): ray_sum(slice(256, 512))[None]]
    broadcast_in_dim x2 -> x0, local copies, waits for them, and re-layouts: 1.42 us -> none  [the longest x1 0.82 us: local(): total[None, 256:512]]
where the time goes in v6:
time: 118 us
  starting transfers between devices  50.2 us (43%)
  waiting for transfers between devices  34.9 us (30%)
  Pallas kernels  26.9 us (23%)
  other arithmetic  3.36 us (3%)
  local copies, waits for them, and re-layouts  1.44 us (1%)
    ppermute x15, starting transfers between devices, local(): got = lax.ppermute(sums[key], 'region', move(axis, step))  24.8 us
    ppermute x15, starting transfers between devices, local(): held[key] = lax.ppermute(held[source], 'region', move(axis, -step))  19 us
    ppermute x15, waiting for transfers between devices, local(): got = lax.ppermute(sums[key], 'region', move(axis, step))  14.9 us
    ppermute x15, waiting for transfers between devices, local(): held[key] = lax.ppermute(held[source], 'region', move(axis, -step))  11.9 us
    pallas_call x1, Pallas kernels, local(): pl.pallas_call(backward_near_kernel, out_shape=(pltpu.VMEM((ROWS, 256), B...  8.71 us
    ppermute x3, waiting for transfers between devices, local(): lax.ppermute(mine, 'ray', [(i, (i + d) % 4) for i in range(4)])  6.9 us
    ppermute x3, starting transfers between devices, local(): lax.ppermute(mine, 'ray', [(i, (i + d) % 4) for i in range(4)])  6.21 us
    pallas_call x1, Pallas kernels, local(): pl.pallas_call(backward_far_kernel, out_shape=(shape((8, 128), F32), pltp...  5.04 us
  transfers between devices with their start and end apart: 36, of which 14 were waited for; matrix products, arithmetic and copies ran while one was open for 2% of the time, Pallas kernels for 16%

profile of v6, /device:TPU:0, one launch (start us, length us, event | category | flops | bytes accessed | tf_op | source)
XLA Modules:
  0.0 117.6 jit_solution(14054416411381732705)
XLA Ops:
  1.7 2.1 %collective-permute-start.5 = (bf16[528,256]{1,0:T(8,128)(2,1)S(1)}, bf16[528,256]{1,0:T(8,128)(2,1)S(1)}, u32[]{:S(2)}, u32[]{:S(2)}) collective-permute-start(bf16[528,256]{1,0:T(8,128)(2,1)S(1)} %fusion.1.refs_2_), channel_id=1, source_target_pairs={{0,8},{1,9},{2,10},{3,11},{4,12},{5,13},{6,14},{7,15},{8,16},{9,17... | collective-permute-start | bytes 811016 | tf_op jit(solution)/shard_map/ppermute | solution.py:376
  3.8 2.8 %collective-permute-start.3 = (bf16[528,256]{1,0:T(8,128)(2,1)S(1)}, bf16[528,256]{1,0:T(8,128)(2,1)S(1)}, u32[]{:S(2)}, u32[]{:S(2)}) collective-permute-start(bf16[528,256]{1,0:T(8,128)(2,1)S(1)} %fusion.1.refs_2_), channel_id=1, source_target_pairs={{0,6},{1,7},{2,0},{3,1},{4,2},{5,3},{6,4},{7,5},{8,14},{9,15},{10,... | collective-permute-start | bytes 811016 | tf_op jit(solution)/shard_map/ppermute | solution.py:376
  6.6 2.2 %collective-permute-start.2 = (bf16[528,256]{1,0:T(8,128)(2,1)S(1)}, bf16[528,256]{1,0:T(8,128)(2,1)S(1)}, u32[]{:S(2)}, u32[]{:S(2)}) collective-permute-start(bf16[528,256]{1,0:T(8,128)(2,1)S(1)} %fusion.1.refs_2_), channel_id=1, source_target_pairs={{0,24},{1,25},{2,26},{3,27},{4,28},{5,29},{6,30},{7,31},{8,0},{9,1... | collective-permute-start | bytes 811016 | tf_op jit(solution)/shard_map/ppermute | solution.py:376
  8.8 4.3 %collective-permute-done.5.refs_6_ = bf16[528,256]{1,0:T(8,128)(2,1)S(1)} collective-permute-done((bf16[528,256]{1,0:T(8,128)(2,1)S(1)}, bf16[528,256]{1,0:T(8,128)(2,1)S(1)}, u32[]{:S(2)}, u32[]{:S(2)}) %collective-permute-start.5) | collective-permute-done | bytes 270368 | tf_op jit(solution)/shard_map/ppermute | solution.py:376
  13.1 1.5 %collective-permute-start.10 = (bf16[528,256]{1,0:T(8,128)(2,1)S(1)}, bf16[528,256]{1,0:T(8,128)(2,1)S(1)}, u32[]{:S(2)}, u32[]{:S(2)}) collective-permute-start(bf16[528,256]{1,0:T(8,128)(2,1)S(1)} %collective-permute-done.5.refs_6_), channel_id=1, source_target_pairs={{0,2},{1,3},{2,4},{3,5},{4,6},{5,7},{6,0},{7,1},{8,10},{9,11},{10,... | collective-permute-start | bytes 811016 | tf_op jit(solution)/shard_map/ppermute | solution.py:379
  14.6 1.6 %meta.1.own = f32[72,128]{1,0:T(8,128)} custom-call(s32[32]{0:T(128)} %owner.1, s32[1,64]{1,0:T(1,128)} %bitcast.23, s32[4,16]{1,0:T(4,128)} %bitcast.21, f32[3,16]{1,0:T(4,128)} %bitcast.22, bf16[64,128]{1,0:T(8,128)(2,1)} %delta.1), custom_call_target="tpu_custom_call" | custom-call | flops 1500000000 | tf_op jit(solution)/shard_map/meta/pallas_call | solution.py:382
  16.8 1.6 %collective-permute-start.9 = (bf16[528,256]{1,0:T(8,128)(2,1)S(1)}, bf16[528,256]{1,0:T(8,128)(2,1)S(1)}, u32[]{:S(2)}, u32[]{:S(2)}) collective-permute-start(bf16[528,256]{1,0:T(8,128)(2,1)S(1)} %collective-permute-done.3.refs_3_), channel_id=1, source_target_pairs={{0,8},{1,9},{2,10},{3,11},{4,12},{5,13},{6,14},{7,15},{8,16},{9,17... | collective-permute-start | bytes 811016 | tf_op jit(solution)/shard_map/ppermute | solution.py:379
  18.4 1.5 %collective-permute-start.6 = (bf16[528,256]{1,0:T(8,128)(2,1)S(1)}, bf16[528,256]{1,0:T(8,128)(2,1)S(1)}, u32[]{:S(2)}, u32[]{:S(2)}) collective-permute-start(bf16[528,256]{1,0:T(8,128)(2,1)S(1)} %collective-permute-done.3.refs_3_), channel_id=1, source_target_pairs={{0,6},{1,7},{2,0},{3,1},{4,2},{5,3},{6,4},{7,5},{8,14},{9,15},{10,... | collective-permute-start | bytes 811016 | tf_op jit(solution)/shard_map/ppermute | solution.py:379
  19.9 1.6 %collective-permute-start.11 = (bf16[528,256]{1,0:T(8,128)(2,1)S(1)}, bf16[528,256]{1,0:T(8,128)(2,1)S(1)}, u32[]{:S(2)}, u32[]{:S(2)}) collective-permute-start(bf16[528,256]{1,0:T(8,128)(2,1)S(1)} %collective-permute-done.4.refs_5_), channel_id=1, source_target_pairs={{0,24},{1,25},{2,26},{3,27},{4,28},{5,29},{6,30},{7,31},{8,0},{9,1... | collective-permute-start | bytes 811016 | tf_op jit(solution)/shard_map/ppermute | solution.py:379
  21.5 2.5 %collective-permute-done.10.refs_11_ = bf16[528,256]{1,0:T(8,128)(2,1)S(1)} collective-permute-done((bf16[528,256]{1,0:T(8,128)(2,1)S(1)}, bf16[528,256]{1,0:T(8,128)(2,1)S(1)}, u32[]{:S(2)}, u32[]{:S(2)}) %collective-permute-start.10) | collective-permute-done | bytes 270368 | tf_op jit(solution)/shard_map/ppermute | solution.py:379
  24.9 3.5 %plan.1 = (s32[8,128]{1,0:T(8,128)S(1)}, f32[144,128]{1,0:T(8,128)S(1)}, bf16[128,128,256]{2,1,0:T(8,128)(2,1)S(1)}) custom-call(f32[72,128]{1,0:T(8,128)S(1)} %copy-done, f32[72,128]{1,0:T(8,128)S(1)} %collective-permute-done.sib, bf16[64,128,256]{2,1,0:T(8,128)(2,1)} %x_own.1, bf16[64,128,256]{2,1,0:T(8,128)(2,1)} %collective-permute-done.1.x_sib), custom_call_target="tpu_custom_call" | custom-call | flops 3000000000 | tf_op jit(solution)/shard_map/plan/pallas_call | solution.py:391
  32.0 1.7 %collective-permute-start.13 = (bf16[528,256]{1,0:T(8,128)(2,1)S(1)}, bf16[528,256]{1,0:T(8,128)(2,1)S(1)}, u32[]{:S(2)}, u32[]{:S(2)}) collective-permute-start(bf16[528,256]{1,0:T(8,128)(2,1)S(1)} %collective-permute-done.7.refs_8_), channel_id=1, source_target_pairs={{0,6},{1,7},{2,0},{3,1},{4,2},{5,3},{6,4},{7,5},{8,14},{9,15},{10,... | collective-permute-start | bytes 811016 | tf_op jit(solution)/shard_map/ppermute | solution.py:379
  33.8 3.2 %collective-permute-done.8.refs_9_ = bf16[528,256]{1,0:T(8,128)(2,1)S(1)} collective-permute-done((bf16[528,256]{1,0:T(8,128)(2,1)S(1)}, bf16[528,256]{1,0:T(8,128)(2,1)S(1)}, u32[]{:S(2)}, u32[]{:S(2)}) %collective-permute-start.8) | collective-permute-done | bytes 270368 | tf_op jit(solution)/shard_map/ppermute | solution.py:379
  38.1 5.0 %forward_near.1 = (f32[2,384,128]{2,1,0:T(8,128)S(1)}, bf16[11,528,256]{2,1,0:T(8,128)(2,1)S(1)}, bf16[48,256,256]{2,1,0:T(8,128)(2,1)S(1)}, bf16[48,256,256]{2,1,0:T(8,128)(2,1)S(1)}) custom-call(s32[8,128]{1,0:T(8,128)S(1)} %get-tuple-element.37.refs_0_, bf16[128,128,256]{2,1,0:T(8,128)(2,1)S(1)} %get-tuple-element.39.refs_1_.refs_2_.refs_4_, ...), custom_call_target="tpu_custom_call" | custom-call | flops 4499999744 | tf_op jit(solution)/shard_map/forward_near/pallas_call | solution.py:405
  43.5 3.1 %forward_far.1 = (f32[8,128]{1,0:T(8,128)S(1)}, f32[6,72,256]{2,1,0:T(8,128)S(1)}, bf16[5,528,256]{2,1,0:T(8,128)(2,1)S(1)}, bf16[24,256,256]{2,1,0:T(8,128)(2,1)S(1)}, bf16[24,256,256]{2,1,0:T(8,128)(2,1)S(1)}) custom-call(s32[8,128]{1,0:T(8,128)S(1)} %get-tuple-element.37.refs_0_, f32[144,128]{1,0:T(8,128)S(1)} %get-tuple-element.38.refs_1_, ...), custom_call_target="tpu_custom_call" | custom-call | flops 3000000000 | tf_op jit(solution)/shard_map/forward_far/pallas_call | solution.py:420
  47.9 5.0 %backward_far.1 = (f32[8,128]{1,0:T(8,128)S(1)}, f32[2,576,128]{2,1,0:T(8,128)S(1)}, bf16[528,256]{1,0:T(8,128)(2,1)S(1)}, bf16[528,256]{1,0:T(8,128)(2,1)S(1)},...) custom-call(s32[8,128]{1,0:T(8,128)S(1)} %get-tuple-element.37.refs_0_, ...), custom_call_target="tpu_custom_call" | custom-call | flops 5600000000 | tf_op jit(solution)/shard_map/backward_far/pallas_call | solution.py:444
  52.9 2.8 %collective-permute-start.19 = (bf16[528,256]{1,0:T(8,128)(2,1)S(1)}, bf16[528,256]{1,0:T(8,128)(2,1)S(1)}, u32[]{:S(2)}, u32[]{:S(2)}) collective-permute-start(bf16[528,256]{1,0:T(8,128)(2,1)S(1)} %get-tuple-element.56), channel_id=1, source_target_pairs={{0,4},{1,5},{2,6},{3,7},{4,0},{5,1},{6,2},{7,3},{8,12},{9,13},{10,... | collective-permute-start | bytes 811016 | tf_op jit(solution)/shard_map/ppermute | solution.py:469
  57.7 8.7 %backward_near.1 = (bf16[528,256]{1,0:T(8,128)(2,1)S(1)}, bf16[528,256]{1,0:T(8,128)(2,1)S(1)}, bf16[528,256]{1,0:T(8,128)(2,1)S(1)}, bf16[528,256]{1,0:T(8,128)...) custom-call(s32[8,128]{1,0:T(8,128)S(1)} %get-tuple-element.37.refs_, ...), custom_call_target="tpu_custom_call" | custom-call | flops 7600000000 | tf_op jit(solution)/shard_map/backward_near/pallas_call | solution.py:455
  67.0 2.6 %collective-permute-start.18 = (bf16[528,256]{1,0:T(8,128)(2,1)S(1)}, bf16[528,256]{1,0:T(8,128)(2,1)S(1)}, u32[]{:S(2)}, u32[]{:S(2)}) collective-permute-start(bf16[528,256]{1,0:T(8,128)(2,1)S(1)} %get-tuple-element.54), channel_id=1, source_target_pairs={{0,6},{1,7},{2,0},{3,1},{4,2},{5,3},{6,4},{7,5},{8,14},{9,15},{10,... | collective-permute-start | bytes 811016 | tf_op jit(solution)/shard_map/ppermute | solution.py:469
  69.6 3.8 %collective-permute-start.29 = (bf16[528,256]{1,0:T(8,128)(2,1)S(1)}, bf16[528,256]{1,0:T(8,128)(2,1)S(1)}, u32[]{:S(2)}, u32[]{:S(2)}) collective-permute-start(bf16[528,256]{1,0:T(8,128)(2,1)S(1)} %get-tuple-element.66), channel_id=1, source_target_pairs={{0,24},{1,25},{2,26},{3,27},{4,28},{5,29},{6,30},{7,31},{8,0},{9,1... | collective-permute-start | bytes 811016 | tf_op jit(solution)/shard_map/ppermute | solution.py:469
  74.5 2.7 %collective-permute-start.28 = (bf16[528,256]{1,0:T(8,128)(2,1)S(1)}, bf16[528,256]{1,0:T(8,128)(2,1)S(1)}, u32[]{:S(2)}, u32[]{:S(2)}) collective-permute-start(bf16[528,256]{1,0:T(8,128)(2,1)S(1)} %get-tuple-element.64), channel_id=1, source_target_pairs={{0,24},{1,25},{2,26},{3,27},{4,28},{5,29},{6,30},{7,31},{8,0},{9,1... | collective-permute-start | bytes 811016 | tf_op jit(solution)/shard_map/ppermute | solution.py:469
  77.3 3.1 %collective-permute-done.29 = bf16[528,256]{1,0:T(8,128)(2,1)S(1)} collective-permute-done((bf16[528,256]{1,0:T(8,128)(2,1)S(1)}, bf16[528,256]{1,0:T(8,128)(2,1)S(1)}, u32[]{:S(2)}, u32[]{:S(2)}) %collective-permute-start.29) | collective-permute-done | bytes 270368 | tf_op jit(solution)/shard_map/ppermute | solution.py:469
  80.3 2.7 %collective-permute-start.25 = (bf16[528,256]{1,0:T(8,128)(2,1)S(1)}, bf16[528,256]{1,0:T(8,128)(2,1)S(1)}, u32[]{:S(2)}, u32[]{:S(2)}) collective-permute-start(bf16[528,256]{1,0:T(8,128)(2,1)S(1)} %add_convert_fusion.8), channel_id=1, source_target_pairs={{0,6},{1,7},{2,0},{3,1},{4,2},{5,3},{6,4},{7,5},{8,14},{9,15},{10,... | collective-permute-start | bytes 811016 | tf_op jit(solution)/shard_map/ppermute | solution.py:469
  83.0 3.0 %collective-permute-start.22 = (bf16[528,256]{1,0:T(8,128)(2,1)S(1)}, bf16[528,256]{1,0:T(8,128)(2,1)S(1)}, u32[]{:S(2)}, u32[]{:S(2)}) collective-permute-start(bf16[528,256]{1,0:T(8,128)(2,1)S(1)} %add_convert_fusion.11), channel_id=1, source_target_pairs={{0,24},{1,25},{2,26},{3,27},{4,28},{5,29},{6,30},{7,31},{8,0},{9,1... | collective-permute-start | bytes 811016 | tf_op jit(solution)/shard_map/ppermute | solution.py:469
  86.4 3.6 %collective-permute-done.22 = bf16[528,256]{1,0:T(8,128)(2,1)S(1)} collective-permute-done((bf16[528,256]{1,0:T(8,128)(2,1)S(1)}, bf16[528,256]{1,0:T(8,128)(2,1)S(1)}, u32[]{:S(2)}, u32[]{:S(2)}) %collective-permute-start.22) | collective-permute-done | bytes 270368 | tf_op jit(solution)/shard_map/ppermute | solution.py:469
  90.2 3.8 %collective-permute-start.23 = (bf16[528,256]{1,0:T(8,128)(2,1)S(1)}, bf16[528,256]{1,0:T(8,128)(2,1)S(1)}, u32[]{:S(2)}, u32[]{:S(2)}) collective-permute-start(bf16[528,256]{1,0:T(8,128)(2,1)S(1)} %add_convert_fusion.10), channel_id=1, source_target_pairs={{0,24},{1,25},{2,26},{3,27},{4,28},{5,29},{6,30},{7,31},{8,0},{9,1... | collective-permute-start | bytes 811016 | tf_op jit(solution)/shard_map/ppermute | solution.py:469
  94.8 3.1 %collective-permute-done.23 = bf16[528,256]{1,0:T(8,128)(2,1)S(1)} collective-permute-done((bf16[528,256]{1,0:T(8,128)(2,1)S(1)}, bf16[528,256]{1,0:T(8,128)(2,1)S(1)}, u32[]{:S(2)}, u32[]{:S(2)}) %collective-permute-start.23) | collective-permute-done | bytes 270368 | tf_op jit(solution)/shard_map/ppermute | solution.py:469
  97.9 4.2 %collective-permute-done.32 = bf16[528,256]{1,0:T(8,128)(2,1)S(1)} collective-permute-done((bf16[528,256]{1,0:T(8,128)(2,1)S(1)}, bf16[528,256]{1,0:T(8,128)(2,1)S(1)}, u32[]{:S(2)}, u32[]{:S(2)}) %collective-permute-start.32) | collective-permute-done | bytes 270368 | tf_op jit(solution)/shard_map/ppermute | solution.py:469
  102.3 4.2 %collective-permute-start.35 = (bf16[528,256]{1,0:T(8,128)(2,1)S(1)}, bf16[528,256]{1,0:T(8,128)(2,1)S(1)}, u32[]{:S(2)}, u32[]{:S(2)}) collective-permute-start(bf16[528,256]{1,0:T(8,128)(2,1)S(1)} %add_convert_fusion), channel_id=1, source_target_pairs={{0,64},{32,96},{64,0},{96,32},{1,65},{33,97},{65,1},{97,33},{2,66}... | collective-permute-start | bytes 811016 | tf_op jit(solution)/shard_map/ppermute | solution.py:474
  106.7 1.9 %collective-permute-start.33 = (bf16[528,256]{1,0:T(8,128)(2,1)S(1)}, bf16[528,256]{1,0:T(8,128)(2,1)S(1)}, u32[]{:S(2)}, u32[]{:S(2)}) collective-permute-start(bf16[528,256]{1,0:T(8,128)(2,1)S(1)} %add_convert_fusion), channel_id=1, source_target_pairs={{0,32},{32,64},{64,96},{96,0},{1,33},{33,65},{65,97},{97,1},{2,34}... | collective-permute-start | bytes 811016 | tf_op jit(solution)/shard_map/ppermute | solution.py:474
  109.2 3.6 %collective-permute-done.35 = bf16[528,256]{1,0:T(8,128)(2,1)S(1)} collective-permute-done((bf16[528,256]{1,0:T(8,128)(2,1)S(1)}, bf16[528,256]{1,0:T(8,128)(2,1)S(1)}, u32[]{:S(2)}, u32[]{:S(2)}) %collective-permute-start.35) | collective-permute-done | bytes 270368 | tf_op jit(solution)/shard_map/ppermute | solution.py:474
  112.8 3.2 %collective-permute-done.34 = bf16[528,256]{1,0:T(8,128)(2,1)S(1)} collective-permute-done((bf16[528,256]{1,0:T(8,128)(2,1)S(1)}, bf16[528,256]{1,0:T(8,128)(2,1)S(1)}, u32[]{:S(2)}, u32[]{:S(2)}) %collective-permute-start.34) | collective-permute-done | bytes 270368 | tf_op jit(solution)/shard_map/ppermute | solution.py:474
  (59 shorter events, 16.7 us)
Async XLA Ops:
  0.6 16.2 %collective-permute-start.1 = (bf16[64,128,256]{2,1,0:T(8,128)(2,1)}, bf16[64,128,256]{2,1,0:T(8,128)(2,1)}, u32[]{:S(2)}, u32[]{:S(2)}) collective-permute-start(bf16[64,128,256]{2,1,0:T(8,128)(2,1)} %x_own.1), channel_id=1, source_target_pairs={{0,1},{1,0},{2,3},{3,2},{4,5},{5,4},{6,7},{7,6},{8,9},{9,8},{10,11... | collective-permute-start | bytes 12582920 | tf_op jit(solution)/shard_map/ppermute | solution.py:370
  1.7 11.3 %collective-permute-start.5 = (bf16[528,256]{1,0:T(8,128)(2,1)S(1)}, bf16[528,256]{1,0:T(8,128)(2,1)S(1)}, u32[]{:S(2)}, u32[]{:S(2)}) collective-permute-start(bf16[528,256]{1,0:T(8,128)(2,1)S(1)} %fusion.1.refs_2_), channel_id=1, source_target_pairs={{0,8},{1,9},{2,10},{3,11},{4,12},{5,13},{6,14},{7,15},{8,16},{9,17... | collective-permute-start | bytes 811016 | tf_op jit(solution)/shard_map/ppermute | solution.py:376
  3.8 12.3 %collective-permute-start.3 = (bf16[528,256]{1,0:T(8,128)(2,1)S(1)}, bf16[528,256]{1,0:T(8,128)(2,1)S(1)}, u32[]{:S(2)}, u32[]{:S(2)}) collective-permute-start(bf16[528,256]{1,0:T(8,128)(2,1)S(1)} %fusion.1.refs_2_), channel_id=1, source_target_pairs={{0,6},{1,7},{2,0},{3,1},{4,2},{5,3},{6,4},{7,5},{8,14},{9,15},{10,... | collective-permute-start | bytes 811016 | tf_op jit(solution)/shard_map/ppermute | solution.py:376
  6.6 9.6 %collective-permute-start.2 = (bf16[528,256]{1,0:T(8,128)(2,1)S(1)}, bf16[528,256]{1,0:T(8,128)(2,1)S(1)}, u32[]{:S(2)}, u32[]{:S(2)}) collective-permute-start(bf16[528,256]{1,0:T(8,128)(2,1)S(1)} %fusion.1.refs_2_), channel_id=1, source_target_pairs={{0,24},{1,25},{2,26},{3,27},{4,28},{5,29},{6,30},{7,31},{8,0},{9,1... | collective-permute-start | bytes 811016 | tf_op jit(solution)/shard_map/ppermute | solution.py:376
  8.8 11.2 %collective-permute-start.4 = (bf16[528,256]{1,0:T(8,128)(2,1)S(1)}, bf16[528,256]{1,0:T(8,128)(2,1)S(1)}, u32[]{:S(2)}, u32[]{:S(2)}) collective-permute-start(bf16[528,256]{1,0:T(8,128)(2,1)S(1)} %fusion.1.refs_2_), channel_id=1, source_target_pairs={{0,2},{1,3},{2,4},{3,5},{4,6},{5,7},{6,0},{7,1},{8,10},{9,11},{10,... | collective-permute-start | bytes 811016 | tf_op jit(solution)/shard_map/ppermute | solution.py:376
  13.1 11.0 %collective-permute-start.10 = (bf16[528,256]{1,0:T(8,128)(2,1)S(1)}, bf16[528,256]{1,0:T(8,128)(2,1)S(1)}, u32[]{:S(2)}, u32[]{:S(2)}) collective-permute-start(bf16[528,256]{1,0:T(8,128)(2,1)S(1)} %collective-permute-done.5.refs_6_), channel_id=1, source_target_pairs={{0,2},{1,3},{2,4},{3,5},{4,6},{5,7},{6,0},{7,1},{8,10},{9,11},{10,... | collective-permute-start | bytes 811016 | tf_op jit(solution)/shard_map/ppermute | solution.py:379
  16.1 12.2 %collective-permute-start.7 = (bf16[528,256]{1,0:T(8,128)(2,1)S(1)}, bf16[528,256]{1,0:T(8,128)(2,1)S(1)}, u32[]{:S(2)}, u32[]{:S(2)}) collective-permute-start(bf16[528,256]{1,0:T(8,128)(2,1)S(1)} %collective-permute-done.5.refs_6_), channel_id=1, source_target_pairs={{0,8},{1,9},{2,10},{3,11},{4,12},{5,13},{6,14},{7,15},{8,16},{9,17... | collective-permute-start | bytes 811016 | tf_op jit(solution)/shard_map/ppermute | solution.py:379
  16.8 15.2 %collective-permute-start.9 = (bf16[528,256]{1,0:T(8,128)(2,1)S(1)}, bf16[528,256]{1,0:T(8,128)(2,1)S(1)}, u32[]{:S(2)}, u32[]{:S(2)}) collective-permute-start(bf16[528,256]{1,0:T(8,128)(2,1)S(1)} %collective-permute-done.3.refs_3_), channel_id=1, source_target_pairs={{0,8},{1,9},{2,10},{3,11},{4,12},{5,13},{6,14},{7,15},{8,16},{9,17... | collective-permute-start | bytes 811016 | tf_op jit(solution)/shard_map/ppermute | solution.py:379
  18.4 15.4 %collective-permute-start.6 = (bf16[528,256]{1,0:T(8,128)(2,1)S(1)}, bf16[528,256]{1,0:T(8,128)(2,1)S(1)}, u32[]{:S(2)}, u32[]{:S(2)}) collective-permute-start(bf16[528,256]{1,0:T(8,128)(2,1)S(1)} %collective-permute-done.3.refs_3_), channel_id=1, source_target_pairs={{0,6},{1,7},{2,0},{3,1},{4,2},{5,3},{6,4},{7,5},{8,14},{9,15},{10,... | collective-permute-start | bytes 811016 | tf_op jit(solution)/shard_map/ppermute | solution.py:379
  19.9 9.6 %collective-permute-start.11 = (bf16[528,256]{1,0:T(8,128)(2,1)S(1)}, bf16[528,256]{1,0:T(8,128)(2,1)S(1)}, u32[]{:S(2)}, u32[]{:S(2)}) collective-permute-start(bf16[528,256]{1,0:T(8,128)(2,1)S(1)} %collective-permute-done.4.refs_5_), channel_id=1, source_target_pairs={{0,24},{1,25},{2,26},{3,27},{4,28},{5,29},{6,30},{7,31},{8,0},{9,1... | collective-permute-start | bytes 811016 | tf_op jit(solution)/shard_map/ppermute | solution.py:379
  24.1 12.9 %collective-permute-start.8 = (bf16[528,256]{1,0:T(8,128)(2,1)S(1)}, bf16[528,256]{1,0:T(8,128)(2,1)S(1)}, u32[]{:S(2)}, u32[]{:S(2)}) collective-permute-start(bf16[528,256]{1,0:T(8,128)(2,1)S(1)} %collective-permute-done.2.refs_4_), channel_id=1, source_target_pairs={{0,6},{1,7},{2,0},{3,1},{4,2},{5,3},{6,4},{7,5},{8,14},{9,15},{10,... | collective-permute-start | bytes 811016 | tf_op jit(solution)/shard_map/ppermute | solution.py:379
  28.4 14.7 %collective-permute-start.16 = (bf16[528,256]{1,0:T(8,128)(2,1)S(1)}, bf16[528,256]{1,0:T(8,128)(2,1)S(1)}, u32[]{:S(2)}, u32[]{:S(2)}) collective-permute-start(bf16[528,256]{1,0:T(8,128)(2,1)S(1)} %collective-permute-done.7.refs_8_), channel_id=1, source_target_pairs={{0,4},{1,5},{2,6},{3,7},{4,0},{5,1},{6,2},{7,3},{8,12},{9,13},{10,... | collective-permute-start | bytes 811016 | tf_op jit(solution)/shard_map/ppermute | solution.py:379
  29.6 13.6 %collective-permute-start.15 = (bf16[528,256]{1,0:T(8,128)(2,1)S(1)}, bf16[528,256]{1,0:T(8,128)(2,1)S(1)}, u32[]{:S(2)}, u32[]{:S(2)}) collective-permute-start(bf16[528,256]{1,0:T(8,128)(2,1)S(1)} %collective-permute-done.7.refs_8_), channel_id=1, source_target_pairs={{0,2},{1,3},{2,4},{3,5},{4,6},{5,7},{6,0},{7,1},{8,10},{9,11},{10,... | collective-permute-start | bytes 811016 | tf_op jit(solution)/shard_map/ppermute | solution.py:379
  32.0 11.5 %collective-permute-start.13 = (bf16[528,256]{1,0:T(8,128)(2,1)S(1)}, bf16[528,256]{1,0:T(8,128)(2,1)S(1)}, u32[]{:S(2)}, u32[]{:S(2)}) collective-permute-start(bf16[528,256]{1,0:T(8,128)(2,1)S(1)} %collective-permute-done.7.refs_8_), channel_id=1, source_target_pairs={{0,6},{1,7},{2,0},{3,1},{4,2},{5,3},{6,4},{7,5},{8,14},{9,15},{10,... | collective-permute-start | bytes 811016 | tf_op jit(solution)/shard_map/ppermute | solution.py:379
  33.8 9.7 %collective-permute-start.14 = (bf16[528,256]{1,0:T(8,128)(2,1)S(1)}, bf16[528,256]{1,0:T(8,128)(2,1)S(1)}, u32[]{:S(2)}, u32[]{:S(2)}) collective-permute-start(bf16[528,256]{1,0:T(8,128)(2,1)S(1)} %collective-permute-done.6.refs_7_), channel_id=1, source_target_pairs={{0,8},{1,9},{2,10},{3,11},{4,12},{5,13},{6,14},{7,15},{8,16},{9,17... | collective-permute-start | bytes 811016 | tf_op jit(solution)/shard_map/ppermute | solution.py:379
  52.9 16.7 %collective-permute-start.19 = (bf16[528,256]{1,0:T(8,128)(2,1)S(1)}, bf16[528,256]{1,0:T(8,128)(2,1)S(1)}, u32[]{:S(2)}, u32[]{:S(2)}) collective-permute-start(bf16[528,256]{1,0:T(8,128)(2,1)S(1)} %get-tuple-element.56), channel_id=1, source_target_pairs={{0,4},{1,5},{2,6},{3,7},{4,0},{5,1},{6,2},{7,3},{8,12},{9,13},{10,... | collective-permute-start | bytes 811016 | tf_op jit(solution)/shard_map/ppermute | solution.py:469
  55.7 13.9 %collective-permute-start.20 = (bf16[528,256]{1,0:T(8,128)(2,1)S(1)}, bf16[528,256]{1,0:T(8,128)(2,1)S(1)}, u32[]{:S(2)}, u32[]{:S(2)}) collective-permute-start(bf16[528,256]{1,0:T(8,128)(2,1)S(1)} %get-tuple-element.57), channel_id=1, source_target_pairs={{0,6},{1,7},{2,0},{3,1},{4,2},{5,3},{6,4},{7,5},{8,14},{9,15},{10,... | collective-permute-start | bytes 811016 | tf_op jit(solution)/shard_map/ppermute | solution.py:469
  56.3 17.1 %collective-permute-start.21 = (bf16[528,256]{1,0:T(8,128)(2,1)S(1)}, bf16[528,256]{1,0:T(8,128)(2,1)S(1)}, u32[]{:S(2)}, u32[]{:S(2)}) collective-permute-start(bf16[528,256]{1,0:T(8,128)(2,1)S(1)} %get-tuple-element.58), channel_id=1, source_target_pairs={{0,2},{1,3},{2,4},{3,5},{4,6},{5,7},{6,0},{7,1},{8,10},{9,11},{10,... | collective-permute-start | bytes 811016 | tf_op jit(solution)/shard_map/ppermute | solution.py:469
  66.5 8.1 %collective-permute-start.24 = (bf16[528,256]{1,0:T(8,128)(2,1)S(1)}, bf16[528,256]{1,0:T(8,128)(2,1)S(1)}, u32[]{:S(2)}, u32[]{:S(2)}) collective-permute-start(bf16[528,256]{1,0:T(8,128)(2,1)S(1)} %get-tuple-element.60), channel_id=1, source_target_pairs={{0,8},{1,9},{2,10},{3,11},{4,12},{5,13},{6,14},{7,15},{8,16},{9,17... | collective-permute-start | bytes 811016 | tf_op jit(solution)/shard_map/ppermute | solution.py:469
  67.0 19.4 %collective-permute-start.18 = (bf16[528,256]{1,0:T(8,128)(2,1)S(1)}, bf16[528,256]{1,0:T(8,128)(2,1)S(1)}, u32[]{:S(2)}, u32[]{:S(2)}) collective-permute-start(bf16[528,256]{1,0:T(8,128)(2,1)S(1)} %get-tuple-element.54), channel_id=1, source_target_pairs={{0,6},{1,7},{2,0},{3,1},{4,2},{5,3},{6,4},{7,5},{8,14},{9,15},{10,... | collective-permute-start | bytes 811016 | tf_op jit(solution)/shard_map/ppermute | solution.py:469
  69.6 16.6 %collective-permute-start.26 = (bf16[528,256]{1,0:T(8,128)(2,1)S(1)}, bf16[528,256]{1,0:T(8,128)(2,1)S(1)}, u32[]{:S(2)}, u32[]{:S(2)}) collective-permute-start(bf16[528,256]{1,0:T(8,128)(2,1)S(1)} %get-tuple-element.62), channel_id=1, source_target_pairs={{0,2},{1,3},{2,4},{3,5},{4,6},{5,7},{6,0},{7,1},{8,10},{9,11},{10,... | collective-permute-start | bytes 811016 | tf_op jit(solution)/shard_map/ppermute | solution.py:469
  69.6 10.7 %collective-permute-start.29 = (bf16[528,256]{1,0:T(8,128)(2,1)S(1)}, bf16[528,256]{1,0:T(8,128)(2,1)S(1)}, u32[]{:S(2)}, u32[]{:S(2)}) collective-permute-start(bf16[528,256]{1,0:T(8,128)(2,1)S(1)} %get-tuple-element.66), channel_id=1, source_target_pairs={{0,24},{1,25},{2,26},{3,27},{4,28},{5,29},{6,30},{7,31},{8,0},{9,1... | collective-permute-start | bytes 811016 | tf_op jit(solution)/shard_map/ppermute | solution.py:469
  73.4 9.6 %collective-permute-start.30 = (bf16[528,256]{1,0:T(8,128)(2,1)S(1)}, bf16[528,256]{1,0:T(8,128)(2,1)S(1)}, u32[]{:S(2)}, u32[]{:S(2)}) collective-permute-start(bf16[528,256]{1,0:T(8,128)(2,1)S(1)} %get-tuple-element.67), channel_id=1, source_target_pairs={{0,8},{1,9},{2,10},{3,11},{4,12},{5,13},{6,14},{7,15},{8,16},{9,17... | collective-permute-start | bytes 811016 | tf_op jit(solution)/shard_map/ppermute | solution.py:469
  74.5 19.4 %collective-permute-start.28 = (bf16[528,256]{1,0:T(8,128)(2,1)S(1)}, bf16[528,256]{1,0:T(8,128)(2,1)S(1)}, u32[]{:S(2)}, u32[]{:S(2)}) collective-permute-start(bf16[528,256]{1,0:T(8,128)(2,1)S(1)} %get-tuple-element.64), channel_id=1, source_target_pairs={{0,24},{1,25},{2,26},{3,27},{4,28},{5,29},{6,30},{7,31},{8,0},{9,1... | collective-permute-start | bytes 811016 | tf_op jit(solution)/shard_map/ppermute | solution.py:469
  80.3 14.5 %collective-permute-start.25 = (bf16[528,256]{1,0:T(8,128)(2,1)S(1)}, bf16[528,256]{1,0:T(8,128)(2,1)S(1)}, u32[]{:S(2)}, u32[]{:S(2)}) collective-permute-start(bf16[528,256]{1,0:T(8,128)(2,1)S(1)} %add_convert_fusion.8), channel_id=1, source_target_pairs={{0,6},{1,7},{2,0},{3,1},{4,2},{5,3},{6,4},{7,5},{8,14},{9,15},{10,... | collective-permute-start | bytes 811016 | tf_op jit(solution)/shard_map/ppermute | solution.py:469
  86.2 7.7 %collective-permute-start.31 = (bf16[528,256]{1,0:T(8,128)(2,1)S(1)}, bf16[528,256]{1,0:T(8,128)(2,1)S(1)}, u32[]{:S(2)}, u32[]{:S(2)}) collective-permute-start(bf16[528,256]{1,0:T(8,128)(2,1)S(1)} %add_convert_fusion.2), channel_id=1, source_target_pairs={{0,2},{1,3},{2,4},{3,5},{4,6},{5,7},{6,0},{7,1},{8,10},{9,11},{10,... | collective-permute-start | bytes 811016 | tf_op jit(solution)/shard_map/ppermute | solution.py:469
  86.4 8.4 %collective-permute-start.27 = (bf16[528,256]{1,0:T(8,128)(2,1)S(1)}, bf16[528,256]{1,0:T(8,128)(2,1)S(1)}, u32[]{:S(2)}, u32[]{:S(2)}) collective-permute-start(bf16[528,256]{1,0:T(8,128)(2,1)S(1)} %add_convert_fusion.6), channel_id=1, source_target_pairs={{0,8},{1,9},{2,10},{3,11},{4,12},{5,13},{6,14},{7,15},{8,16},{9,17... | collective-permute-start | bytes 811016 | tf_op jit(solution)/shard_map/ppermute | solution.py:469
  90.2 7.7 %collective-permute-start.23 = (bf16[528,256]{1,0:T(8,128)(2,1)S(1)}, bf16[528,256]{1,0:T(8,128)(2,1)S(1)}, u32[]{:S(2)}, u32[]{:S(2)}) collective-permute-start(bf16[528,256]{1,0:T(8,128)(2,1)S(1)} %add_convert_fusion.10), channel_id=1, source_target_pairs={{0,24},{1,25},{2,26},{3,27},{4,28},{5,29},{6,30},{7,31},{8,0},{9,1... | collective-permute-start | bytes 811016 | tf_op jit(solution)/shard_map/ppermute | solution.py:469
  94.0 8.1 %collective-permute-start.32 = (bf16[528,256]{1,0:T(8,128)(2,1)S(1)}, bf16[528,256]{1,0:T(8,128)(2,1)S(1)}, u32[]{:S(2)}, u32[]{:S(2)}) collective-permute-start(bf16[528,256]{1,0:T(8,128)(2,1)S(1)} %add_convert_fusion.1), channel_id=1, source_target_pairs={{0,2},{1,3},{2,4},{3,5},{4,6},{5,7},{6,0},{7,1},{8,10},{9,11},{10,... | collective-permute-start | bytes 811016 | tf_op jit(solution)/shard_map/ppermute | solution.py:469
  102.3 10.4 %collective-permute-start.35 = (bf16[528,256]{1,0:T(8,128)(2,1)S(1)}, bf16[528,256]{1,0:T(8,128)(2,1)S(1)}, u32[]{:S(2)}, u32[]{:S(2)}) collective-permute-start(bf16[528,256]{1,0:T(8,128)(2,1)S(1)} %add_convert_fusion), channel_id=1, source_target_pairs={{0,64},{32,96},{64,0},{96,32},{1,65},{33,97},{65,1},{97,33},{2,66}... | collective-permute-start | bytes 811016 | tf_op jit(solution)/shard_map/ppermute | solution.py:474
  106.5 9.5 %collective-permute-start.34 = (bf16[528,256]{1,0:T(8,128)(2,1)S(1)}, bf16[528,256]{1,0:T(8,128)(2,1)S(1)}, u32[]{:S(2)}, u32[]{:S(2)}) collective-permute-start(bf16[528,256]{1,0:T(8,128)(2,1)S(1)} %add_convert_fusion), channel_id=1, source_target_pairs={{0,96},{32,0},{64,32},{96,64},{1,97},{33,1},{65,33},{97,65},{2,98}... | collective-permute-start | bytes 811016 | tf_op jit(solution)/shard_map/ppermute | solution.py:474
  106.7 9.4 %collective-permute-start.33 = (bf16[528,256]{1,0:T(8,128)(2,1)S(1)}, bf16[528,256]{1,0:T(8,128)(2,1)S(1)}, u32[]{:S(2)}, u32[]{:S(2)}) collective-permute-start(bf16[528,256]{1,0:T(8,128)(2,1)S(1)} %add_convert_fusion), channel_id=1, source_target_pairs={{0,32},{32,64},{64,96},{96,0},{1,33},{33,65},{65,97},{97,1},{2,34}... | collective-permute-start | bytes 811016 | tf_op jit(solution)/shard_map/ppermute | solution.py:474
  (5 other events, 17.9 us)

commit v7 on v6

--- a/solution.py
+++ b/solution.py
@@ -38,7 +38,7 @@
 NEAR = ((0, 0), (0, 1), (1, 0), (0, 3), (3, 0), (0, 2), (2, 0), (1, 1), (3, 1), (3, 3), (1, 3))
 FAR = ((1, 2), (2, 1), (3, 2), (2, 3), (2, 2))
 SLOTS = NEAR + FAR
-NN, NF = len(NEAR), len(FAR)
+NN, NF, NT = len(NEAR), len(FAR), 7
 
 
 def move(axis, step):
@@ -283,25 +283,29 @@
             d_col = weight * col[c] * rgb[c] * (1.0 - rgb[c])
             dr[h, pl.ds(c + 1, NP, stride=8), :] = d_col
 
-    gradients(table, dr, xa, wv, h1, h2, grads, accs, NN, NA, table[5, 0])
-
-
-def backward_near_kernel(*refs):
-    table, dr, xa, wv, h1, h2 = refs[:6]
-    grads = refs[6 : 6 + NN]
-    gradients(table, dr, xa, wv, h1, h2, grads, refs[6 + NN :], 0, 0, table[4, 0])
-
-
-def gradients(table, dr, xa, wv, h1, h2, grads, accs, first, base, total):
+    gradients(table, dr, xa, wv, h1, h2, grads, accs, NN, NA, 0, table[5, 0], 0)
+
+
+def backward_leaf_kernel(*refs):
+    grads, accs = refs[6 : 6 + NN - NT], refs[6 + NN - NT :]
+    gradients(*refs[:6], grads, accs, 0, 0, refs[0][2, NT], refs[0][4, 0], NT)
+
+
+def backward_trunk_kernel(*refs):
+    grads, accs = refs[6 : 6 + NT], refs[6 + NT :]
+    gradients(*refs[:6], grads, accs, 0, 0, 0, refs[0][2, NT], 0)
+
+
+def gradients(table, dr, xa, wv, h1, h2, grads, accs, first, base, begin, end, low):
     acc1, acc2, acc3 = accs
     for s in range(len(grads)):
 
-        @pl.when(table[3, first + s] == 0)
+        @pl.when(table[3, first + low + s] == 0)
         def _():
             grads[s][...] = jnp.zeros((ROWS, 256), BF16)
 
     def step(t, _):
-        ids = [G * t + g for g in range(G)]
+        ids = [begin + G * t + g for g in range(G)]
         slots = [table[1, base + i] - first for i in ids]
         tn, nt = (((0,), (0,)), ((), ())), (((1,), (1,)), ((), ()))
         raws = []
@@ -329,17 +333,18 @@
             lax.dot_general(samples(table, xa, base + i), d, tn, preferred_element_type=F32)
             for i, d in zip(ids, d_one)
         ]
-        for g, s in enumerate(slots):
-            begins = base + ids[g] == table[2, first + s]
+        for g, slot in enumerate(slots):
+            begins = base + ids[g] == table[2, first + slot]
+            s = slot - low
             acc1[s] = jnp.where(begins, 0.0, acc1[s]) + g1[g]
             acc2[s] = jnp.where(begins, 0.0, acc2[s]) + g2[g]
             acc3[s] = jnp.where(begins, 0.0, acc3[s]) + g3[g]
         return 0
 
-    lax.fori_loop(0, (total + G - 1) // G, step, 0)
+    lax.fori_loop(0, (end - begin + G - 1) // G, step, 0)
     for s in range(len(grads)):
 
-        @pl.when(table[3, first + s] > 0)
+        @pl.when(table[3, first + low + s] > 0)
         def _():
             grads[s][0:256] = acc1[s].astype(BF16)
             grads[s][256:512] = acc2[s].astype(BF16)
@@ -452,17 +457,27 @@
         cost_estimate=cost(5.6),
         name="backward_far",
     )(table, info, res, res_sib, xa, saved, *far_side)
-    near_grads = pl.pallas_call(
-        backward_near_kernel,
-        out_shape=(pltpu.VMEM((ROWS, 256), BF16),) * NN,
+    leaf_grads = pl.pallas_call(
+        backward_leaf_kernel,
+        out_shape=(pltpu.VMEM((ROWS, 256), BF16),) * (NN - NT),
         in_specs=[smem] + [vmem] * 5,
-        out_specs=(vmem,) * NN,
+        out_specs=(vmem,) * (NN - NT),
+        scratch_shapes=accs(NN - NT),
+        compiler_params=limit,
+        cost_estimate=cost(3),
+        name="backward_leaf",
+    )(table, dr, xa, *near)
+    trunk_grads = pl.pallas_call(
+        backward_trunk_kernel,
+        out_shape=(pltpu.VMEM((ROWS, 256), BF16),) * NT,
+        in_specs=[smem] + [vmem] * 5,
+        out_specs=(vmem,) * NT,
         scratch_shapes=accs(NN),
         compiler_params=limit,
-        cost_estimate=cost(7.6),
-        name="backward_near",
+        cost_estimate=cost(5),
+        name="backward_trunk",
     )(table, dr, xa, *near)
-    grads = list(near_grads) + far_grads
+    grads = list(trunk_grads) + list(leaf_grads) + far_grads
 
     sums = dict(zip(SLOTS, grads))
     for key, source, axis, step in reversed(TREE):

time: 118 us -> 118 us (level)
  waiting for transfers between devices: 34.9 us -> 39.1 us
  starting transfers between devices: 50.2 us -> 46.5 us
  Pallas kernels: 26.9 us -> 25.4 us
    ppermute x3, waiting for transfers between devices: 6.9 us -> 9.16 us  [local(): lax.ppermute(mine, 'ray', [(i, (i + d) % 4) for i in range(4)])]
    ppermute x3, starting transfers between devices: 6.21 us -> 4.21 us  [local(): lax.ppermute(mine, 'ray', [(i, (i + d) % 4) for i in range(4)])]
    ppermute x15, starting transfers between devices: 24.8 us -> 23.2 us  [local(): got = lax.ppermute(sums[key], 'region', move(axis, step))]
    pallas_call x1 -> x2, Pallas kernels: 8.71 us -> 8.36 us  [the longest x1 5.24 us: local(): pl.pallas_call(backward_trunk_kernel, out_shape=(pltpu.VMEM((ROWS, 256),...]
  transfers between devices with their start and end apart: 36 -> 36, of which waited for: 14 -> 16; matrix products, arithmetic and copies ran while one was open for 2% -> 2% of each run, Pallas kernels for 16% -> 15%
where the time goes in v7:
time: 118 us; the launch traced here: 117 us
  starting transfers between devices  46.5 us (39%)
  waiting for transfers between devices  39.1 us (33%)
  Pallas kernels  25.4 us (22%)
  other arithmetic  3.34 us (3%)
  local copies, waits for them, and re-layouts  1.44 us (1%)
    ppermute x15, starting transfers between devices, local(): got = lax.ppermute(sums[key], 'region', move(axis, step))  23.2 us
    ppermute x15, starting transfers between devices, local(): held[key] = lax.ppermute(held[source], 'region', move(axis, -step))  19 us
    ppermute x15, waiting for transfers between devices, local(): got = lax.ppermute(sums[key], 'region', move(axis, step))  15.8 us
    ppermute x15, waiting for transfers between devices, local(): held[key] = lax.ppermute(held[source], 'region', move(axis, -step))  13 us
    ppermute x3, waiting for transfers between devices, local(): lax.ppermute(mine, 'ray', [(i, (i + d) % 4) for i in range(4)])  9.16 us
    pallas_call x1, Pallas kernels, local(): pl.pallas_call(backward_trunk_kernel, out_shape=(pltpu.VMEM((ROWS, 256),...  5.24 us
    pallas_call x1, Pallas kernels, local(): pl.pallas_call(backward_far_kernel, out_shape=(shape((8, 128), F32), pltp...  4.96 us
    ppermute x3, starting transfers between devices, local(): lax.ppermute(mine, 'ray', [(i, (i + d) % 4) for i in range(4)])  4.21 us
  transfers between devices with their start and end apart: 36, of which 16 were waited for; matrix products, arithmetic and copies ran while one was open for 2% of the time, Pallas kernels for 15%

profile of v7, /device:TPU:0, one launch (start us, length us, event | category | flops | bytes accessed | tf_op | source)
XLA Modules:
  0.0 116.6 jit_solution(18064784173554699726)
XLA Ops:
  1.7 2.1 %collective-permute-start.5 = (bf16[528,256]{1,0:T(8,128)(2,1)S(1)}, bf16[528,256]{1,0:T(8,128)(2,1)S(1)}, u32[]{:S(2)}, u32[]{:S(2)}) collective-permute-start(bf16[528,256]{1,0:T(8,128)(2,1)S(1)} %fusion.1.refs_2_), channel_id=1, source_target_pairs={{0,8},{1,9},{2,10},{3,11},{4,12},{5,13},{6,14},{7,15},{8,16},{9,17... | collective-permute-start | bytes 811016 | tf_op jit(solution)/shard_map/ppermute | solution.py:381
  3.8 2.8 %collective-permute-start.3 = (bf16[528,256]{1,0:T(8,128)(2,1)S(1)}, bf16[528,256]{1,0:T(8,128)(2,1)S(1)}, u32[]{:S(2)}, u32[]{:S(2)}) collective-permute-start(bf16[528,256]{1,0:T(8,128)(2,1)S(1)} %fusion.1.refs_2_), channel_id=1, source_target_pairs={{0,6},{1,7},{2,0},{3,1},{4,2},{5,3},{6,4},{7,5},{8,14},{9,15},{10,... | collective-permute-start | bytes 811016 | tf_op jit(solution)/shard_map/ppermute | solution.py:381
  6.6 2.2 %collective-permute-start.2 = (bf16[528,256]{1,0:T(8,128)(2,1)S(1)}, bf16[528,256]{1,0:T(8,128)(2,1)S(1)}, u32[]{:S(2)}, u32[]{:S(2)}) collective-permute-start(bf16[528,256]{1,0:T(8,128)(2,1)S(1)} %fusion.1.refs_2_), channel_id=1, source_target_pairs={{0,24},{1,25},{2,26},{3,27},{4,28},{5,29},{6,30},{7,31},{8,0},{9,1... | collective-permute-start | bytes 811016 | tf_op jit(solution)/shard_map/ppermute | solution.py:381
  8.8 4.3 %collective-permute-done.5.refs_6_ = bf16[528,256]{1,0:T(8,128)(2,1)S(1)} collective-permute-done((bf16[528,256]{1,0:T(8,128)(2,1)S(1)}, bf16[528,256]{1,0:T(8,128)(2,1)S(1)}, u32[]{:S(2)}, u32[]{:S(2)}) %collective-permute-start.5) | collective-permute-done | bytes 270368 | tf_op jit(solution)/shard_map/ppermute | solution.py:381
  13.1 1.5 %collective-permute-start.10 = (bf16[528,256]{1,0:T(8,128)(2,1)S(1)}, bf16[528,256]{1,0:T(8,128)(2,1)S(1)}, u32[]{:S(2)}, u32[]{:S(2)}) collective-permute-start(bf16[528,256]{1,0:T(8,128)(2,1)S(1)} %collective-permute-done.5.refs_6_), channel_id=1, source_target_pairs={{0,2},{1,3},{2,4},{3,5},{4,6},{5,7},{6,0},{7,1},{8,10},{9,11},{10,... | collective-permute-start | bytes 811016 | tf_op jit(solution)/shard_map/ppermute | solution.py:384
  14.6 1.6 %meta.1.own = f32[72,128]{1,0:T(8,128)} custom-call(s32[32]{0:T(128)} %owner.1, s32[1,64]{1,0:T(1,128)} %bitcast.23, s32[4,16]{1,0:T(4,128)} %bitcast.21, f32[3,16]{1,0:T(4,128)} %bitcast.22, bf16[64,128]{1,0:T(8,128)(2,1)} %delta.1), custom_call_target="tpu_custom_call" | custom-call | flops 1500000000 | tf_op jit(solution)/shard_map/meta/pallas_call | solution.py:387
  16.8 1.6 %collective-permute-start.9 = (bf16[528,256]{1,0:T(8,128)(2,1)S(1)}, bf16[528,256]{1,0:T(8,128)(2,1)S(1)}, u32[]{:S(2)}, u32[]{:S(2)}) collective-permute-start(bf16[528,256]{1,0:T(8,128)(2,1)S(1)} %collective-permute-done.3.refs_3_), channel_id=1, source_target_pairs={{0,8},{1,9},{2,10},{3,11},{4,12},{5,13},{6,14},{7,15},{8,16},{9,17... | collective-permute-start | bytes 811016 | tf_op jit(solution)/shard_map/ppermute | solution.py:384
  18.4 1.5 %collective-permute-start.6 = (bf16[528,256]{1,0:T(8,128)(2,1)S(1)}, bf16[528,256]{1,0:T(8,128)(2,1)S(1)}, u32[]{:S(2)}, u32[]{:S(2)}) collective-permute-start(bf16[528,256]{1,0:T(8,128)(2,1)S(1)} %collective-permute-done.3.refs_3_), channel_id=1, source_target_pairs={{0,6},{1,7},{2,0},{3,1},{4,2},{5,3},{6,4},{7,5},{8,14},{9,15},{10,... | collective-permute-start | bytes 811016 | tf_op jit(solution)/shard_map/ppermute | solution.py:384
  19.9 1.6 %collective-permute-start.11 = (bf16[528,256]{1,0:T(8,128)(2,1)S(1)}, bf16[528,256]{1,0:T(8,128)(2,1)S(1)}, u32[]{:S(2)}, u32[]{:S(2)}) collective-permute-start(bf16[528,256]{1,0:T(8,128)(2,1)S(1)} %collective-permute-done.4.refs_5_), channel_id=1, source_target_pairs={{0,24},{1,25},{2,26},{3,27},{4,28},{5,29},{6,30},{7,31},{8,0},{9,1... | collective-permute-start | bytes 811016 | tf_op jit(solution)/shard_map/ppermute | solution.py:384
  21.5 2.5 %collective-permute-done.10.refs_11_ = bf16[528,256]{1,0:T(8,128)(2,1)S(1)} collective-permute-done((bf16[528,256]{1,0:T(8,128)(2,1)S(1)}, bf16[528,256]{1,0:T(8,128)(2,1)S(1)}, u32[]{:S(2)}, u32[]{:S(2)}) %collective-permute-start.10) | collective-permute-done | bytes 270368 | tf_op jit(solution)/shard_map/ppermute | solution.py:384
  24.9 3.5 %plan.1 = (s32[8,128]{1,0:T(8,128)S(1)}, f32[144,128]{1,0:T(8,128)S(1)}, bf16[128,128,256]{2,1,0:T(8,128)(2,1)S(1)}) custom-call(f32[72,128]{1,0:T(8,128)S(1)} %copy-done, f32[72,128]{1,0:T(8,128)S(1)} %collective-permute-done.sib, bf16[64,128,256]{2,1,0:T(8,128)(2,1)} %x_own.1, bf16[64,128,256]{2,1,0:T(8,128)(2,1)} %collective-permute-done.1.x_sib), custom_call_target="tpu_custom_call" | custom-call | flops 3000000000 | tf_op jit(solution)/shard_map/plan/pallas_call | solution.py:396
  32.0 1.7 %collective-permute-start.13 = (bf16[528,256]{1,0:T(8,128)(2,1)S(1)}, bf16[528,256]{1,0:T(8,128)(2,1)S(1)}, u32[]{:S(2)}, u32[]{:S(2)}) collective-permute-start(bf16[528,256]{1,0:T(8,128)(2,1)S(1)} %collective-permute-done.7.refs_8_), channel_id=1, source_target_pairs={{0,6},{1,7},{2,0},{3,1},{4,2},{5,3},{6,4},{7,5},{8,14},{9,15},{10,... | collective-permute-start | bytes 811016 | tf_op jit(solution)/shard_map/ppermute | solution.py:384
  33.8 3.2 %collective-permute-done.8.refs_9_ = bf16[528,256]{1,0:T(8,128)(2,1)S(1)} collective-permute-done((bf16[528,256]{1,0:T(8,128)(2,1)S(1)}, bf16[528,256]{1,0:T(8,128)(2,1)S(1)}, u32[]{:S(2)}, u32[]{:S(2)}) %collective-permute-start.8) | collective-permute-done | bytes 270368 | tf_op jit(solution)/shard_map/ppermute | solution.py:384
  38.1 3.9 %forward_near.1 = (f32[2,384,128]{2,1,0:T(8,128)S(1)}, bf16[11,528,256]{2,1,0:T(8,128)(2,1)S(1)}, bf16[48,256,256]{2,1,0:T(8,128)(2,1)S(1)}, bf16[48,256,256]{2,1,0:T(8,128)(2,1)S(1)}) custom-call(s32[8,128]{1,0:T(8,128)S(1)} %get-tuple-element.37.refs_0_, bf16[128,128,256]{2,1,0:T(8,128)(2,1)S(1)} %get-tuple-element.39.refs_1_.refs_2_.refs_4_, ...), custom_call_target="tpu_custom_call" | custom-call | flops 4499999744 | tf_op jit(solution)/shard_map/forward_near/pallas_call | solution.py:410
  43.5 3.1 %forward_far.1 = (f32[8,128]{1,0:T(8,128)S(1)}, f32[6,72,256]{2,1,0:T(8,128)S(1)}, bf16[5,528,256]{2,1,0:T(8,128)(2,1)S(1)}, bf16[24,256,256]{2,1,0:T(8,128)(2,1)S(1)}, bf16[24,256,256]{2,1,0:T(8,128)(2,1)S(1)}) custom-call(s32[8,128]{1,0:T(8,128)S(1)} %get-tuple-element.37.refs_0_, f32[144,128]{1,0:T(8,128)S(1)} %get-tuple-element.38.refs_1_, ...), custom_call_target="tpu_custom_call" | custom-call | flops 3000000000 | tf_op jit(solution)/shard_map/forward_far/pallas_call | solution.py:425
  47.9 5.0 %backward_far.1 = (f32[8,128]{1,0:T(8,128)S(1)}, f32[2,576,128]{2,1,0:T(8,128)S(1)}, bf16[528,256]{1,0:T(8,128)(2,1)S(1)}, bf16[528,256]{1,0:T(8,128)(2,1)S(1)},...) custom-call(s32[8,128]{1,0:T(8,128)S(1)} %get-tuple-element.37.refs_0_, ...), custom_call_target="tpu_custom_call" | custom-call | flops 5600000000 | tf_op jit(solution)/shard_map/backward_far/pallas_call | solution.py:449
  54.0 3.9 %collective-permute-start.20 = (bf16[528,256]{1,0:T(8,128)(2,1)S(1)}, bf16[528,256]{1,0:T(8,128)(2,1)S(1)}, u32[]{:S(2)}, u32[]{:S(2)}) collective-permute-start(bf16[528,256]{1,0:T(8,128)(2,1)S(1)} %get-tuple-element.57), channel_id=1, source_target_pairs={{0,6},{1,7},{2,0},{3,1},{4,2},{5,3},{6,4},{7,5},{8,14},{9,15},{10,... | collective-permute-start | bytes 811016 | tf_op jit(solution)/shard_map/ppermute | solution.py:484
  57.9 3.1 %backward_leaf.1 = (bf16[528,256]{1,0:T(8,128)(2,1)S(1)}, bf16[528,256]{1,0:T(8,128)(2,1)S(1)}, bf16[528,256]{1,0:T(8,128)(2,1)S(1)}, bf16[528,256]{1,0:T(8,128)(2,1)S(1)}) custom-call(s32[8,128]{1,0:T(8,128)S(1)} %get-tuple-element.37.refs_0_, f32[2,576,128]{2,1,0:T(8,128)S(1)} %get-tuple-element.48.refs_1_, ...), custom_call_target="tpu_custom_call" | custom-call | flops 3000000000 | tf_op jit(solution)/shard_map/backward_leaf/pallas_call | solution.py:460
  62.4 5.2 %backward_trunk.1 = (bf16[528,256]{1,0:T(8,128)(2,1)S(1)}, bf16[528,256]{1,0:T(8,128)(2,1)S(1)}, bf16[528,256]{1,0:T(8,128)(2,1)S(1)}, bf16[528,256]{1,0:T(8,128...) custom-call(s32[8,128]{1,0:T(8,128)S(1)} %get-tuple-element.37.refs_0_, ...), custom_call_target="tpu_custom_call" | custom-call | flops 5000000000 | tf_op jit(solution)/shard_map/backward_trunk/pallas_call | solution.py:470
  70.2 3.2 %collective-permute-start.18 = (bf16[528,256]{1,0:T(8,128)(2,1)S(1)}, bf16[528,256]{1,0:T(8,128)(2,1)S(1)}, u32[]{:S(2)}, u32[]{:S(2)}) collective-permute-start(bf16[528,256]{1,0:T(8,128)(2,1)S(1)} %get-tuple-element.54), channel_id=1, source_target_pairs={{0,6},{1,7},{2,0},{3,1},{4,2},{5,3},{6,4},{7,5},{8,14},{9,15},{10,... | collective-permute-start | bytes 811016 | tf_op jit(solution)/shard_map/ppermute | solution.py:484
  73.6 1.7 %collective-permute-start.28 = (bf16[528,256]{1,0:T(8,128)(2,1)S(1)}, bf16[528,256]{1,0:T(8,128)(2,1)S(1)}, u32[]{:S(2)}, u32[]{:S(2)}) collective-permute-start(bf16[528,256]{1,0:T(8,128)(2,1)S(1)} %get-tuple-element.64), channel_id=1, source_target_pairs={{0,24},{1,25},{2,26},{3,27},{4,28},{5,29},{6,30},{7,31},{8,0},{9,1... | collective-permute-start | bytes 811016 | tf_op jit(solution)/shard_map/ppermute | solution.py:484
  75.4 1.7 %collective-permute-done.29 = bf16[528,256]{1,0:T(8,128)(2,1)S(1)} collective-permute-done((bf16[528,256]{1,0:T(8,128)(2,1)S(1)}, bf16[528,256]{1,0:T(8,128)(2,1)S(1)}, u32[]{:S(2)}, u32[]{:S(2)}) %collective-permute-start.29) | collective-permute-done | bytes 270368 | tf_op jit(solution)/shard_map/ppermute | solution.py:484
  77.1 2.1 %collective-permute-start.25 = (bf16[528,256]{1,0:T(8,128)(2,1)S(1)}, bf16[528,256]{1,0:T(8,128)(2,1)S(1)}, u32[]{:S(2)}, u32[]{:S(2)}) collective-permute-start(bf16[528,256]{1,0:T(8,128)(2,1)S(1)} %add_convert_fusion.8), channel_id=1, source_target_pairs={{0,6},{1,7},{2,0},{3,1},{4,2},{5,3},{6,4},{7,5},{8,14},{9,15},{10,... | collective-permute-start | bytes 811016 | tf_op jit(solution)/shard_map/ppermute | solution.py:484
  79.2 2.9 %collective-permute-start.22 = (bf16[528,256]{1,0:T(8,128)(2,1)S(1)}, bf16[528,256]{1,0:T(8,128)(2,1)S(1)}, u32[]{:S(2)}, u32[]{:S(2)}) collective-permute-start(bf16[528,256]{1,0:T(8,128)(2,1)S(1)} %add_convert_fusion.11), channel_id=1, source_target_pairs={{0,24},{1,25},{2,26},{3,27},{4,28},{5,29},{6,30},{7,31},{8,0},{9,1... | collective-permute-start | bytes 811016 | tf_op jit(solution)/shard_map/ppermute | solution.py:484
  83.4 5.0 %collective-permute-done.22 = bf16[528,256]{1,0:T(8,128)(2,1)S(1)} collective-permute-done((bf16[528,256]{1,0:T(8,128)(2,1)S(1)}, bf16[528,256]{1,0:T(8,128)(2,1)S(1)}, u32[]{:S(2)}, u32[]{:S(2)}) %collective-permute-start.22) | collective-permute-done | bytes 270368 | tf_op jit(solution)/shard_map/ppermute | solution.py:484
  88.5 3.6 %collective-permute-start.23 = (bf16[528,256]{1,0:T(8,128)(2,1)S(1)}, bf16[528,256]{1,0:T(8,128)(2,1)S(1)}, u32[]{:S(2)}, u32[]{:S(2)}) collective-permute-start(bf16[528,256]{1,0:T(8,128)(2,1)S(1)} %add_convert_fusion.10), channel_id=1, source_target_pairs={{0,24},{1,25},{2,26},{3,27},{4,28},{5,29},{6,30},{7,31},{8,0},{9,1... | collective-permute-start | bytes 811016 | tf_op jit(solution)/shard_map/ppermute | solution.py:484
  92.3 5.0 %collective-permute-done.23 = bf16[528,256]{1,0:T(8,128)(2,1)S(1)} collective-permute-done((bf16[528,256]{1,0:T(8,128)(2,1)S(1)}, bf16[528,256]{1,0:T(8,128)(2,1)S(1)}, u32[]{:S(2)}, u32[]{:S(2)}) %collective-permute-start.23) | collective-permute-done | bytes 270368 | tf_op jit(solution)/shard_map/ppermute | solution.py:484
  97.2 3.6 %collective-permute-done.32 = bf16[528,256]{1,0:T(8,128)(2,1)S(1)} collective-permute-done((bf16[528,256]{1,0:T(8,128)(2,1)S(1)}, bf16[528,256]{1,0:T(8,128)(2,1)S(1)}, u32[]{:S(2)}, u32[]{:S(2)}) %collective-permute-start.32) | collective-permute-done | bytes 270368 | tf_op jit(solution)/shard_map/ppermute | solution.py:484
  101.0 2.1 %collective-permute-start.35 = (bf16[528,256]{1,0:T(8,128)(2,1)S(1)}, bf16[528,256]{1,0:T(8,128)(2,1)S(1)}, u32[]{:S(2)}, u32[]{:S(2)}) collective-permute-start(bf16[528,256]{1,0:T(8,128)(2,1)S(1)} %add_convert_fusion), channel_id=1, source_target_pairs={{0,64},{32,96},{64,0},{96,32},{1,65},{33,97},{65,1},{97,33},{2,66}... | collective-permute-start | bytes 811016 | tf_op jit(solution)/shard_map/ppermute | solution.py:489
  103.1 2.1 %collective-permute-start.34 = (bf16[528,256]{1,0:T(8,128)(2,1)S(1)}, bf16[528,256]{1,0:T(8,128)(2,1)S(1)}, u32[]{:S(2)}, u32[]{:S(2)}) collective-permute-start(bf16[528,256]{1,0:T(8,128)(2,1)S(1)} %add_convert_fusion), channel_id=1, source_target_pairs={{0,96},{32,0},{64,32},{96,64},{1,97},{33,1},{65,33},{97,65},{2,98}... | collective-permute-start | bytes 811016 | tf_op jit(solution)/shard_map/ppermute | solution.py:489
  105.9 6.2 %collective-permute-done.35 = bf16[528,256]{1,0:T(8,128)(2,1)S(1)} collective-permute-done((bf16[528,256]{1,0:T(8,128)(2,1)S(1)}, bf16[528,256]{1,0:T(8,128)(2,1)S(1)}, u32[]{:S(2)}, u32[]{:S(2)}) %collective-permute-start.35) | collective-permute-done | bytes 270368 | tf_op jit(solution)/shard_map/ppermute | solution.py:489
  113.1 2.0 %collective-permute-done.33 = bf16[528,256]{1,0:T(8,128)(2,1)S(1)} collective-permute-done((bf16[528,256]{1,0:T(8,128)(2,1)S(1)}, bf16[528,256]{1,0:T(8,128)(2,1)S(1)}, u32[]{:S(2)}, u32[]{:S(2)}) %collective-permute-start.33) | collective-permute-done | bytes 270368 | tf_op jit(solution)/shard_map/ppermute | solution.py:489
  (60 shorter events, 20.3 us)
Async XLA Ops:
  0.6 16.2 %collective-permute-start.1 = (bf16[64,128,256]{2,1,0:T(8,128)(2,1)}, bf16[64,128,256]{2,1,0:T(8,128)(2,1)}, u32[]{:S(2)}, u32[]{:S(2)}) collective-permute-start(bf16[64,128,256]{2,1,0:T(8,128)(2,1)} %x_own.1), channel_id=1, source_target_pairs={{0,1},{1,0},{2,3},{3,2},{4,5},{5,4},{6,7},{7,6},{8,9},{9,8},{10,11... | collective-permute-start | bytes 12582920 | tf_op jit(solution)/shard_map/ppermute | solution.py:375
  1.7 11.3 %collective-permute-start.5 = (bf16[528,256]{1,0:T(8,128)(2,1)S(1)}, bf16[528,256]{1,0:T(8,128)(2,1)S(1)}, u32[]{:S(2)}, u32[]{:S(2)}) collective-permute-start(bf16[528,256]{1,0:T(8,128)(2,1)S(1)} %fusion.1.refs_2_), channel_id=1, source_target_pairs={{0,8},{1,9},{2,10},{3,11},{4,12},{5,13},{6,14},{7,15},{8,16},{9,17... | collective-permute-start | bytes 811016 | tf_op jit(solution)/shard_map/ppermute | solution.py:381
  3.8 12.3 %collective-permute-start.3 = (bf16[528,256]{1,0:T(8,128)(2,1)S(1)}, bf16[528,256]{1,0:T(8,128)(2,1)S(1)}, u32[]{:S(2)}, u32[]{:S(2)}) collective-permute-start(bf16[528,256]{1,0:T(8,128)(2,1)S(1)} %fusion.1.refs_2_), channel_id=1, source_target_pairs={{0,6},{1,7},{2,0},{3,1},{4,2},{5,3},{6,4},{7,5},{8,14},{9,15},{10,... | collective-permute-start | bytes 811016 | tf_op jit(solution)/shard_map/ppermute | solution.py:381
  6.6 9.6 %collective-permute-start.2 = (bf16[528,256]{1,0:T(8,128)(2,1)S(1)}, bf16[528,256]{1,0:T(8,128)(2,1)S(1)}, u32[]{:S(2)}, u32[]{:S(2)}) collective-permute-start(bf16[528,256]{1,0:T(8,128)(2,1)S(1)} %fusion.1.refs_2_), channel_id=1, source_target_pairs={{0,24},{1,25},{2,26},{3,27},{4,28},{5,29},{6,30},{7,31},{8,0},{9,1... | collective-permute-start | bytes 811016 | tf_op jit(solution)/shard_map/ppermute | solution.py:381
  8.8 11.2 %collective-permute-start.4 = (bf16[528,256]{1,0:T(8,128)(2,1)S(1)}, bf16[528,256]{1,0:T(8,128)(2,1)S(1)}, u32[]{:S(2)}, u32[]{:S(2)}) collective-permute-start(bf16[528,256]{1,0:T(8,128)(2,1)S(1)} %fusion.1.refs_2_), channel_id=1, source_target_pairs={{0,2},{1,3},{2,4},{3,5},{4,6},{5,7},{6,0},{7,1},{8,10},{9,11},{10,... | collective-permute-start | bytes 811016 | tf_op jit(solution)/shard_map/ppermute | solution.py:381
  13.1 11.0 %collective-permute-start.10 = (bf16[528,256]{1,0:T(8,128)(2,1)S(1)}, bf16[528,256]{1,0:T(8,128)(2,1)S(1)}, u32[]{:S(2)}, u32[]{:S(2)}) collective-permute-start(bf16[528,256]{1,0:T(8,128)(2,1)S(1)} %collective-permute-done.5.refs_6_), channel_id=1, source_target_pairs={{0,2},{1,3},{2,4},{3,5},{4,6},{5,7},{6,0},{7,1},{8,10},{9,11},{10,... | collective-permute-start | bytes 811016 | tf_op jit(solution)/shard_map/ppermute | solution.py:384
  16.1 12.2 %collective-permute-start.7 = (bf16[528,256]{1,0:T(8,128)(2,1)S(1)}, bf16[528,256]{1,0:T(8,128)(2,1)S(1)}, u32[]{:S(2)}, u32[]{:S(2)}) collective-permute-start(bf16[528,256]{1,0:T(8,128)(2,1)S(1)} %collective-permute-done.5.refs_6_), channel_id=1, source_target_pairs={{0,8},{1,9},{2,10},{3,11},{4,12},{5,13},{6,14},{7,15},{8,16},{9,17... | collective-permute-start | bytes 811016 | tf_op jit(solution)/shard_map/ppermute | solution.py:384
  16.8 15.2 %collective-permute-start.9 = (bf16[528,256]{1,0:T(8,128)(2,1)S(1)}, bf16[528,256]{1,0:T(8,128)(2,1)S(1)}, u32[]{:S(2)}, u32[]{:S(2)}) collective-permute-start(bf16[528,256]{1,0:T(8,128)(2,1)S(1)} %collective-permute-done.3.refs_3_), channel_id=1, source_target_pairs={{0,8},{1,9},{2,10},{3,11},{4,12},{5,13},{6,14},{7,15},{8,16},{9,17... | collective-permute-start | bytes 811016 | tf_op jit(solution)/shard_map/ppermute | solution.py:384
  18.4 15.4 %collective-permute-start.6 = (bf16[528,256]{1,0:T(8,128)(2,1)S(1)}, bf16[528,256]{1,0:T(8,128)(2,1)S(1)}, u32[]{:S(2)}, u32[]{:S(2)}) collective-permute-start(bf16[528,256]{1,0:T(8,128)(2,1)S(1)} %collective-permute-done.3.refs_3_), channel_id=1, source_target_pairs={{0,6},{1,7},{2,0},{3,1},{4,2},{5,3},{6,4},{7,5},{8,14},{9,15},{10,... | collective-permute-start | bytes 811016 | tf_op jit(solution)/shard_map/ppermute | solution.py:384
  19.9 9.6 %collective-permute-start.11 = (bf16[528,256]{1,0:T(8,128)(2,1)S(1)}, bf16[528,256]{1,0:T(8,128)(2,1)S(1)}, u32[]{:S(2)}, u32[]{:S(2)}) collective-permute-start(bf16[528,256]{1,0:T(8,128)(2,1)S(1)} %collective-permute-done.4.refs_5_), channel_id=1, source_target_pairs={{0,24},{1,25},{2,26},{3,27},{4,28},{5,29},{6,30},{7,31},{8,0},{9,1... | collective-permute-start | bytes 811016 | tf_op jit(solution)/shard_map/ppermute | solution.py:384
  24.1 12.9 %collective-permute-start.8 = (bf16[528,256]{1,0:T(8,128)(2,1)S(1)}, bf16[528,256]{1,0:T(8,128)(2,1)S(1)}, u32[]{:S(2)}, u32[]{:S(2)}) collective-permute-start(bf16[528,256]{1,0:T(8,128)(2,1)S(1)} %collective-permute-done.2.refs_4_), channel_id=1, source_target_pairs={{0,6},{1,7},{2,0},{3,1},{4,2},{5,3},{6,4},{7,5},{8,14},{9,15},{10,... | collective-permute-start | bytes 811016 | tf_op jit(solution)/shard_map/ppermute | solution.py:384
  28.4 13.6 %collective-permute-start.16 = (bf16[528,256]{1,0:T(8,128)(2,1)S(1)}, bf16[528,256]{1,0:T(8,128)(2,1)S(1)}, u32[]{:S(2)}, u32[]{:S(2)}) collective-permute-start(bf16[528,256]{1,0:T(8,128)(2,1)S(1)} %collective-permute-done.7.refs_8_), channel_id=1, source_target_pairs={{0,4},{1,5},{2,6},{3,7},{4,0},{5,1},{6,2},{7,3},{8,12},{9,13},{10,... | collective-permute-start | bytes 811016 | tf_op jit(solution)/shard_map/ppermute | solution.py:384
  29.6 13.6 %collective-permute-start.15 = (bf16[528,256]{1,0:T(8,128)(2,1)S(1)}, bf16[528,256]{1,0:T(8,128)(2,1)S(1)}, u32[]{:S(2)}, u32[]{:S(2)}) collective-permute-start(bf16[528,256]{1,0:T(8,128)(2,1)S(1)} %collective-permute-done.7.refs_8_), channel_id=1, source_target_pairs={{0,2},{1,3},{2,4},{3,5},{4,6},{5,7},{6,0},{7,1},{8,10},{9,11},{10,... | collective-permute-start | bytes 811016 | tf_op jit(solution)/shard_map/ppermute | solution.py:384
  32.0 11.5 %collective-permute-start.13 = (bf16[528,256]{1,0:T(8,128)(2,1)S(1)}, bf16[528,256]{1,0:T(8,128)(2,1)S(1)}, u32[]{:S(2)}, u32[]{:S(2)}) collective-permute-start(bf16[528,256]{1,0:T(8,128)(2,1)S(1)} %collective-permute-done.7.refs_8_), channel_id=1, source_target_pairs={{0,6},{1,7},{2,0},{3,1},{4,2},{5,3},{6,4},{7,5},{8,14},{9,15},{10,... | collective-permute-start | bytes 811016 | tf_op jit(solution)/shard_map/ppermute | solution.py:384
  33.8 9.7 %collective-permute-start.14 = (bf16[528,256]{1,0:T(8,128)(2,1)S(1)}, bf16[528,256]{1,0:T(8,128)(2,1)S(1)}, u32[]{:S(2)}, u32[]{:S(2)}) collective-permute-start(bf16[528,256]{1,0:T(8,128)(2,1)S(1)} %collective-permute-done.6.refs_7_), channel_id=1, source_target_pairs={{0,8},{1,9},{2,10},{3,11},{4,12},{5,13},{6,14},{7,15},{8,16},{9,17... | collective-permute-start | bytes 811016 | tf_op jit(solution)/shard_map/ppermute | solution.py:384
  52.8 15.7 %collective-permute-start.19 = (bf16[528,256]{1,0:T(8,128)(2,1)S(1)}, bf16[528,256]{1,0:T(8,128)(2,1)S(1)}, u32[]{:S(2)}, u32[]{:S(2)}) collective-permute-start(bf16[528,256]{1,0:T(8,128)(2,1)S(1)} %get-tuple-element.56), channel_id=1, source_target_pairs={{0,4},{1,5},{2,6},{3,7},{4,0},{5,1},{6,2},{7,3},{8,12},{9,13},{10,... | collective-permute-start | bytes 811016 | tf_op jit(solution)/shard_map/ppermute | solution.py:484
  54.0 16.2 %collective-permute-start.20 = (bf16[528,256]{1,0:T(8,128)(2,1)S(1)}, bf16[528,256]{1,0:T(8,128)(2,1)S(1)}, u32[]{:S(2)}, u32[]{:S(2)}) collective-permute-start(bf16[528,256]{1,0:T(8,128)(2,1)S(1)} %get-tuple-element.57), channel_id=1, source_target_pairs={{0,6},{1,7},{2,0},{3,1},{4,2},{5,3},{6,4},{7,5},{8,14},{9,15},{10,... | collective-permute-start | bytes 811016 | tf_op jit(solution)/shard_map/ppermute | solution.py:484
  57.9 15.6 %collective-permute-start.21 = (bf16[528,256]{1,0:T(8,128)(2,1)S(1)}, bf16[528,256]{1,0:T(8,128)(2,1)S(1)}, u32[]{:S(2)}, u32[]{:S(2)}) collective-permute-start(bf16[528,256]{1,0:T(8,128)(2,1)S(1)} %get-tuple-element.58), channel_id=1, source_target_pairs={{0,2},{1,3},{2,4},{3,5},{4,6},{5,7},{6,0},{7,1},{8,10},{9,11},{10,... | collective-permute-start | bytes 811016 | tf_op jit(solution)/shard_map/ppermute | solution.py:484
  61.0 12.6 %collective-permute-start.24 = (bf16[528,256]{1,0:T(8,128)(2,1)S(1)}, bf16[528,256]{1,0:T(8,128)(2,1)S(1)}, u32[]{:S(2)}, u32[]{:S(2)}) collective-permute-start(bf16[528,256]{1,0:T(8,128)(2,1)S(1)} %get-tuple-element.60), channel_id=1, source_target_pairs={{0,8},{1,9},{2,10},{3,11},{4,12},{5,13},{6,14},{7,15},{8,16},{9,17... | collective-permute-start | bytes 811016 | tf_op jit(solution)/shard_map/ppermute | solution.py:484
  67.7 9.4 %collective-permute-start.29 = (bf16[528,256]{1,0:T(8,128)(2,1)S(1)}, bf16[528,256]{1,0:T(8,128)(2,1)S(1)}, u32[]{:S(2)}, u32[]{:S(2)}) collective-permute-start(bf16[528,256]{1,0:T(8,128)(2,1)S(1)} %get-tuple-element.66), channel_id=1, source_target_pairs={{0,24},{1,25},{2,26},{3,27},{4,28},{5,29},{6,30},{7,31},{8,0},{9,1... | collective-permute-start | bytes 811016 | tf_op jit(solution)/shard_map/ppermute | solution.py:484
  68.6 10.6 %collective-permute-start.30 = (bf16[528,256]{1,0:T(8,128)(2,1)S(1)}, bf16[528,256]{1,0:T(8,128)(2,1)S(1)}, u32[]{:S(2)}, u32[]{:S(2)}) collective-permute-start(bf16[528,256]{1,0:T(8,128)(2,1)S(1)} %get-tuple-element.67), channel_id=1, source_target_pairs={{0,8},{1,9},{2,10},{3,11},{4,12},{5,13},{6,14},{7,15},{8,16},{9,17... | collective-permute-start | bytes 811016 | tf_op jit(solution)/shard_map/ppermute | solution.py:484
  70.2 12.2 %collective-permute-start.18 = (bf16[528,256]{1,0:T(8,128)(2,1)S(1)}, bf16[528,256]{1,0:T(8,128)(2,1)S(1)}, u32[]{:S(2)}, u32[]{:S(2)}) collective-permute-start(bf16[528,256]{1,0:T(8,128)(2,1)S(1)} %get-tuple-element.54), channel_id=1, source_target_pairs={{0,6},{1,7},{2,0},{3,1},{4,2},{5,3},{6,4},{7,5},{8,14},{9,15},{10,... | collective-permute-start | bytes 811016 | tf_op jit(solution)/shard_map/ppermute | solution.py:484
  73.5 8.8 %collective-permute-start.26 = (bf16[528,256]{1,0:T(8,128)(2,1)S(1)}, bf16[528,256]{1,0:T(8,128)(2,1)S(1)}, u32[]{:S(2)}, u32[]{:S(2)}) collective-permute-start(bf16[528,256]{1,0:T(8,128)(2,1)S(1)} %get-tuple-element.62), channel_id=1, source_target_pairs={{0,2},{1,3},{2,4},{3,5},{4,6},{5,7},{6,0},{7,1},{8,10},{9,11},{10,... | collective-permute-start | bytes 811016 | tf_op jit(solution)/shard_map/ppermute | solution.py:484
  73.6 18.4 %collective-permute-start.28 = (bf16[528,256]{1,0:T(8,128)(2,1)S(1)}, bf16[528,256]{1,0:T(8,128)(2,1)S(1)}, u32[]{:S(2)}, u32[]{:S(2)}) collective-permute-start(bf16[528,256]{1,0:T(8,128)(2,1)S(1)} %get-tuple-element.64), channel_id=1, source_target_pairs={{0,24},{1,25},{2,26},{3,27},{4,28},{5,29},{6,30},{7,31},{8,0},{9,1... | collective-permute-start | bytes 811016 | tf_op jit(solution)/shard_map/ppermute | solution.py:484
  77.1 15.2 %collective-permute-start.25 = (bf16[528,256]{1,0:T(8,128)(2,1)S(1)}, bf16[528,256]{1,0:T(8,128)(2,1)S(1)}, u32[]{:S(2)}, u32[]{:S(2)}) collective-permute-start(bf16[528,256]{1,0:T(8,128)(2,1)S(1)} %add_convert_fusion.8), channel_id=1, source_target_pairs={{0,6},{1,7},{2,0},{3,1},{4,2},{5,3},{6,4},{7,5},{8,14},{9,15},{10,... | collective-permute-start | bytes 811016 | tf_op jit(solution)/shard_map/ppermute | solution.py:484
  79.2 9.2 %collective-permute-start.22 = (bf16[528,256]{1,0:T(8,128)(2,1)S(1)}, bf16[528,256]{1,0:T(8,128)(2,1)S(1)}, u32[]{:S(2)}, u32[]{:S(2)}) collective-permute-start(bf16[528,256]{1,0:T(8,128)(2,1)S(1)} %add_convert_fusion.11), channel_id=1, source_target_pairs={{0,24},{1,25},{2,26},{3,27},{4,28},{5,29},{6,30},{7,31},{8,0},{9,1... | collective-permute-start | bytes 811016 | tf_op jit(solution)/shard_map/ppermute | solution.py:484
  82.3 9.7 %collective-permute-start.31 = (bf16[528,256]{1,0:T(8,128)(2,1)S(1)}, bf16[528,256]{1,0:T(8,128)(2,1)S(1)}, u32[]{:S(2)}, u32[]{:S(2)}) collective-permute-start(bf16[528,256]{1,0:T(8,128)(2,1)S(1)} %add_convert_fusion.2), channel_id=1, source_target_pairs={{0,2},{1,3},{2,4},{3,5},{4,6},{5,7},{6,0},{7,1},{8,10},{9,11},{10,... | collective-permute-start | bytes 811016 | tf_op jit(solution)/shard_map/ppermute | solution.py:484
  82.4 9.9 %collective-permute-start.27 = (bf16[528,256]{1,0:T(8,128)(2,1)S(1)}, bf16[528,256]{1,0:T(8,128)(2,1)S(1)}, u32[]{:S(2)}, u32[]{:S(2)}) collective-permute-start(bf16[528,256]{1,0:T(8,128)(2,1)S(1)} %add_convert_fusion.6), channel_id=1, source_target_pairs={{0,8},{1,9},{2,10},{3,11},{4,12},{5,13},{6,14},{7,15},{8,16},{9,17... | collective-permute-start | bytes 811016 | tf_op jit(solution)/shard_map/ppermute | solution.py:484
  88.5 8.8 %collective-permute-start.23 = (bf16[528,256]{1,0:T(8,128)(2,1)S(1)}, bf16[528,256]{1,0:T(8,128)(2,1)S(1)}, u32[]{:S(2)}, u32[]{:S(2)}) collective-permute-start(bf16[528,256]{1,0:T(8,128)(2,1)S(1)} %add_convert_fusion.10), channel_id=1, source_target_pairs={{0,24},{1,25},{2,26},{3,27},{4,28},{5,29},{6,30},{7,31},{8,0},{9,1... | collective-permute-start | bytes 811016 | tf_op jit(solution)/shard_map/ppermute | solution.py:484
  101.0 11.1 %collective-permute-start.35 = (bf16[528,256]{1,0:T(8,128)(2,1)S(1)}, bf16[528,256]{1,0:T(8,128)(2,1)S(1)}, u32[]{:S(2)}, u32[]{:S(2)}) collective-permute-start(bf16[528,256]{1,0:T(8,128)(2,1)S(1)} %add_convert_fusion), channel_id=1, source_target_pairs={{0,64},{32,96},{64,0},{96,32},{1,65},{33,97},{65,1},{97,33},{2,66}... | collective-permute-start | bytes 811016 | tf_op jit(solution)/shard_map/ppermute | solution.py:489
  103.1 9.9 %collective-permute-start.34 = (bf16[528,256]{1,0:T(8,128)(2,1)S(1)}, bf16[528,256]{1,0:T(8,128)(2,1)S(1)}, u32[]{:S(2)}, u32[]{:S(2)}) collective-permute-start(bf16[528,256]{1,0:T(8,128)(2,1)S(1)} %add_convert_fusion), channel_id=1, source_target_pairs={{0,96},{32,0},{64,32},{96,64},{1,97},{33,1},{65,33},{97,65},{2,98}... | collective-permute-start | bytes 811016 | tf_op jit(solution)/shard_map/ppermute | solution.py:489
  105.2 9.8 %collective-permute-start.33 = (bf16[528,256]{1,0:T(8,128)(2,1)S(1)}, bf16[528,256]{1,0:T(8,128)(2,1)S(1)}, u32[]{:S(2)}, u32[]{:S(2)}) collective-permute-start(bf16[528,256]{1,0:T(8,128)(2,1)S(1)} %add_convert_fusion), channel_id=1, source_target_pairs={{0,32},{32,64},{64,96},{96,0},{1,33},{33,65},{65,97},{97,1},{2,34}... | collective-permute-start | bytes 811016 | tf_op jit(solution)/shard_map/ppermute | solution.py:489
  (5 other events, 19.6 us)
